TPU v7x, 256 devices: a whole 4x4x8 slice. The times are simulated.
256 devices in a mesh: ctx: 16 (over x_hi, y, core), head: 16 (over x_lo, z).
Axes of the slice: x: 4 (x_hi: 2, x_lo: 2; x = x_hi * 2 + x_lo), y: 4, z: 8, core: 2. Of those that a mesh axis runs over, the one named last changes fastest.
Arguments:
- q_nope: bfloat16 [2048, 16384], P('ctx', 'head'), may hold values from -6 to 6
- q_rope: bfloat16 [2048, 8192], P('ctx', 'head'), may hold values from -6 to 6
- compressed: bfloat16 [2048, 576], P('ctx'), may hold values from -6 to 6
- w_uk: bfloat16 [512, 16384], P(None, 'head'), may hold values from -0.25 to 0.25
- w_uv: bfloat16 [512, 16384], P(None, 'head'), may hold values from -0.25 to 0.25
- grad_out: bfloat16 [2048, 16384], P('ctx', 'head'), may hold values from -6 to 6
- positions: int32 [2048], P('ctx'), may hold values from 0 to 16383, as said below
- block_map: int32 [16, 2], replicated, may hold values from 0 to 31, as said below
Outputs:
- grad_q_nope: bfloat16 [2048, 16384], P('ctx', 'head')
- grad_q_rope: bfloat16 [2048, 8192], P('ctx', 'head')
- grad_compressed: bfloat16 [2048, 576], P('ctx')
Inputs may be any that keep to these rules, and one draw needn't show every extreme that they name: Token rows r * 128 to (r + 1) * 128 - 1 hold block block_map[r, 0] followed by block block_map[r, 1] of the 32 blocks of 64 tokens; block_map[r, 1] = 31 - block_map[r, 0]; every block appears once. Within each block the positions rise by one from a start of their own.
All inputs are finite; a program needn't handle non-finite values.
Results may differ from a plain program's by a relative error of at most 0.034.
Values may be sent and summed in bfloat16 or wider, within the bound.
No kernel may reach another device: no remote copies, remote signals or barrier semaphores. Data moves between devices by JAX's collectives and lax.ppermute only.
A program may use at most 128 MiB of HBM per device.

v0:
```python
import math

import jax
import jax.numpy as jnp
from jax import lax
from jax.sharding import PartitionSpec as P

D_NOPE = 128
D_ROPE = 64
D_V = 128
D_LAT = 512


attn_boost = (0.1 * math.log(40.0) + 1.0) ** 2


def yarn_freqs(half):
    index = jnp.arange(half, dtype=jnp.float32)
    width = 2 * half
    extra = jnp.power(10000.0, -2.0 * index / width)
    inter = extra / 40.0
    lower = math.floor(
        width * math.log(4096.0 / (32.0 * 2.0 * math.pi)) / (2.0 * math.log(10000.0))
    )
    upper = math.ceil(width * math.log(4096.0 / (1.0 * 2.0 * math.pi)) / (2.0 * math.log(10000.0)))
    lower = max(lower, 0)
    upper = min(upper, half - 1)
    spread = max(upper - lower, 0.001)
    ramp = jnp.clip((index - lower) / spread, 0.0, 1.0)
    return inter * ramp + extra * (1.0 - ramp)


def angles(positions, half):
    turn = positions.astype(jnp.float32)[:, None] * yarn_freqs(half)[None, :]
    return (jnp.cos(turn), jnp.sin(turn))


def rotate(values, cosine, sine):
    half = values.shape[-1] // 2
    first, second = (values[..., :half], values[..., half:])
    return jnp.concatenate(
        [first * cosine - second * sine, second * cosine + first * sine], axis=-1
    )


def unrotate(grads, cosine, sine):
    half = grads.shape[-1] // 2
    first, second = (grads[..., :half], grads[..., half:])
    return jnp.concatenate(
        [first * cosine + second * sine, second * cosine - first * sine], axis=-1
    )


def project_back(dkeys, dvalues, w_uk, w_uv):
    result = jnp.dot(dkeys, w_uk.astype(jnp.float32).T, precision=lax.Precision.HIGHEST)
    return result + jnp.dot(dvalues, w_uv.astype(jnp.float32).T, precision=lax.Precision.HIGHEST)


def on_device(q_nope, q_rope, compressed, w_uk, w_uv, grad_out, positions, block_map):
    rows = q_nope.shape[0]
    half_rows = rows // 2
    heads = w_uk.shape[1] // D_NOPE
    total = rows * lax.axis_size("ctx")
    start_own = lax.axis_index("ctx") * rows
    cosine, sine = angles(positions, D_ROPE // 2)
    blocks = jnp.repeat(block_map.reshape(-1), half_rows, total_repeat_length=total)
    order_all = blocks * half_rows + jnp.arange(total, dtype=jnp.int32) % half_rows
    order_own = lax.dynamic_slice_in_dim(order_all, start_own, rows)
    latent = compressed[:, :D_LAT]
    k_rot_own = rotate(compressed[:, D_LAT:].astype(jnp.float32), cosine, sine).astype(jnp.bfloat16)
    keys_own = jnp.dot(latent, w_uk, preferred_element_type=jnp.float32).astype(jnp.bfloat16)
    values_own = jnp.dot(latent, w_uv, preferred_element_type=jnp.float32).astype(jnp.bfloat16)
    keys_all, values_all, k_rot_all = (
        lax.all_gather(keys_own, "ctx", axis=0, tiled=True),
        lax.all_gather(values_own, "ctx", axis=0, tiled=True),
        lax.all_gather(k_rot_own, "ctx", axis=0, tiled=True),
    )
    key_heads = keys_all.reshape(total, heads, D_NOPE)
    value_heads = values_all.reshape(total, heads, D_V)
    query_plain = q_nope.reshape(rows, heads, D_NOPE)
    query_rot = rotate(
        q_rope.reshape(rows, heads, D_ROPE).astype(jnp.float32),
        cosine[:, None, :],
        sine[:, None, :],
    )
    query_rot = query_rot.astype(jnp.bfloat16)
    cotangent = grad_out.reshape(rows, heads, D_V)
    scale = (D_NOPE + D_ROPE) ** (-0.5) * attn_boost
    allowed = (order_all[None, :] <= order_own[:, None])[None, :, :]
    scores = jnp.einsum("thd,shd->hts", query_plain, key_heads, preferred_element_type=jnp.float32)
    scores = (
        scores + jnp.einsum("thd,sd->hts", query_rot, k_rot_all, preferred_element_type=jnp.float32)
    ) * scale
    scores = jnp.where(allowed, scores, -1e30)
    row_max = jnp.max(scores, axis=2, keepdims=True)
    log_total = row_max + jnp.log(jnp.sum(jnp.exp(scores - row_max), axis=2, keepdims=True))
    probs = jnp.exp(scores - log_total).astype(jnp.bfloat16)
    dprobs = jnp.einsum("thd,shd->hts", cotangent, value_heads, preferred_element_type=jnp.float32)
    delta = jnp.sum(probs.astype(jnp.float32) * dprobs, axis=2, keepdims=True)
    dscores = (probs.astype(jnp.float32) * (dprobs - delta) * scale).astype(jnp.bfloat16)
    dplain = jnp.einsum("hts,shd->thd", dscores, key_heads, preferred_element_type=jnp.float32)
    drot = jnp.einsum("hts,sd->thd", dscores, k_rot_all, preferred_element_type=jnp.float32)
    grad_q_nope = dplain.reshape(rows, heads * D_NOPE).astype(jnp.bfloat16)
    grad_q_rope = unrotate(drot, cosine[:, None, :], sine[:, None, :])
    grad_q_rope = grad_q_rope.reshape(rows, heads * D_ROPE).astype(jnp.bfloat16)
    dkeys = jnp.einsum("hts,thd->shd", dscores, query_plain, preferred_element_type=jnp.float32)
    dkeys = dkeys.reshape(total, heads * D_NOPE)
    dvalues = jnp.einsum("hts,thd->shd", probs, cotangent, preferred_element_type=jnp.float32)
    dvalues = dvalues.reshape(total, heads * D_V)
    dkrot = jnp.einsum("hts,thd->sd", dscores, query_rot, preferred_element_type=jnp.float32)
    mine_keys, mine_values, mine_rot = (
        lax.psum_scatter(dkeys.astype(jnp.bfloat16), "ctx", scatter_dimension=0, tiled=True).astype(
            jnp.float32
        ),
        lax.psum_scatter(
            dvalues.astype(jnp.bfloat16), "ctx", scatter_dimension=0, tiled=True
        ).astype(jnp.float32),
        lax.psum_scatter(dkrot.astype(jnp.bfloat16), "ctx", scatter_dimension=0, tiled=True).astype(
            jnp.float32
        ),
    )
    grad_lat = project_back(mine_keys, mine_values, w_uk, w_uv)
    side_lat, side_rot = (
        lax.psum(grad_lat.astype(jnp.bfloat16), "head").astype(jnp.float32),
        lax.psum(mine_rot.astype(jnp.bfloat16), "head").astype(jnp.float32),
    )
    grad_compressed = jnp.concatenate([side_lat, unrotate(side_rot, cosine, sine)], axis=1)
    return (grad_q_nope, grad_q_rope, grad_compressed.astype(jnp.bfloat16))


def solution(mesh):
    in_specs = (
        P("ctx", "head"),
        P("ctx", "head"),
        P("ctx", None),
        P(None, "head"),
        P(None, "head"),
        P("ctx", "head"),
        P("ctx"),
        P(),
    )
    out_specs = (P("ctx", "head"), P("ctx", "head"), P("ctx", None))
    return jax.shard_map(
        on_device, mesh=mesh, in_specs=in_specs, out_specs=out_specs, check_vma=False
    )
```

profile of v0, /device:TPU:4, one launch (start us, length us, event | category | flops | bytes accessed | tf_op | source)
XLA Modules:
  0.0 553.4 jit_solution(18267401273319791977)
XLA Ops:
  7.2 1.2 copy-done
  8.4 1.9 convolution_convert_fusion.3
  10.4 2.3 convolution_convert_fusion.2
  12.8 1.0 copy.52
  14.5 1.1 copy.80
  16.5 1.1 copy.81
  19.8 4.5 compare_select_fusion.1
  24.9 16.5 %fusion.37 = s32[2048]{0:T(1024)S(1)} fusion(pred[2048]{0:T(1024)(128)(4,1)S(1)} %get-tuple-element.48, pred[2048]{0:T(1024)(128)(4,1)S(1)} %get-tuple-element.47, pred[2048]{0:T(1024)(128)(4,1)S(1)} %get-tuple-element.46, pred[2048]{0:T(1024)(128)(4,1)S(1)} %get-tuple-element.45, pred[2048]{0:T(1024)(128)(4,1)S(1)} %get-tuple-element.44, ...), kind=kLoop, calls=%fused_computation.96 | loop fusion | flops 86016 | bytes 75940 | tf_op jit(solution)/shard_map/add | solution.py:67
  42.4 23.3 %all_gather.10 = bf16[2048,64]{0,1:T(8,128)(2,1)S(1)} all-gather(bf16[128,64]{0,1:T(8,128)(2,1)S(1)} %pad_maximum_fusion.5), channel_id=1, replica_groups=mesh['ctx'=16,'head'=16] {'ctx'}, dimensions={0}, use_global_device_ids=true | all-gather | bytes 278528 | tf_op jit(solution)/shard_map/all_gather | solution.py:76
  66.1 7.2 %all-gather.3.cloned.1.call-done = bf16[2048,1024]{1,0:T(8,128)(2,1)} async-done(((bf16[128,1024]{1,0:T(8,128)(2,1)}), bf16[2048,1024]{1,0:T(8,128)(2,1)}) %all-gather.3.cloned.1.call-update) | async-done | bytes 4194320 | tf_op jit(solution)/shard_map/all_gather | solution.py:74
  73.3 6.5 %copy.79 = bf16[2048,1024]{0,1:T(8,128)(2,1)} copy(bf16[2048,1024]{1,0:T(8,128)(2,1)} %all-gather.3.cloned.1.call-done) | data formatting | bytes 8388608 | tf_op jit(solution)/shard_map/reshape | solution.py:78
  79.8 3.6 fusion.58
  83.4 1.8 fusion.57
  85.1 1.1 exponential_reduce_fusion
  86.3 3.0 exponential_convert_fusion
  89.3 44.8 %all-gather.5.cloned.1.call-done = bf16[2048,1024]{1,0:T(8,128)(2,1)} async-done(((bf16[128,1024]{1,0:T(8,128)(2,1)}), bf16[2048,1024]{1,0:T(8,128)(2,1)}) %all-gather.5.cloned.1.call-update) | async-done | bytes 4194320 | tf_op jit(solution)/shard_map/all_gather | solution.py:75
  134.1 6.6 %fusion.6 = f32[8,2048,128]{2,1,0:T(8,128)} fusion(bf16[128,8,128]{0,2,1:T(8,128)(2,1)S(1)} %bitcast.147, bf16[2048,1024]{1,0:T(8,128)(2,1)} %all-gather.5.cloned.1.call-done), kind=kOutput, calls=%fused_computation.12 | convolution fusion | flops 536870912 | bytes 12845056 | tf_op jit(solution)/shard_map/thd,shd->hts/dot_general | solution.py:98
  140.7 11.0 %fusion.13 = bf16[2048,64]{0,1:T(8,128)(2,1)S(1)} fusion(bf16[8,128,2048]{1,2,0:T(8,128)(2,1)} %exponential_convert_fusion, f32[8,2048,128]{2,1,0:T(8,128)} %fusion.6, bf16[128,8,32]{0,2,1:T(8,128)(2,1)S(1)} %get-tuple-element.54, bf16[128,8,32]{0,2,1:T(8,128)(2,1)S(1)} %get-tuple-element.53), kind=kOutput, calls=%fused_computation.21 | convolution fusion | flops 283511808 | bytes 12976128 | tf_op jit(solution)/shard_map/hts,thd->sd/dot_general | solution.py:110
  151.8 1.0 copy.77
  153.1 13.1 %convolution_convert_fusion.1 = bf16[8,2048,128]{1,2,0:T(8,128)(2,1)} fusion(bf16[128,8,128]{0,2,1:T(8,128)(2,1)S(1)} %bitcast.150, bf16[8,128,2048]{1,2,0:T(8,128)(2,1)} %exponential_convert_fusion, f32[8,2048,128]{2,1,0:T(8,128)} %fusion.6), kind=kOutput, calls=%fused_computation.16 | convolution fusion | flops 553651200 | bytes 17039360 | tf_op jit(solution)/shard_map/hts,thd->shd/dot_general | solution.py:106
  166.2 6.4 %copy.73 = bf16[2048,1024]{1,0:T(8,128)(2,1)} copy(bf16[2048,1024]{0,1:T(8,128)(2,1)} %bitcast.146) | data formatting | bytes 8388608
  172.7 5.5 convolution_convert_fusion
  178.2 6.4 %copy.75 = bf16[2048,1024]{1,0:T(8,128)(2,1)} copy(bf16[2048,1024]{0,1:T(8,128)(2,1)} %bitcast.145) | data formatting | bytes 8388608
  184.7 12.8 %fusion.14 = bf16[8,128,128]{2,1,0:T(8,128)(2,1)S(1)} fusion(bf16[2048,8,128]{0,2,1:T(8,128)(2,1)} %bitcast.144, bf16[8,128,2048]{1,2,0:T(8,128)(2,1)} %exponential_convert_fusion, f32[8,2048,128]{2,1,0:T(8,128)} %fusion.6), kind=kOutput, calls=%fused_computation.22 | convolution fusion | flops 551685120 | bytes 17039360 | tf_op jit(solution)/shard_map/hts,shd->thd/dot_general | solution.py:101
  198.3 10.9 %fusion.15 = f32[128,8,64]{0,2,1:T(8,128)S(1)} fusion(bf16[8,128,2048]{1,2,0:T(8,128)(2,1)} %exponential_convert_fusion, f32[8,2048,128]{2,1,0:T(8,128)} %fusion.6, bf16[2048,64]{0,1:T(8,128)(2,1)S(1)} %all_gather.10), kind=kOutput, calls=%fused_computation.25 | convolution fusion | flops 283118592 | bytes 13107200 | tf_op jit(solution)/shard_map/hts,sd->thd/dot_general | solution.py:102
  210.0 15.7 %reduce-scatter.14.cloned.1.call-done = bf16[128,64]{1,0:T(8,128)(2,1)} async-done(((bf16[2048,64]{1,0:T(8,128)(2,1)}), bf16[128,64]{1,0:T(8,128)(2,1)}) %reduce-scatter.14.cloned.1.call-update) | async-done | bytes 16400
  226.6 63.9 %psum.15 = bf16[128,64]{0,1:T(8,128)(2,1)S(1)} all-reduce(bf16[128,64]{0,1:T(8,128)(2,1)S(1)} %copy.78), channel_id=1, replica_groups=mesh['ctx'=16,'head'=16] {'head'}, use_global_device_ids=true, to_apply=%region_7.8 | all-reduce | flops 8192 | bytes 32768 | tf_op jit(solution)/shard_map/psum | solution.py:125
  290.5 26.8 %reduce-scatter.10.cloned.1.call-done = bf16[128,1024]{1,0:T(8,128)(2,1)} async-done(((bf16[2048,1024]{1,0:T(8,128)(2,1)}), bf16[128,1024]{1,0:T(8,128)(2,1)}) %reduce-scatter.10.cloned.1.call-update) | async-done | bytes 262160
  317.3 1.4 fusion.59
  318.8 89.8 %reduce-scatter.12.cloned.1.call-done = bf16[128,1024]{1,0:T(8,128)(2,1)} async-done(((bf16[2048,1024]{1,0:T(8,128)(2,1)}), bf16[128,1024]{1,0:T(8,128)(2,1)}) %reduce-scatter.12.cloned.1.call-update) | async-done | bytes 262160
  408.6 2.1 fusion.16
  411.1 133.8 %all-reduce.2.cloned.1.call-done = bf16[128,512]{1,0:T(8,128)(2,1)} async-done(((bf16[128,512]{1,0:T(8,128)(2,1)}), bf16[128,512]{1,0:T(8,128)(2,1)}) %all-reduce.2.cloned.1.call-update) | async-done | bytes 131088 | tf_op jit(solution)/shard_map/psum | solution.py:124
  (42 shorter events, 10.9 us)
Async XLA Ops:
  7.2 1.2 copy-start
  7.2 66.1 %all-gather.3.cloned.1.call-start = ((), (), s32[]{:S(2)}) async-start(), calls=%async_computation.3 | async-start | bytes 4456448 | tf_op jit(solution)/shard_map/all_gather | solution.py:74
  10.4 123.7 %all-gather.5.cloned.1.call-start = ((), (), s32[]{:S(2)}) async-start(), calls=%async_computation.4 | async-start | bytes 4456448 | tf_op jit(solution)/shard_map/all_gather | solution.py:75
  12.8 213.0 %reduce-scatter.14.cloned.1.call-start = ((), (), s32[]{:S(2)}) async-start(), calls=%async_computation.8 | async-start | bytes 557056
  152.9 164.5 %reduce-scatter.10.cloned.1.call-start = ((), (), s32[]{:S(2)}) async-start(), calls=%async_computation.6 | async-start | bytes 4456448
  172.7 235.9 %reduce-scatter.12.cloned.1.call-start = ((), (), s32[]{:S(2)}) async-start(), calls=%async_computation.7 | async-start | bytes 4456448
  184.6 360.2 %all-reduce.2.cloned.1.call-start = ((), (), s32[]{:S(2)}) async-start(), calls=%async_computation.5 | async-start | bytes 262144 | tf_op jit(solution)/shard_map/psum | solution.py:124
  197.5 211.1 %copy-start.1 = (bf16[512,1024]{1,0:T(8,128)(2,1)S(1)}, bf16[512,1024]{1,0:T(8,128)(2,1)}, u32[]{:S(2)}) copy-start(bf16[512,1024]{1,0:T(8,128)(2,1)} %param.14) | copy-start | bytes 3145732
Sparse Core Ops, SparseCore 0:
  11.3 61.8 all-gather.2
  76.0 58.0 all-gather.4
  153.0 72.7 reduce-scatter.13
  230.5 86.7 reduce-scatter.9
  321.5 87.0 reduce-scatter.11
  411.8 133.0 all-reduce.1
where the time goes:
time: 555 us; the launch traced here: 553 us
  waiting for transfers between devices  318 us (57%)
  blocking collectives  87.2 us (16%)
  matrix products  73.1 us (13%)
  local copies, waits for them, and re-layouts  30.7 us (6%)
  other arithmetic  29.6 us (5%)
  between operations  14.3 us (3%)
    psum x1, waiting for transfers between devices, on_device(): lax.psum(grad_lat.astype(jnp.bfloat16), 'head').astype(jnp.float32)  134 us
    unnamed x9, waiting for transfers between devices  132 us
    psum x1, blocking collectives, on_device(): lax.psum(mine_rot.astype(jnp.bfloat16), 'head').astype(jnp.float32)  63.9 us
    all_gather x1, waiting for transfers between devices, on_device(): lax.all_gather(values_own, 'ctx', axis=0, tiled=True)  44.8 us
    all_gather x1, blocking collectives, on_device(): lax.all_gather(k_rot_own, 'ctx', axis=0, tiled=True)  23.3 us
    unnamed x12, local copies, waits for them, and re-layouts  19.1 us
    add x1, other arithmetic, on_device(): blocks * half_rows + jnp.arange(total, dtype=jnp.int32) % half_rows  16.5 us
    dot_general x1, matrix products, on_device(): jnp.einsum('hts,thd->shd', dscores, query_plain, preferred_element_type=j...  13.1 us
  transfers between devices with their start and end apart: 6, of which 6 were waited for; matrix products, arithmetic and copies ran while one was open for 19% of the time, Pallas kernels for 0%

commit v1 on v0

v1 whole, which is shorter than its diff:
```python
import math

import jax
import jax.numpy as jnp
import numpy as np
from jax import lax
from jax.experimental import pallas as pl
from jax.experimental.pallas import tpu as pltpu
from jax.sharding import PartitionSpec as P

D_NOPE = 128
D_ROPE = 64
D_V = 128
D_LAT = 512
D_ALL = D_LAT + D_ROPE
N_CTX = 16
N_CHIP = 8
N_HEAD = 16
ROWS = 128
HALF = 64
TOTAL = ROWS * N_CTX
HEADS = 8
LANES = HEADS * HALF
CHUNK = 256
N_CHUNK = TOTAL // CHUNK
PER_CHUNK = CHUNK // HALF
N_BLOCK = TOTAL // HALF

SCALE = (D_NOPE + D_ROPE) ** (-0.5) * (0.1 * math.log(40.0) + 1.0) ** 2
LOG2E = math.log2(math.e)
HIDDEN = -1e30
CORES = [[c for c in range(N_CTX) if c % 2 == k] for k in range(2)]
SWAP = [(c, c ^ 1) for c in range(N_CTX)]

bf16 = jnp.bfloat16
f32 = jnp.float32


def frequencies():
    half = D_ROPE // 2
    index = np.arange(half, dtype=np.float64)
    width = 2 * half
    extra = np.power(10000.0, -2.0 * index / width)
    inter = extra / 40.0
    lower = math.floor(width * math.log(4096.0 / (32.0 * 2.0 * math.pi)) / (2.0 * math.log(10000.0)))
    upper = math.ceil(width * math.log(4096.0 / (1.0 * 2.0 * math.pi)) / (2.0 * math.log(10000.0)))
    lower = max(lower, 0)
    upper = min(upper, half - 1)
    spread = max(upper - lower, 0.001)
    ramp = np.clip((index - lower) / spread, 0.0, 1.0)
    inv = inter * ramp + extra * (1.0 - ramp)
    return np.tile(inv, 4).astype(np.float32)[None, :]


def split_half_pi():
    rest = math.pi / 2
    parts = []
    for bits in (9, 19):
        part = math.floor(rest * 2.0**bits) / 2.0**bits
        parts.append(part)
        rest -= part
    return parts + [rest]


HALF_PI = split_half_pi()


def cos_sin(angle):
    turns = jnp.floor(angle * (2.0 / math.pi) + 0.5)
    r = angle - turns * HALF_PI[0]
    r = r - turns * HALF_PI[1]
    r = r - turns * HALF_PI[2]
    r2 = r * r
    sine = r + r * r2 * (-1.0 / 6 + r2 * (1.0 / 120 + r2 * (-1.0 / 5040 + r2 * (1.0 / 362880))))
    cosine = 1.0 + r2 * (-0.5 + r2 * (1.0 / 24 + r2 * (-1.0 / 720 + r2 * (1.0 / 40320))))
    quarter = turns.astype(jnp.int32) & 3
    odd = (quarter & 1) == 1
    cos_out = jnp.where(odd, sine, cosine)
    sin_out = jnp.where(odd, cosine, sine)
    cos_out = jnp.where((quarter == 1) | (quarter == 2), -cos_out, cos_out)
    sin_out = jnp.where(quarter >= 2, -sin_out, sin_out)
    return cos_out, sin_out


def lanes_of(shape):
    return lax.broadcasted_iota(jnp.int32, shape, 1)


def swap_halves(x):
    return jnp.where((lanes_of(x.shape) & 63) < 32, pltpu.roll(x, 96, 1), pltpu.roll(x, 32, 1))


def pair_tile(first, second, half):
    low = lanes_of(first.shape) < HALF
    if half == 0:
        return jnp.where(low, first, pltpu.roll(second, HALF, 1))
    return jnp.where(low, pltpu.roll(first, HALF, 1), second)


def share_kernel(pos_ref, inv_ref, comp_ref, out_ref, cos_ref, sin_ref):
    pos = jnp.broadcast_to(pos_ref[...].astype(f32), (ROWS, ROWS)).T
    cosine, sine = cos_sin(pos * inv_ref[...])
    sine = jnp.where((lanes_of(sine.shape) & 63) < 32, -sine, sine)
    cos_ref[...] = cosine
    sin_ref[...] = sine
    x = comp_ref[:, D_LAT:].astype(f32)
    x = jnp.concatenate([x, x], axis=1)
    rotated = (x * cosine + pltpu.roll(x, 32, 1) * sine)[:, :D_ROPE].astype(bf16)
    latent = comp_ref[:, :D_LAT]
    for i in range(N_CHIP):
        out_ref[i, :, :D_LAT] = latent
        out_ref[i, :, D_LAT:] = rotated


def absorb_kernel(qn_ref, qr_ref, go_ref, uk_ref, uv_ref, cos_ref, sin_ref,
                  qt_ref, qa_ref, gt_ref, ga_ref, tall):
    contract = (((1,), (1,)), ((), ()))
    x = qr_ref[...].astype(f32)
    rotated = x * cos_ref[...] + swap_halves(x) * sin_ref[...]
    turned = pltpu.roll(rotated, HALF, 1)
    for h in range(2):
        cols = slice(h * D_NOPE, (h + 1) * D_NOPE)
        q = lax.dot_general(qn_ref[:, cols], uk_ref[:, cols], contract, preferred_element_type=f32)
        g = lax.dot_general(go_ref[:, cols], uv_ref[:, cols], contract, preferred_element_type=f32)
        rope = rotated if h == 0 else turned
        for j in range(2):
            src = slice(j * HALF, (j + 1) * HALF)
            dst = slice(h * HALF, (h + 1) * HALF)
            tall[j, dst, :D_LAT] = q[src]
            tall[j, dst, D_LAT:D_LAT + 128] = rope[src]
            tall[j, dst, D_LAT + 128:] = g[src]
    for j in range(2):
        both = tall[j, :, :D_LAT + 128]
        qa_ref[j] = (both[:, :D_ALL] * SCALE).astype(bf16)
        ga_ref[j] = tall[j, :, D_LAT + 128:].astype(bf16)
        for k in range(4):
            piece = slice(k * 128, (k + 1) * 128)
            qt_ref[j, piece, :] = (both[:, piece] * (SCALE * LOG2E)).T.astype(bf16)
            gt_ref[j, piece, :] = tall[j, :, D_LAT + 128 + k * 128:D_LAT + 256 + k * 128].T.astype(bf16)
        qt_ref[j, D_LAT:, :] = (both[:, D_LAT:] * (SCALE * LOG2E)).T[:D_ROPE].astype(bf16)


def sort_copies(bm_ref, core, mine_ref, other_ref, keys, sems):
    for chip in range(N_CHIP):
        for j in range(2):
            for k, ref in enumerate((mine_ref, other_ref)):
                row = 2 * chip + (core ^ k)
                block = bm_ref[row, j]
                yield pltpu.make_async_copy(
                    ref.at[chip, pl.ds(j * HALF, HALF)],
                    keys.at[pl.ds(pl.multiple_of(block * HALF, HALF), HALF)],
                    sems.at[(chip * 2 + j) * 2 + k],
                )


def attend_kernel(bm_ref, rank_ref, mine_ref, other_ref, qt_hbm, qa_hbm, gt_hbm, ga_hbm,
                  dmine_ref, dother_ref, ds_hbm,
                  keys, qt, qa, gt, ga, probs, dprobs, tops, dlat, dlat_out, ds, place,
                  key_sems, load_sems, out_sems, ds_sems):
    rank = rank_ref[0]
    core = rank & 1
    loads = [
        pltpu.make_async_copy(src, dst, load_sems.at[i])
        for i, (src, dst) in enumerate(((qt_hbm, qt), (gt_hbm, gt), (qa_hbm, qa), (ga_hbm, ga)))
    ]
    copies = list(sort_copies(bm_ref, core, mine_ref, other_ref, keys, key_sems))
    loads[0].start()
    for copy in copies:
        copy.start()
    for load in loads[1:]:
        load.start()
    for row in range(N_CTX):
        for j in range(2):
            place[bm_ref[row, j]] = row * 2 + j
    dlat[...] = jnp.zeros_like(dlat)
    loads[0].wait()
    for copy in copies:
        copy.wait()
    loads[1].wait()

    first, second = bm_ref[rank, 0], bm_ref[rank, 1]
    low_j = jnp.where(first < second, 0, 1)
    low, high = jnp.minimum(first, second), jnp.maximum(first, second)

    def half_pass(j, block, emit):
        count = (block + PER_CHUNK) // PER_CHUNK

        def scores_step(c, carry):
            top, total, weighted = carry
            rows = pl.ds(pl.multiple_of(c * CHUNK, CHUNK), CHUNK)
            scores = jnp.dot(keys[rows, :], qt[j], preferred_element_type=f32)
            dp = jnp.dot(keys[rows, :D_LAT], gt[j], preferred_element_type=f32)
            key_at = lax.broadcasted_iota(jnp.int32, (CHUNK, LANES), 0) + c * CHUNK
            query_at = (lax.broadcasted_iota(jnp.int32, (CHUNK, LANES), 1) & (HALF - 1)) + block * HALF
            scores = jnp.where(key_at <= query_at, scores, HIDDEN)
            new_top = jnp.maximum(top, jnp.max(scores, axis=0, keepdims=True))
            e = jnp.exp2(scores - new_top)
            keep = jnp.exp2(top - new_top)
            probs[rows, :] = e
            dprobs[rows, :] = dp
            tops[c] = new_top
            total = total * keep + jnp.sum(e, axis=0, keepdims=True)
            weighted = weighted * keep + jnp.sum(e * dp, axis=0, keepdims=True)
            return new_top, total, weighted

        zero = jnp.zeros((1, LANES), f32)
        top, total, weighted = lax.fori_loop(
            0, count, scores_step, (jnp.full((1, LANES), HIDDEN, f32), zero, zero)
        )
        inverse = 1.0 / total
        delta = weighted * inverse

        def grads_step(c, carry):
            rows = pl.ds(pl.multiple_of(c * CHUNK, CHUNK), CHUNK)
            factor = jnp.exp2(tops[c] - top) * inverse
            p = probs[rows, :] * factor
            d = (p * (dprobs[rows, :] - delta)).astype(bf16)
            ds[j, rows, :] = d
            pltpu.make_async_copy(ds.at[j, rows], ds_hbm.at[j, rows], ds_sems.at[j, c]).start()
            part = jnp.dot(d, qa[j], preferred_element_type=f32)
            values = jnp.dot(p.astype(bf16), ga[j], preferred_element_type=f32)
            if emit is None:
                dlat[rows, :D_LAT] = part[:, :D_LAT] + values
                dlat[rows, D_LAT:] = part[:, D_LAT:]
            else:
                dlat_out[rows, :D_LAT] = (dlat[rows, :D_LAT] + part[:, :D_LAT] + values).astype(bf16)
                dlat_out[rows, D_LAT:] = (dlat[rows, D_LAT:] + part[:, D_LAT:]).astype(bf16)
                emit(c)
            return carry

        return count, grads_step

    def emit(c):
        for i in range(PER_CHUNK):
            block = c * PER_CHUNK + i
            src = dlat_out.at[pl.ds(pl.multiple_of(block * HALF, HALF), HALF)]
            at = place[block]
            row = at // 2
            rows = pl.ds(pl.multiple_of((at & 1) * HALF, HALF), HALF)
            ours = (row & 1) == core

            @pl.when(ours)
            def _():
                pltpu.make_async_copy(src, dmine_ref.at[row // 2, rows], out_sems.at[block]).start()

            @pl.when(jnp.logical_not(ours))
            def _():
                pltpu.make_async_copy(src, dother_ref.at[row // 2, rows], out_sems.at[block]).start()

    low_count, low_step = half_pass(low_j, low, None)
    loads[2].wait()
    loads[3].wait()
    lax.fori_loop(0, low_count, low_step, 0)
    high_count, high_step = half_pass(1 - low_j, high, emit)
    lax.fori_loop(0, high_count, high_step, 0)

    def blank_step(c, carry):
        dlat_out[pl.ds(pl.multiple_of(c * CHUNK, CHUNK), CHUNK), :] = jnp.zeros((CHUNK, D_ALL), bf16)
        emit(c)
        return carry

    lax.fori_loop(high_count, N_CHUNK, blank_step, 0)

    for block in range(N_BLOCK):
        pltpu.make_async_copy(
            dlat_out.at[pl.ds(block * HALF, HALF)], dmine_ref.at[0, pl.ds(0, HALF)], out_sems.at[block]
        ).wait()
    for j, count in ((low_j, low_count), (1 - low_j, high_count)):
        def wait_step(c, carry):
            rows = pl.ds(pl.multiple_of(c * CHUNK, CHUNK), CHUNK)
            pltpu.make_async_copy(ds.at[j, rows], ds_hbm.at[j, rows], ds_sems.at[j, c]).wait()
            return carry

        lax.fori_loop(0, count, wait_step, 0)


def queries_kernel(bm_ref, rank_ref, mine_ref, other_ref, ds_hbm, uk_ref, cos_ref, sin_ref,
                   gqn_ref, gqr_ref, keys, ds, total, key_sems, ds_sems):
    rank = rank_ref[0]
    copies = list(sort_copies(bm_ref, rank & 1, mine_ref, other_ref, keys, key_sems))
    for copy in copies:
        copy.start()

    def moves(j, c):
        rows = pl.ds(pl.multiple_of(c * CHUNK, CHUNK), CHUNK)
        return pltpu.make_async_copy(ds_hbm.at[j, rows], ds.at[j, rows], ds_sems.at[j, c])

    counts = [(bm_ref[rank, j] + PER_CHUNK) // PER_CHUNK for j in range(2)]
    for j in range(2):
        def start_step(c, carry):
            moves(j, c).start()
            return carry

        lax.fori_loop(0, counts[j], start_step, 0)
    for copy in copies:
        copy.wait()
    total[...] = jnp.zeros_like(total)
    for j in range(2):
        def step(c, carry):
            rows = pl.ds(pl.multiple_of(c * CHUNK, CHUNK), CHUNK)
            moves(j, c).wait()
            total[j] += lax.dot_general(
                ds[j, rows, :], keys[rows, :], (((0,), (0,)), ((), ())), preferred_element_type=f32
            )
            return carry

        lax.fori_loop(0, counts[j], step, 0)
    for pair in range(HEADS // 2):
        ropes = []
        for h in (2 * pair, 2 * pair + 1):
            rows = slice(h * HALF, (h + 1) * HALF)
            both = jnp.concatenate([total[0, rows, :], total[1, rows, :]], axis=0) * SCALE
            cols = slice(h * D_NOPE, (h + 1) * D_NOPE)
            gqn_ref[:, cols] = jnp.dot(
                both[:, :D_LAT].astype(bf16), uk_ref[:, cols], preferred_element_type=f32
            ).astype(bf16)
            ropes.append(both[:, D_LAT:])
        g = jnp.concatenate(ropes, axis=1)
        g = g * cos_ref[...] - swap_halves(g) * sin_ref[...]
        gqr_ref[:, pair * 128:(pair + 1) * 128] = g.astype(bf16)


def chips_kernel(parts_ref, cos_ref, sin_ref, out_ref):
    total = parts_ref[0].astype(f32)
    for i in range(1, N_CHIP):
        total = total + parts_ref[i].astype(f32)
    out_ref[:, :D_LAT] = total[:, :D_LAT].astype(bf16)
    g = total[:, D_LAT:]
    g = jnp.concatenate([g, g], axis=1)
    g = g * cos_ref[...] - pltpu.roll(g, 32, 1) * sin_ref[...]
    out_ref[:, D_LAT:] = g[:, :D_ROPE].astype(bf16)


def heads_kernel(parts_ref, out_ref):
    total = parts_ref[0].astype(f32)
    for i in range(1, N_HEAD):
        total = total + parts_ref[i].astype(f32)
    total = total.astype(bf16)
    for i in range(N_HEAD):
        out_ref[i] = total


def whole(count):
    return [pl.BlockSpec(memory_space=pltpu.VMEM)] * count


def params(mib):
    return pltpu.CompilerParams(vmem_limit_bytes=mib * 1024 * 1024)


ANY = pl.BlockSpec(memory_space=pl.ANY)
SMEM = pl.BlockSpec(memory_space=pltpu.SMEM)


def on_device(q_nope, q_rope, compressed, w_uk, w_uv, grad_out, positions, block_map):
    rank = lax.axis_index("ctx").astype(jnp.int32).reshape(1)
    shape = jax.ShapeDtypeStruct
    table = shape((ROWS, 128), f32)
    shared, cosine, sine = pl.pallas_call(
        share_kernel,
        in_specs=whole(3),
        out_specs=tuple(whole(3)),
        out_shape=(shape((N_CHIP, ROWS, D_ALL), bf16), table, table),
        name="share",
    )(positions.reshape(1, ROWS), jnp.asarray(frequencies()), compressed)
    mine = lax.all_to_all(shared, "ctx", 0, 0, axis_index_groups=CORES)
    other = lax.ppermute(mine, "ctx", SWAP)

    pair_cols = lambda width: pl.BlockSpec((ROWS, width), lambda p: (0, p))
    fixed = pl.BlockSpec((ROWS, 128), lambda p: (0, 0))
    weight = pl.BlockSpec((D_LAT, 256), lambda p: (0, p))
    wide = lambda rows: pl.BlockSpec((2, rows, 128), lambda p: (0, 0, p))
    tall = lambda cols: pl.BlockSpec((2, 128, cols), lambda p: (0, p, 0))
    qt, qa, gt, ga = pl.pallas_call(
        absorb_kernel,
        grid=(HEADS // 2,),
        in_specs=[pair_cols(256), pair_cols(128), pair_cols(256), weight, weight, fixed, fixed],
        out_specs=(wide(D_ALL), tall(D_ALL), wide(D_LAT), tall(D_LAT)),
        out_shape=(
            shape((2, D_ALL, LANES), bf16),
            shape((2, LANES, D_ALL), bf16),
            shape((2, D_LAT, LANES), bf16),
            shape((2, LANES, D_LAT), bf16),
        ),
        scratch_shapes=[pltpu.VMEM((2, 128, 2 * D_LAT + 128), f32)],
        compiler_params=params(32),
        cost_estimate=pl.CostEstimate(flops=300_000_000, bytes_accessed=8_000_000, transcendentals=0),
        name="absorb",
    )(q_nope, q_rope, grad_out, w_uk, w_uv, cosine, sine)

    piece = shape((N_CHIP, ROWS, D_ALL), bf16)
    dma = pltpu.SemaphoreType.DMA
    dmine, dother, ds = pl.pallas_call(
        attend_kernel,
        in_specs=[SMEM, SMEM] + [ANY] * 6,
        out_specs=(ANY, ANY, ANY),
        out_shape=(piece, piece, shape((2, TOTAL, LANES), bf16)),
        scratch_shapes=[
            pltpu.VMEM((TOTAL, D_ALL), bf16),
            pltpu.VMEM((2, D_ALL, LANES), bf16),
            pltpu.VMEM((2, LANES, D_ALL), bf16),
            pltpu.VMEM((2, D_LAT, LANES), bf16),
            pltpu.VMEM((2, LANES, D_LAT), bf16),
            pltpu.VMEM((TOTAL, LANES), f32),
            pltpu.VMEM((TOTAL, LANES), f32),
            pltpu.VMEM((N_CHUNK, 1, LANES), f32),
            pltpu.VMEM((TOTAL, D_ALL), f32),
            pltpu.VMEM((TOTAL, D_ALL), bf16),
            pltpu.VMEM((2, TOTAL, LANES), bf16),
            pltpu.SMEM((N_BLOCK,), jnp.int32),
            dma((N_BLOCK,)),
            dma((4,)),
            dma((N_BLOCK,)),
            dma((2, N_CHUNK)),
        ],
        compiler_params=params(48),
        name="attend",
    )(block_map, rank, mine, other, qt, qa, gt, ga)

    theirs = lax.ppermute(dother, "ctx", SWAP)
    summed = (dmine.astype(f32) + theirs.astype(f32)).astype(bf16)
    parts = lax.all_to_all(summed, "ctx", 0, 0, axis_index_groups=CORES)

    grad_q_nope, grad_q_rope = pl.pallas_call(
        queries_kernel,
        in_specs=[SMEM, SMEM] + [ANY] * 3 + whole(3),
        out_specs=tuple(whole(2)),
        out_shape=(shape((ROWS, HEADS * D_NOPE), bf16), shape((ROWS, HEADS * D_ROPE), bf16)),
        scratch_shapes=[
            pltpu.VMEM((TOTAL, D_ALL), bf16),
            pltpu.VMEM((2, TOTAL, LANES), bf16),
            pltpu.VMEM((2, LANES, D_ALL), f32),
            dma((N_BLOCK,)),
            dma((2, N_CHUNK)),
        ],
        compiler_params=params(32),
        cost_estimate=pl.CostEstimate(flops=4_000_000_000, bytes_accessed=9_000_000, transcendentals=0),
        name="queries",
    )(block_map, rank, mine, other, ds, w_uk, cosine, sine)

    owned = pl.pallas_call(
        chips_kernel,
        in_specs=whole(3),
        out_specs=whole(1)[0],
        out_shape=shape((ROWS, D_ALL), bf16),
        name="chips",
    )(parts, cosine, sine)
    slabs = lax.all_to_all(owned.reshape(N_HEAD, ROWS // N_HEAD, D_ALL), "head", 0, 0)
    slabs = pl.pallas_call(
        heads_kernel,
        in_specs=whole(1),
        out_specs=whole(1)[0],
        out_shape=shape((N_HEAD, ROWS // N_HEAD, D_ALL), bf16),
        name="heads",
    )(slabs)
    grad_compressed = lax.all_to_all(slabs, "head", 0, 0).reshape(ROWS, D_ALL)
    return grad_q_nope, grad_q_rope, grad_compressed


def solution(mesh):
    in_specs = (
        P("ctx", "head"),
        P("ctx", "head"),
        P("ctx", None),
        P(None, "head"),
        P(None, "head"),
        P("ctx", "head"),
        P("ctx"),
        P(),
    )
    out_specs = (P("ctx", "head"), P("ctx", "head"), P("ctx", None))
    return jax.shard_map(
        on_device, mesh=mesh, in_specs=in_specs, out_specs=out_specs, check_vma=False
    )
```

time: 555 us -> 139 us (0.25)
  waiting for transfers between devices: 318 us -> 2.82 us
  matrix products: 73.1 us -> 0 us
  Pallas kernels: 0 us -> 36.4 us
  other arithmetic: 29.6 us -> 1.46 us
  blocking collectives: 87.2 us -> 63.5 us
  between operations: 14.3 us -> 0.81 us
    psum x1 -> x0, waiting for transfers between devices: 134 us -> none  [on_device(): lax.psum(grad_lat.astype(jnp.bfloat16), 'head').astype(jnp.float32)]
    unnamed x9 -> x0, waiting for transfers between devices: 132 us -> none
    dot_general x12 -> x0, matrix products: 73.1 us -> none  [the longest x1 13.1 us: on_device(): jnp.einsum('hts,thd->shd', dscores, query_plain, preferred_element_type=j...]
    psum x1 -> x0, blocking collectives: 63.9 us -> none  [on_device(): lax.psum(mine_rot.astype(jnp.bfloat16), 'head').astype(jnp.float32)]
    all_to_all x0 -> x3, blocking collectives: none -> 63.5 us  [the longest x1 23.5 us: on_device(): mine = lax.all_to_all(shared, 'ctx', 0, 0, axis_index_groups=CORES)]
    all_gather x2 -> x0, waiting for transfers between devices: 52 us -> none  [the longest x1 44.8 us: on_device(): lax.all_gather(values_own, 'ctx', axis=0, tiled=True)]
    pallas_call x0 -> x6, Pallas kernels: none -> 36.4 us  [the longest x1 17.2 us: on_device(): pl.pallas_call(attend_kernel, in_specs=[SMEM, SMEM] + [ANY] * 6, out_spec...]
    all_gather x1 -> x0, blocking collectives: 23.3 us -> none  [on_device(): lax.all_gather(k_rot_own, 'ctx', axis=0, tiled=True)]
  transfers between devices with their start and end apart: 6 -> 3, of which waited for: 6 -> 1; matrix products, arithmetic and copies ran while one was open for 19% -> 2% of each run, Pallas kernels for 0% -> 9%
where the time goes in v1:
time: 139 us; the launch traced here: 137 us
  blocking collectives  63.5 us (46%)
  Pallas kernels  36.4 us (26%)
  local copies, waits for them, and re-layouts  27.6 us (20%)
  starting transfers between devices  4.09 us (3%)
  waiting for transfers between devices  2.82 us (2%)
  other arithmetic  1.46 us (1%)
    all_to_all x1, blocking collectives, on_device(): mine = lax.all_to_all(shared, 'ctx', 0, 0, axis_index_groups=CORES)  23.5 us
    all_to_all x1, blocking collectives, on_device(): parts = lax.all_to_all(summed, 'ctx', 0, 0, axis_index_groups=CORES)  21.8 us
    all_to_all x1, blocking collectives, on_device(): lax.all_to_all(owned.reshape(N_HEAD, ROWS // N_HEAD, D_ALL), 'head', 0, 0)  18.2 us
    pallas_call x1, Pallas kernels, on_device(): pl.pallas_call(attend_kernel, in_specs=[SMEM, SMEM] + [ANY] * 6, out_spec...  17.2 us
    unnamed x45, local copies, waits for them, and re-layouts  13.9 us
    pallas_call x1, Pallas kernels, on_device(): pl.pallas_call(queries_kernel, in_specs=[SMEM, SMEM] + [ANY] * 3 + whole(...  10 us
    all_to_all x1, starting transfers between devices, on_device(): grad_compressed = lax.all_to_all(slabs, 'head', 0, 0).reshape(ROWS, D_ALL)  3.52 us
    pallas_call x1, Pallas kernels, on_device(): pl.pallas_call(absorb_kernel, grid=(HEADS // 2,), in_specs=[pair_cols(256...  2.84 us
  transfers between devices with their start and end apart: 3, of which 1 were waited for; matrix products, arithmetic and copies ran while one was open for 2% of the time, Pallas kernels for 9%

profile of v1, /device:TPU:4, one launch (start us, length us, event | category | flops | bytes accessed | tf_op | source)
XLA Modules:
  0.0 136.6 jit_solution(10498520697849247833)
XLA Ops:
  0.6 1.7 %copy.16.comp_ref = bf16[128,576]{1,0:T(8,128)(2,1)} copy(bf16[128,576]{0,1:T(8,128)(2,1)} %param.11) | data formatting | bytes 294912 | tf_op args[2]
  2.3 2.3 %share.1 = (bf16[8,128,576]{2,1,0:T(8,128)(2,1)}, f32[128,128]{1,0:T(8,128)}, f32[128,128]{1,0:T(8,128)}) custom-call(s32[1,128]{1,0:T(1,128)} %bitcast.6, f32[1,128]{1,0:T(1,128)} %constant.7.clone.inv_ref, bf16[128,576]{1,0:T(8,128)(2,1)} %copy.16.comp_ref), custom_call_target="tpu_custom_call" | custom-call | tf_op jit(solution)/shard_map/share/pallas_call | solution.py:359
  4.7 2.5 %copy.17 = bf16[8,128,576]{1,2,0:T(8,128)(2,1)} copy(bf16[8,128,576]{2,1,0:T(8,128)(2,1)} %get-tuple-element.15) | data formatting | bytes 2359296 | tf_op jit(solution)/shard_map/share/pallas_call | solution.py:359
  7.2 23.5 %all_to_all.20 = bf16[8,128,576]{1,2,0:T(8,128)(2,1)} all-to-all(bf16[8,128,576]{1,2,0:T(8,128)(2,1)} %copy.17), channel_id=1, replica_groups={{0,32,64,96,128,160,192,224},{16,48,80,112,144,176,208,240},{1,33,65,97..., dimensions={0} | all-to-all | bytes 2359296 | tf_op jit(solution)/shard_map/all_to_all | solution.py:366
  30.6 0.1 copy.21.bm_ref
  30.8 2.8 %absorb.1 = (bf16[2,576,512]{2,1,0:T(8,128)(2,1)S(1)}, bf16[2,512,576]{2,1,0:T(8,128)(2,1)S(1)}, bf16[2,512,512]{2,1,0:T(8,128)(2,1)S(1)}, bf16[2,512,512]{2,1,0:T(8,128)(2,1)S(1)}) custom-call(bf16[128,1024]{1,0:T(8,128)(2,1)S(1)} %copy-done.16, bf16[128,512]{1,0:T(8,128)(2,1)S(1)} %copy-done.18, bf16[128,1024]{1,0:T(8,128)(2,1)S(1)} %copy-done.17, ...), custom_call_target="tpu_custom_call" | custom-call | flops 300000000 | bytes 8000000 | tf_op jit(solution)/shard_map/absorb/pallas_call | solution.py:374
  33.6 1.1 copy-done.2
  34.7 1.0 copy-done.3
  35.7 1.0 copy-done.8
  36.7 1.1 copy-done.10
  37.8 2.4 %copy.22.mine_ref = bf16[8,128,576]{2,1,0:T(8,128)(2,1)} copy(bf16[8,128,576]{1,2,0:T(8,128)(2,1)} %all_to_all.20) | data formatting | bytes 2359296 | tf_op jit(solution)/shard_map/all_to_all | solution.py:366
  40.2 2.4 %copy.23.other_ref = bf16[8,128,576]{2,1,0:T(8,128)(2,1)} copy(bf16[8,128,576]{1,2,0:T(8,128)(2,1)} %collective-permute-done) | data formatting | bytes 2359296 | tf_op jit(solution)/shard_map/ppermute | solution.py:367
  42.7 1.3 copy-done.4
  43.9 1.2 copy-done.9
  45.1 1.2 copy-done.11
  46.4 17.2 %attend.1 = (bf16[8,128,576]{2,1,0:T(8,128)(2,1)S(1)}, bf16[8,128,576]{2,1,0:T(8,128)(2,1)S(1)}, bf16[2,2048,512]{2,1,0:T(8,128)(2,1)}) custom-call(s32[16,2]{1,0:T(8,128)S(1)} %copy.21.bm_ref, s32[1]{0:T(128)} %bitcast.rank_ref, bf16[8,128,576]{2,1,0:T(8,128)(2,1)} %copy.22.mine_ref, bf16[8,128,576]{2,1,0:T(8,128)(2,1)} %copy.23.other_ref, ...), custom_call_target="tpu_custom_call" | custom-call | tf_op jit(solution)/shard_map/attend/pallas_call | solution.py:393
  63.6 1.5 %copy.24 = bf16[8,128,576]{1,2,0:T(8,128)(2,1)} copy(bf16[8,128,576]{2,1,0:T(8,128)(2,1)S(1)} %get-tuple-element.26) | data formatting | bytes 2359296 | tf_op jit(solution)/shard_map/attend/pallas_call | solution.py:393
  65.0 0.6 collective-permute-start.1
  65.6 2.8 %collective-permute-done.1 = bf16[8,128,576]{1,2,0:T(8,128)(2,1)} collective-permute-done((bf16[8,128,576]{1,2,0:T(8,128)(2,1)}, bf16[8,128,576]{1,2,0:T(8,128)(2,1)}, u32[]{:S(2)}, u32[]{:S(2)}) %collective-permute-start.1) | collective-permute-done | bytes 1179680 | tf_op jit(solution)/shard_map/ppermute | solution.py:420
  68.4 1.7 %copy.25 = bf16[8,128,576]{2,1,0:T(8,128)(2,1)S(1)} copy(bf16[8,128,576]{1,2,0:T(8,128)(2,1)} %collective-permute-done.1) | data formatting | bytes 2359296 | tf_op jit(solution)/shard_map/ppermute | solution.py:420
  70.1 1.5 %add_convert_fusion = bf16[8,128,576]{2,1,0:T(8,128)(2,1)} fusion(bf16[8,128,576]{2,1,0:T(8,128)(2,1)S(1)} %copy.25, bf16[8,128,576]{2,1,0:T(8,128)(2,1)S(1)} %get-tuple-element.25), kind=kLoop, calls=%fused_computation | loop fusion | flops 2359296 | bytes 3538944 | tf_op jit(solution)/shard_map/convert_element_type | solution.py:421
  71.6 1.7 %copy.26 = bf16[8,128,576]{1,2,0:T(8,128)(2,1)S(1)} copy(bf16[8,128,576]{2,1,0:T(8,128)(2,1)} %add_convert_fusion) | data formatting | bytes 2359296 | tf_op jit(solution)/shard_map/convert_element_type | solution.py:421
  73.3 21.8 %all_to_all.21 = bf16[8,128,576]{1,2,0:T(8,128)(2,1)S(1)} all-to-all(bf16[8,128,576]{1,2,0:T(8,128)(2,1)S(1)} %copy.26), channel_id=1, replica_groups={{0,32,64,96,128,160,192,224},{16,48,80,112,144,176,208,240},{1,33,65,97..., dimensions={0} | all-to-all | bytes 2359296 | tf_op jit(solution)/shard_map/all_to_all | solution.py:422
  95.1 1.5 %copy.27.parts_ref = bf16[8,128,576]{2,1,0:T(8,128)(2,1)} copy(bf16[8,128,576]{1,2,0:T(8,128)(2,1)S(1)} %all_to_all.21) | data formatting | bytes 2359296 | tf_op jit(solution)/shard_map/all_to_all | solution.py:422
  96.6 2.4 %chips.1 = bf16[128,576]{1,0:T(8,128)(2,1)} custom-call(bf16[8,128,576]{2,1,0:T(8,128)(2,1)} %copy.27.parts_ref, f32[128,128]{1,0:T(8,128)} %get-tuple-element.16.cos_ref, f32[128,128]{1,0:T(8,128)} %get-tuple-element.17.sin_ref), custom_call_target="tpu_custom_call" | custom-call | tf_op jit(solution)/shard_map/chips/pallas_call | solution.py:441
  99.0 18.2 %all_to_all.22.parts_ref = bf16[16,8,576]{2,1,0:T(8,128)(2,1)} all-to-all(bf16[16,8,576]{2,1,0:T(8,128)(2,1)} %bitcast.4), channel_id=1, replica_groups=mesh['ctx'=16,'head'=16] {'head'}, dimensions={0} | all-to-all | bytes 294912 | tf_op jit(solution)/shard_map/all_to_all | solution.py:448
  117.2 1.6 %heads.1 = bf16[16,8,576]{2,1,0:T(8,128)(2,1)} custom-call(bf16[16,8,576]{2,1,0:T(8,128)(2,1)} %all_to_all.22.parts_ref), custom_call_target="tpu_custom_call" | custom-call | tf_op jit(solution)/shard_map/heads/pallas_call | solution.py:449
  118.8 3.5 %all-to-all-start.3 = ((bf16[16,8,576]{2,1,0:T(8,128)(2,1)}), bf16[16,8,576]{2,1,0:T(8,128)(2,1)S(1)}, u32[]{:S(2)}, u32[]{:S(2)}) async-start(bf16[16,8,576]{2,1,0:T(8,128)(2,1)} %heads.1), calls=%async_computation.3 | async-start | bytes 327680 | tf_op jit(solution)/shard_map/all_to_all | solution.py:456
  122.4 1.2 copy-done.7
  123.6 2.2 %copy-done.19 = bf16[2,2048,512]{2,1,0:T(8,128)(2,1)S(1)} copy-done((bf16[2,2048,512]{2,1,0:T(8,128)(2,1)S(1)}, bf16[2,2048,512]{2,1,0:T(8,128)(2,1)}, u32[]{:S(2)}) %copy-start.19) | copy-done | bytes 4194328
  125.8 10.0 %queries.1 = (bf16[128,1024]{1,0:T(8,128)(2,1)}, bf16[128,512]{1,0:T(8,128)(2,1)}) custom-call(s32[16,2]{1,0:T(8,128)S(1)} %copy.21.bm_ref, s32[1]{0:T(128)} %bitcast.rank_ref, bf16[8,128,576]{2,1,0:T(8,128)(2,1)S(1)} %copy-done, bf16[8,128,576]{2,1,0:T(8,128)(2,1)S(1)} %copy-done.1, bf16[2,2048,512]{2,1,0:T(8,128)(2,1)S(1)} %copy-done.19, ...), custom_call_target="tpu_custom_call" | custom-call | flops 4000000000 | bytes 9000000 | tf_op jit(solution)/shard_map/queries/pallas_call | solution.py:424
  135.9 0.8 copy.28
  (36 shorter events, 0.1 us)
Async XLA Ops:
  4.7 26.0 %copy-start.16 = (bf16[128,1024]{1,0:T(8,128)(2,1)S(1)}, bf16[128,1024]{1,0:T(8,128)(2,1)}, u32[]{:S(2)}) copy-start(bf16[128,1024]{1,0:T(8,128)(2,1)} %qn_ref.1) | copy-start | bytes 786436
  4.7 26.0 %copy-start.17 = (bf16[128,1024]{1,0:T(8,128)(2,1)S(1)}, bf16[128,1024]{1,0:T(8,128)(2,1)}, u32[]{:S(2)}) copy-start(bf16[128,1024]{1,0:T(8,128)(2,1)} %go_ref.1) | copy-start | bytes 786436
  7.1 23.5 %copy-start.20 = (s32[16,2]{0,1:T(2,128)S(1)}, s32[16,2]{0,1:T(2,128)}, u32[]{:S(2)}) copy-start(s32[16,2]{0,1:T(2,128)} %param.16) | copy-start | bytes 388
  7.1 23.6 %copy-start.5 = (bf16[512,1024]{1,0:T(8,128)(2,1)S(1)}, bf16[512,1024]{1,0:T(8,128)(2,1)}, u32[]{:S(2)}) copy-start(bf16[512,1024]{1,0:T(8,128)(2,1)} %uv_ref.1) | copy-start | bytes 3145732
  7.1 23.6 %copy-start.6 = (bf16[512,1024]{1,0:T(8,128)(2,1)S(1)}, bf16[512,1024]{1,0:T(8,128)(2,1)}, u32[]{:S(2)}) copy-start(bf16[512,1024]{1,0:T(8,128)(2,1)} %uk_ref.3) | copy-start | bytes 3145732
  7.1 23.6 %copy-start.12 = (f32[128,128]{1,0:T(8,128)S(1)}, f32[128,128]{1,0:T(8,128)}, u32[]{:S(2)}) copy-start(f32[128,128]{1,0:T(8,128)} %get-tuple-element.16.cos_ref) | copy-start | bytes 196612
  7.2 23.6 %copy-start.14 = (f32[128,128]{1,0:T(8,128)S(1)}, f32[128,128]{1,0:T(8,128)}, u32[]{:S(2)}) copy-start(f32[128,128]{1,0:T(8,128)} %get-tuple-element.17.sin_ref) | copy-start | bytes 196612
  7.2 23.6 %copy-start.18 = (bf16[128,512]{1,0:T(8,128)(2,1)S(1)}, bf16[128,512]{1,0:T(8,128)(2,1)}, u32[]{:S(2)}) copy-start(bf16[128,512]{1,0:T(8,128)(2,1)} %qr_ref.1) | copy-start | bytes 393220
  30.6 9.6 %collective-permute-start = (bf16[8,128,576]{1,2,0:T(8,128)(2,1)}, bf16[8,128,576]{1,2,0:T(8,128)(2,1)}, u32[]{:S(2)}, u32[]{:S(2)}) collective-permute-start(bf16[8,128,576]{1,2,0:T(8,128)(2,1)} %all_to_all.20), channel_id=1, source_target_pairs={{0,16},{16,0},{32,48},{48,32},{64,80},{80,64},{96,112},{112,96},{1... | collective-permute-start | bytes 3538952 | tf_op jit(solution)/shard_map/ppermute | solution.py:367
  33.6 1.1 copy-start.2
  34.7 1.0 copy-start.3
  35.7 1.0 copy-start.8
  36.7 1.1 copy-start.10
  42.6 1.3 copy-start.4
  43.9 1.2 copy-start.9
  45.1 1.2 copy-start.11
  65.0 3.4 %collective-permute-start.1 = (bf16[8,128,576]{1,2,0:T(8,128)(2,1)}, bf16[8,128,576]{1,2,0:T(8,128)(2,1)}, u32[]{:S(2)}, u32[]{:S(2)}) collective-permute-start(bf16[8,128,576]{1,2,0:T(8,128)(2,1)} %copy.24), channel_id=1, source_target_pairs={{0,16},{16,0},{32,48},{48,32},{64,80},{80,64},{96,112},{112,96},{1... | collective-permute-start | bytes 3538952 | tf_op jit(solution)/shard_map/ppermute | solution.py:420
  95.1 27.3 %copy-start.1 = (bf16[8,128,576]{2,1,0:T(8,128)(2,1)S(1)}, bf16[8,128,576]{2,1,0:T(8,128)(2,1)}, u32[]{:S(2)}) copy-start(bf16[8,128,576]{2,1,0:T(8,128)(2,1)} %copy.23.other_ref) | copy-start | bytes 3538948
  96.6 25.8 %copy-start = (bf16[8,128,576]{2,1,0:T(8,128)(2,1)S(1)}, bf16[8,128,576]{2,1,0:T(8,128)(2,1)}, u32[]{:S(2)}) copy-start(bf16[8,128,576]{2,1,0:T(8,128)(2,1)} %copy.22.mine_ref) | copy-start | bytes 3538948
  96.6 25.8 %copy-start.13 = (f32[128,128]{1,0:T(8,128)S(1)}, f32[128,128]{1,0:T(8,128)}, u32[]{:S(2)}) copy-start(f32[128,128]{1,0:T(8,128)} %get-tuple-element.16.cos_ref) | copy-start | bytes 196612
  96.6 25.8 %copy-start.15 = (f32[128,128]{1,0:T(8,128)S(1)}, f32[128,128]{1,0:T(8,128)}, u32[]{:S(2)}) copy-start(f32[128,128]{1,0:T(8,128)} %get-tuple-element.17.sin_ref) | copy-start | bytes 196612
  118.8 17.0 %all-to-all-start.3 = ((bf16[16,8,576]{2,1,0:T(8,128)(2,1)}), bf16[16,8,576]{2,1,0:T(8,128)(2,1)S(1)}, u32[]{:S(2)}, u32[]{:S(2)}) async-start(bf16[16,8,576]{2,1,0:T(8,128)(2,1)} %heads.1), calls=%async_computation.3 | async-start | bytes 327680 | tf_op jit(solution)/shard_map/all_to_all | solution.py:456
  122.4 1.2 copy-start.7
  123.6 2.2 %copy-start.19 = (bf16[2,2048,512]{2,1,0:T(8,128)(2,1)S(1)}, bf16[2,2048,512]{2,1,0:T(8,128)(2,1)}, u32[]{:S(2)}) copy-start(bf16[2,2048,512]{2,1,0:T(8,128)(2,1)} %get-tuple-element.22.ds_hbm) | copy-start | bytes 12582916

commit v2 on v1

v2 whole, which is shorter than its diff:
```python
import math

import jax
import jax.numpy as jnp
import numpy as np
from jax import lax
from jax.experimental import pallas as pl
from jax.experimental.pallas import tpu as pltpu
from jax.sharding import PartitionSpec as P

D_NOPE = 128
D_ROPE = 64
D_V = 128
D_LAT = 512
D_ALL = D_LAT + D_ROPE
D_PAD = D_LAT + 128
PACKED = 144
N_CTX = 16
N_CHIP = 8
N_HEAD = 16
ROWS = 128
HALF = 64
TOTAL = ROWS * N_CTX
HEADS = 8
LANES = HEADS * HALF
CHUNK = 256
N_CHUNK = TOTAL // CHUNK
PER_CHUNK = CHUNK // HALF
N_BLOCK = TOTAL // HALF
STEPS = N_CHUNK + 1

SCALE = (D_NOPE + D_ROPE) ** (-0.5) * (0.1 * math.log(40.0) + 1.0) ** 2
LOG2E = math.log2(math.e)
HIDDEN = -1e30

GROUPS = [
    [c * N_HEAD + ((c // 8) ^ side) * 8 + z for c in range(core, N_CTX, 2)]
    for core in range(2)
    for side in range(2)
    for z in range(8)
]
SWAP = [(c, c ^ 1) for c in range(N_CTX)]

bf16 = jnp.bfloat16
f32 = jnp.float32


def frequencies():
    half = D_ROPE // 2
    index = np.arange(half, dtype=np.float64)
    width = 2 * half
    extra = np.power(10000.0, -2.0 * index / width)
    inter = extra / 40.0
    lower = math.floor(width * math.log(4096.0 / (32.0 * 2.0 * math.pi)) / (2.0 * math.log(10000.0)))
    upper = math.ceil(width * math.log(4096.0 / (1.0 * 2.0 * math.pi)) / (2.0 * math.log(10000.0)))
    lower = max(lower, 0)
    upper = min(upper, half - 1)
    spread = max(upper - lower, 0.001)
    ramp = np.clip((index - lower) / spread, 0.0, 1.0)
    inv = inter * ramp + extra * (1.0 - ramp)
    return np.tile(inv, 4).astype(np.float32)[None, :]


def split_half_pi():
    rest = math.pi / 2
    parts = []
    for bits in (9, 19):
        part = math.floor(rest * 2.0**bits) / 2.0**bits
        parts.append(part)
        rest -= part
    return parts + [rest]


HALF_PI = split_half_pi()


def cos_sin(angle):
    turns = jnp.floor(angle * (2.0 / math.pi) + 0.5)
    r = angle - turns * HALF_PI[0]
    r = r - turns * HALF_PI[1]
    r = r - turns * HALF_PI[2]
    r2 = r * r
    sine = r + r * r2 * (-1.0 / 6 + r2 * (1.0 / 120 + r2 * (-1.0 / 5040 + r2 * (1.0 / 362880))))
    cosine = 1.0 + r2 * (-0.5 + r2 * (1.0 / 24 + r2 * (-1.0 / 720 + r2 * (1.0 / 40320))))
    quarter = turns.astype(jnp.int32) & 3
    odd = (quarter & 1) == 1
    cos_out = jnp.where(odd, sine, cosine)
    sin_out = jnp.where(odd, cosine, sine)
    cos_out = jnp.where((quarter == 1) | (quarter == 2), -cos_out, cos_out)
    sin_out = jnp.where(quarter >= 2, -sin_out, sin_out)
    return cos_out, sin_out


def lanes_of(shape):
    return lax.broadcasted_iota(jnp.int32, shape, 1)


def swap_halves(x):
    return jnp.where((lanes_of(x.shape) & 63) < 32, pltpu.roll(x, 96, 1), pltpu.roll(x, 32, 1))


def pair_tile(first, second, half):
    low = lanes_of(first.shape) < HALF
    if half == 0:
        return jnp.where(low, first, pltpu.roll(second, HALF, 1))
    return jnp.where(low, pltpu.roll(first, HALF, 1), second)


def pack_rope(rope):
    low = lanes_of((16, 128)) < D_ROPE
    tiles = []
    for m in (0, 2):
        tiles.append(jnp.where(low, rope[16 * m:16 * m + 16], pltpu.roll(rope[16 * m + 16:16 * m + 32], D_ROPE, 1)))
    return jnp.concatenate(tiles, axis=1)


def unpack_rope(packed):
    low = lanes_of((16, 128)) < D_ROPE
    pieces = []
    for m in range(4):
        tile = packed[:, (m // 2) * 128:(m // 2 + 1) * 128]
        pieces.append(jnp.where(low, pltpu.roll(tile, D_ROPE, 1) if m % 2 else tile, 0.0))
    return jnp.concatenate(pieces, axis=0)


def share_kernel(rank_ref, pos_ref, inv_ref, comp_ref, out_ref, cos_ref, sin_ref, tile):
    pos = jnp.broadcast_to(pos_ref[...].astype(f32), (ROWS, ROWS)).T
    cosine, sine = cos_sin(pos * inv_ref[...])
    sine = jnp.where((lanes_of(sine.shape) & 63) < 32, -sine, sine)
    for k in range(D_LAT // 128):
        piece = slice(k * 128, (k + 1) * 128)
        tile[:ROWS, piece] = comp_ref[piece, :].astype(f32).T.astype(bf16)
    x = comp_ref[D_LAT:, :].astype(f32)
    x = jnp.concatenate([x, x], axis=0).T
    rotated = x * cosine + pltpu.roll(x, 32, 1) * sine
    for j in range(2):
        tile[ROWS:, j * 256:(j + 1) * 256] = pack_rope(rotated[j * HALF:(j + 1) * HALF]).astype(bf16)
    for i in range(N_CHIP):
        out_ref[i] = tile[...]
    cos_ref[...] = cosine
    sin_ref[...] = sine


def absorb_kernel(qn_ref, qr_ref, go_ref, uk_ref, uv_ref, cos_ref, sin_ref,
                  qt_ref, qa_ref, gt_ref, ga_ref, tall):
    contract = (((1,), (1,)), ((), ()))
    x = qr_ref[...].astype(f32)
    rotated = x * cos_ref[...] + swap_halves(x) * sin_ref[...]
    turned = pltpu.roll(rotated, HALF, 1)
    for h in range(2):
        cols = slice(h * D_NOPE, (h + 1) * D_NOPE)
        q = lax.dot_general(qn_ref[:, cols], uk_ref[:, cols], contract, preferred_element_type=f32)
        g = lax.dot_general(go_ref[:, cols], uv_ref[:, cols], contract, preferred_element_type=f32)
        rope = jnp.where(lanes_of(x.shape) < D_ROPE, rotated if h == 0 else turned, 0.0)
        for j in range(2):
            src = slice(j * HALF, (j + 1) * HALF)
            dst = slice(h * HALF, (h + 1) * HALF)
            tall[j, dst, :D_LAT] = q[src]
            tall[j, dst, D_LAT:D_PAD] = rope[src]
            tall[j, dst, D_PAD:] = g[src]
    for j in range(2):
        both = tall[j, :, :D_PAD]
        qa_ref[j] = (both * SCALE).astype(bf16)
        ga_ref[j] = tall[j, :, D_PAD:].astype(bf16)
        for k in range(D_PAD // 128):
            piece = slice(k * 128, (k + 1) * 128)
            qt_ref[j, piece, :] = (both[:, piece] * (SCALE * LOG2E)).T.astype(bf16)
        for k in range(D_LAT // 128):
            piece = slice(k * 128, (k + 1) * 128)
            gt_ref[j, piece, :] = tall[j, :, D_PAD + k * 128:D_PAD + (k + 1) * 128].T.astype(bf16)


def step_places(bm_ref, rank):
    first, second = bm_ref[0, rank], bm_ref[1, rank]
    early = jnp.where(first < second, 0, 1)
    low, high = jnp.minimum(first, second), jnp.maximum(first, second)
    count = (low + PER_CHUNK) // PER_CHUNK
    places = [(True, early, 0, low)] + [(False, 1 - early, c, high) for c in range(5)]
    for k in range(1, 4):
        is_early = k < count
        places.append((
            is_early,
            jnp.where(is_early, early, 1 - early),
            jnp.where(is_early, k, N_CHUNK - k),
            jnp.where(is_early, low, high),
        ))
    return places


def pick(flag, first, second):
    if flag is True:
        return first
    if flag is False:
        return second
    return jnp.where(flag, first, second)


def chunk_rows(c):
    return pl.ds(c * CHUNK if isinstance(c, int) else pl.multiple_of(c * CHUNK, CHUNK), CHUNK)


def attend_kernel(bm_ref, rank_ref, mine_ref, other_ref, qt_hbm, qa_hbm, gt_hbm, ga_hbm,
                  dmine_ref, dother_ref, ds_hbm, keys_hbm,
                  qt, qa, gt, ga, probs, dprobs, tops, ds, keys, place, load_sems, key_sem, ds_sems):
    sources = ((qt_hbm, qt), (gt_hbm, gt), (qa_hbm, qa), (ga_hbm, ga))
    loads = [pltpu.make_async_copy(src, dst, load_sems.at[i]) for i, (src, dst) in enumerate(sources)]
    for load in loads:
        load.start()
    rank = rank_ref[0]
    core = rank & 1
    places = step_places(bm_ref, rank)
    for chip in range(N_CHIP):
        for k, ref in enumerate((mine_ref, other_ref)):
            row = 2 * chip + (core ^ k)
            for j in range(2):
                block = bm_ref[j, row]
                place[block] = row * 2 + j
                rows = pl.ds(pl.multiple_of(block * HALF, HALF), HALF)
                keys[rows, :D_LAT] = ref[chip, j * HALF:(j + 1) * HALF, :]
                packed = ref[chip, ROWS:, j * 256:(j + 1) * 256].astype(f32)
                keys[rows, D_LAT:] = unpack_rope(packed).astype(bf16)

    moves = [pltpu.make_async_copy(keys, keys_hbm, key_sem)]
    moves[0].start()
    loads[0].wait()
    loads[1].wait()

    zero = jnp.zeros((1, LANES), f32)
    start = (jnp.full((1, LANES), HIDDEN, f32), zero, zero)
    state = {True: start, False: start}
    offset = lax.broadcasted_iota(jnp.int32, (CHUNK, LANES), 0) - (
        lax.broadcasted_iota(jnp.int32, (CHUNK, LANES), 1) & (HALF - 1)
    )
    for i, (is_early, j, c, block) in enumerate(places):
        rows = chunk_rows(c)
        top, total, weighted = (pick(is_early, a, b) for a, b in zip(state[True], state[False]))
        scores = jnp.dot(keys[rows, :], qt[j], preferred_element_type=f32)
        dp = jnp.dot(keys[rows, :D_LAT], gt[j], preferred_element_type=f32)
        scores = jnp.where(offset <= block * HALF - c * CHUNK, scores, HIDDEN)
        new_top = jnp.maximum(top, jnp.max(scores, axis=0, keepdims=True))
        e = jnp.exp2(scores - new_top)
        keep = jnp.exp2(top - new_top)
        probs[i] = e
        dprobs[i] = dp
        tops[i] = new_top
        new = (
            new_top,
            total * keep + jnp.sum(e, axis=0, keepdims=True),
            weighted * keep + jnp.sum(e * dp, axis=0, keepdims=True),
        )
        if is_early is not False:
            state[True] = tuple(pick(is_early, a, b) for a, b in zip(new, state[True]))
        if is_early is not True:
            state[False] = tuple(pick(is_early, b, a) for a, b in zip(new, state[False]))

    stats = {}
    for flag, (top, total, weighted) in state.items():
        inverse = 1.0 / total
        stats[flag] = (top, inverse, weighted * inverse)

    loads[2].wait()
    loads[3].wait()

    def change(i):
        is_early, j, c, block = places[i]
        top, inverse, delta = (pick(is_early, a, b) for a, b in zip(stats[True], stats[False]))
        p = probs[i] * (jnp.exp2(tops[i] - top) * inverse)
        d = (p * (dprobs[i] - delta)).astype(bf16)
        ds[i] = d
        moves.append(pltpu.make_async_copy(ds.at[i], ds_hbm.at[i], ds_sems.at[i]))
        moves[-1].start()
        values = jnp.dot(p.astype(bf16), ga[j], preferred_element_type=f32)
        latent = jnp.dot(d, qa[j, :, :D_LAT], preferred_element_type=f32) + values
        return latent, jnp.dot(d, qa[j, :, D_LAT:], preferred_element_type=f32)

    def put(c, parts):
        for i in range(PER_CHUNK):
            at = place[c * PER_CHUNK + i]
            chip = at // 4
            j = at & 1
            ours = ((at // 2) & 1) == core
            src = slice(i * HALF, (i + 1) * HALF)
            latent = parts[0][src].astype(bf16)
            rope = pack_rope(parts[1][src]).astype(bf16)
            rows = pl.ds(pl.multiple_of(j * HALF, HALF), HALF)
            cols = pl.ds(pl.multiple_of(j * 256, 256), 256)
            for ref, to in ((dmine_ref, jnp.where(ours, chip, N_CHIP)), (dother_ref, jnp.where(ours, N_CHIP, chip))):
                ref[to, rows, :] = latent
                ref[to, ROWS:, cols] = rope

    put(0, [a + b for a, b in zip(change(0), change(1))])
    put(4, change(5))
    for k in range(1, 4):
        is_early = places[5 + k][0]
        turn = change(5 + k)
        put(k, [a + jnp.where(is_early, b, 0.0) for a, b in zip(change(1 + k), turn)])
        put(N_CHUNK - k, [jnp.where(is_early, 0.0, b) for b in turn])
    for move in moves:
        move.wait()


def queries_kernel(bm_ref, rank_ref, keys_hbm, ds_hbm, uk_hbm, cos_ref, sin_ref, gqn_ref, gqr_ref,
                   keys, ds, uk_ref, total, sems, ds_sems):
    first = pltpu.make_async_copy(keys_hbm, keys, sems.at[0])
    weights = pltpu.make_async_copy(uk_hbm, uk_ref, sems.at[1])
    moves = [pltpu.make_async_copy(ds_hbm.at[i], ds.at[i], ds_sems.at[i]) for i in range(STEPS)]
    first.start()
    for move in moves:
        move.start()
    weights.start()
    total[...] = jnp.zeros_like(total)
    first.wait()
    for i, (_, j, c, _) in enumerate(step_places(bm_ref, rank_ref[0])):
        moves[i].wait()
        total[j] += lax.dot_general(
            ds[i], keys[chunk_rows(c), :], (((0,), (0,)), ((), ())), preferred_element_type=f32
        )
    weights.wait()
    for pair in range(HEADS // 2):
        ropes = []
        for h in (2 * pair, 2 * pair + 1):
            rows = slice(h * HALF, (h + 1) * HALF)
            both = jnp.concatenate([total[0, rows, :], total[1, rows, :]], axis=0) * SCALE
            cols = slice(h * D_NOPE, (h + 1) * D_NOPE)
            gqn_ref[:, cols] = jnp.dot(
                both[:, :D_LAT].astype(bf16), uk_ref[:, cols], preferred_element_type=f32
            ).astype(bf16)
            ropes.append(both[:, D_LAT:])
        g = jnp.where(lanes_of(ropes[0].shape) < D_ROPE, ropes[0], pltpu.roll(ropes[1], D_ROPE, 1))
        g = g * cos_ref[...] - swap_halves(g) * sin_ref[...]
        gqr_ref[:, pair * 128:(pair + 1) * 128] = g.astype(bf16)


def after_kernel(first_ref, second_ref, out_ref):
    pass


def chips_kernel(parts_ref, cos_ref, sin_ref, later_ref, out_ref):
    total = parts_ref[0].astype(f32)
    for i in range(1, N_CHIP):
        total = total + parts_ref[i].astype(f32)
    out_ref[:, :D_LAT] = total[:ROWS].astype(bf16)
    g = jnp.concatenate([unpack_rope(total[ROWS:, j * 256:(j + 1) * 256]) for j in range(2)], axis=0)
    g = g * cos_ref[...] - swap_halves(g) * sin_ref[...]
    out_ref[:, D_LAT:] = g[:, :D_ROPE].astype(bf16)


def heads_kernel(parts_ref, out_ref):
    total = parts_ref[0].astype(f32)
    for i in range(1, N_HEAD):
        total = total + parts_ref[i].astype(f32)
    total = total.astype(bf16)
    for i in range(N_HEAD):
        out_ref[i] = total


def whole(count):
    return [pl.BlockSpec(memory_space=pltpu.VMEM)] * count


def in_hbm(x):
    return pltpu.with_memory_space_constraint(x, pltpu.HBM)


def params(mib):
    return pltpu.CompilerParams(vmem_limit_bytes=mib * 1024 * 1024)


ANY = pl.BlockSpec(memory_space=pl.ANY)
HBM = pl.BlockSpec(memory_space=pltpu.HBM)
ALL_MIB = 60

SMEM = pl.BlockSpec(memory_space=pltpu.SMEM)


def attend_call(*operands):
    shape = jax.ShapeDtypeStruct
    dma = pltpu.SemaphoreType.DMA
    piece = shape((N_CHIP + 1, PACKED, D_LAT), bf16)
    return pl.pallas_call(
        attend_kernel,
        in_specs=[SMEM, SMEM] + whole(2) + [HBM] * 4,
        out_specs=(*whole(2), HBM, HBM),
        out_shape=(piece, piece, pltpu.HBM((STEPS, CHUNK, LANES), bf16), pltpu.HBM((TOTAL, D_PAD), bf16)),
        scratch_shapes=[
            pltpu.VMEM((2, D_PAD, LANES), bf16),
            pltpu.VMEM((2, LANES, D_PAD), bf16),
            pltpu.VMEM((2, D_LAT, LANES), bf16),
            pltpu.VMEM((2, LANES, D_LAT), bf16),
            pltpu.VMEM((STEPS, CHUNK, LANES), f32),
            pltpu.VMEM((STEPS, CHUNK, LANES), f32),
            pltpu.VMEM((STEPS, 1, LANES), f32),
            pltpu.VMEM((STEPS, CHUNK, LANES), bf16),
            pltpu.VMEM((TOTAL, D_PAD), bf16),
            pltpu.SMEM((N_BLOCK,), jnp.int32),
            dma((4,)),
            dma,
            dma((STEPS,)),
        ],
        compiler_params=params(36),
        name="attend",
    )(*operands)


def on_device(q_nope, q_rope, compressed, w_uk, w_uv, grad_out, positions, block_map):
    rank = lax.axis_index("ctx").astype(jnp.int32).reshape(1)
    blocks = block_map.T
    shape = jax.ShapeDtypeStruct
    table = shape((ROWS, 128), f32)
    shared, cosine, sine = pl.pallas_call(
        share_kernel,
        in_specs=[SMEM] + whole(3),
        out_specs=tuple(whole(3)),
        out_shape=(shape((N_CHIP, PACKED, D_LAT), bf16), table, table),
        scratch_shapes=[pltpu.VMEM((PACKED, D_LAT), bf16)],
        compiler_params=params(ALL_MIB),
        name="share",
    )(rank, positions.reshape(1, ROWS), jnp.asarray(frequencies()), compressed.T)
    mine = lax.all_to_all(shared, ("ctx", "head"), 0, 0, axis_index_groups=GROUPS)
    pair_cols = lambda width: pl.BlockSpec((ROWS, width), lambda p: (0, p))
    fixed = pl.BlockSpec((ROWS, 128), lambda p: (0, 0))
    weight = pl.BlockSpec((D_LAT, 256), lambda p: (0, p))
    wide = lambda rows: pl.BlockSpec((2, rows, 128), lambda p: (0, 0, p))
    tall = lambda cols: pl.BlockSpec((2, 128, cols), lambda p: (0, p, 0))
    qt, qa, gt, ga = pl.pallas_call(
        absorb_kernel,
        grid=(HEADS // 2,),
        in_specs=[pair_cols(256), pair_cols(128), pair_cols(256), weight, weight, fixed, fixed],
        out_specs=(wide(D_PAD), tall(D_PAD), wide(D_LAT), tall(D_LAT)),
        out_shape=(
            shape((2, D_PAD, LANES), bf16),
            shape((2, LANES, D_PAD), bf16),
            shape((2, D_LAT, LANES), bf16),
            shape((2, LANES, D_LAT), bf16),
        ),
        scratch_shapes=[pltpu.VMEM((2, 128, D_LAT + D_PAD), f32)],
        compiler_params=params(ALL_MIB),
        cost_estimate=pl.CostEstimate(flops=300_000_000, bytes_accessed=8_000_000, transcendentals=0),
        name="absorb",
    )(q_nope, q_rope, grad_out, w_uk, w_uv, cosine, sine)

    mine = pl.pallas_call(
        after_kernel,
        in_specs=[ANY, ANY],
        out_specs=ANY,
        out_shape=shape(mine.shape, bf16),
        input_output_aliases={0: 0},
        compiler_params=params(8),
        name="after",
    )(mine, in_hbm(qt))
    other = lax.ppermute(mine, "ctx", SWAP)
    dmine, dother, ds, keys = attend_call(blocks, rank, mine, other, *map(in_hbm, (qt, qa, gt, ga)))

    theirs = lax.ppermute(dother, "ctx", SWAP)
    summed = (dmine[:N_CHIP].astype(f32) + theirs[:N_CHIP].astype(f32)).astype(bf16)
    parts = lax.all_to_all(summed, ("ctx", "head"), 0, 0, axis_index_groups=GROUPS)

    grad_q_nope, grad_q_rope = pl.pallas_call(
        queries_kernel,
        in_specs=[SMEM, SMEM, HBM, HBM, HBM] + whole(2),
        out_specs=tuple(whole(2)),
        out_shape=(shape((ROWS, HEADS * D_NOPE), bf16), shape((ROWS, HEADS * D_ROPE), bf16)),
        scratch_shapes=[
            pltpu.VMEM((TOTAL, D_PAD), bf16),
            pltpu.VMEM((STEPS, CHUNK, LANES), bf16),
            pltpu.VMEM((D_LAT, HEADS * D_NOPE), bf16),
            pltpu.VMEM((2, LANES, D_PAD), f32),
            pltpu.SemaphoreType.DMA((2,)),
            pltpu.SemaphoreType.DMA((STEPS,)),
        ],
        compiler_params=params(ALL_MIB),
        cost_estimate=pl.CostEstimate(flops=4_000_000_000, bytes_accessed=9_000_000, transcendentals=0),
        name="queries",
    )(blocks, rank, in_hbm(keys), in_hbm(ds), in_hbm(w_uk), cosine, sine)

    owned = pl.pallas_call(
        chips_kernel,
        in_specs=whole(3) + [HBM],
        out_specs=whole(1)[0],
        out_shape=shape((ROWS, D_ALL), bf16),
        compiler_params=params(16),
        name="chips",
    )(parts, cosine, sine, in_hbm(grad_q_rope))
    slabs = lax.all_to_all(owned.reshape(N_HEAD, ROWS // N_HEAD, D_ALL), "head", 0, 0)
    slabs = pl.pallas_call(
        heads_kernel,
        in_specs=whole(1),
        out_specs=whole(1)[0],
        out_shape=shape((N_HEAD, ROWS // N_HEAD, D_ALL), bf16),
        compiler_params=params(16),
        name="heads",
    )(slabs)
    grad_compressed = lax.all_to_all(slabs, "head", 0, 0).reshape(ROWS, D_ALL)
    return grad_q_nope, grad_q_rope, grad_compressed


def solution(mesh):
    in_specs = (
        P("ctx", "head"),
        P("ctx", "head"),
        P("ctx", None),
        P(None, "head"),
        P(None, "head"),
        P("ctx", "head"),
        P("ctx"),
        P(),
    )
    out_specs = (P("ctx", "head"), P("ctx", "head"), P("ctx", None))
    return jax.shard_map(
        on_device, mesh=mesh, in_specs=in_specs, out_specs=out_specs, check_vma=False
    )
```

time: 139 us -> 97.4 us (0.70); the launches traced: 137 us -> 97 us
  blocking collectives: 63.5 us -> 32.1 us
  local copies, waits for them, and re-layouts: 27.6 us -> 0.8 us
  waiting for transfers between devices: 2.82 us -> 23.6 us
  Pallas kernels: 36.4 us -> 28.1 us
  starting transfers between devices: 4.09 us -> 10.3 us
    all_to_all x2 -> x1, blocking collectives: 45.2 us -> 12 us  [on_device(): grad_compressed = lax.all_to_all(slabs, 'head', 0, 0).reshape(ROWS, D_ALL)]
    all_to_all x1 -> x2, waiting for transfers between devices: 0.01 us -> 17.9 us  [the longest x1 10.2 us: on_device(): lax.all_to_all(shared, ('ctx', 'head'), 0, 0, axis_index_groups=GROUPS)]
    unnamed x45 -> x7, local copies, waits for them, and re-layouts: 13.9 us -> 0.8 us
    pallas_call x4 -> x5, Pallas kernels: 31.9 us -> 22.6 us  [the longest x1 11.5 us: attend_call(): pl.pallas_call(attend_kernel, in_specs=[SMEM, SMEM] + whole(2) + [HBM] *...]
    all_to_all x1 -> x2, starting transfers between devices: 3.52 us -> 10.1 us  [the longest x1 5.93 us: on_device(): lax.all_to_all(shared, ('ctx', 'head'), 0, 0, axis_index_groups=GROUPS)]
    ppermute x2 -> x0, local copies, waits for them, and re-layouts: 4.1 us -> none  [the longest x1 2.42 us: on_device(): other = lax.ppermute(mine, 'ctx', SWAP)]
    pallas_call x2 -> x0, local copies, waits for them, and re-layouts: 3.94 us -> none  [the longest x1 2.46 us: on_device(): pl.pallas_call(share_kernel, in_specs=whole(3), out_specs=tuple(whole(3))...]
    all_to_all x2 -> x0, local copies, waits for them, and re-layouts: 3.92 us -> none  [the longest x1 2.44 us: on_device(): mine = lax.all_to_all(shared, 'ctx', 0, 0, axis_index_groups=CORES)]
  transfers between devices with their start and end apart: 3 -> 4, of which waited for: 1 -> 4; matrix products, arithmetic and copies ran while one was open for 2% -> 0% of each run, Pallas kernels for 9% -> 14%
where the time goes in v2:
time: 97.4 us; the launch traced here: 97 us
  blocking collectives  32.1 us (33%)
  Pallas kernels  28.1 us (29%)
  waiting for transfers between devices  23.6 us (24%)
  starting transfers between devices  10.3 us (11%)
  other arithmetic  1.42 us (1%)
    all_to_all x1, blocking collectives, on_device(): lax.all_to_all(owned.reshape(N_HEAD, ROWS // N_HEAD, D_ALL), 'head', 0, 0)  20.1 us
    all_to_all x1, blocking collectives, on_device(): grad_compressed = lax.all_to_all(slabs, 'head', 0, 0).reshape(ROWS, D_ALL)  12 us
    pallas_call x1, Pallas kernels, attend_call(): pl.pallas_call(attend_kernel, in_specs=[SMEM, SMEM] + whole(2) + [HBM] *...  11.5 us
    all_to_all x1, waiting for transfers between devices, on_device(): lax.all_to_all(shared, ('ctx', 'head'), 0, 0, axis_index_groups=GROUPS)  10.2 us
    pallas_call x1, Pallas kernels, on_device(): pl.pallas_call(queries_kernel, in_specs=[SMEM, SMEM, HBM, HBM, HBM] + who...  8.38 us
    all_to_all x1, waiting for transfers between devices, on_device(): lax.all_to_all(summed, ('ctx', 'head'), 0, 0, axis_index_groups=GROUPS)  7.71 us
    all_to_all x1, starting transfers between devices, on_device(): lax.all_to_all(shared, ('ctx', 'head'), 0, 0, axis_index_groups=GROUPS)  5.93 us
    pallas_call x1, Pallas kernels, on_device(): pl.pallas_call(absorb_kernel, grid=(HEADS // 2,), in_specs=[pair_cols(256...  5.48 us
  transfers between devices with their start and end apart: 4, of which 4 were waited for; matrix products, arithmetic and copies ran while one was open for 0% of the time, Pallas kernels for 14%

profile of v2, /device:TPU:4, one launch (start us, length us, event | category | flops | bytes accessed | tf_op | source)
XLA Modules:
  0.0 97.0 jit_solution(8151713252452693831)
XLA Ops:
  0.6 2.4 %share.1 = (bf16[8,144,512]{2,1,0:T(8,128)(2,1)}, f32[128,128]{1,0:T(8,128)}, f32[128,128]{1,0:T(8,128)}) custom-call(s32[1]{0:T(128)} %bitcast.1.rank_ref, s32[1,128]{1,0:T(1,128)} %bitcast.11, f32[1,128]{1,0:T(1,128)} %constant.7.clone.inv_ref, bf16[576,128]{1,0:T(8,128)(2,1)} %bitcast.10), custom_call_target="tpu_custom_call" | custom-call | tf_op jit(solution)/shard_map/share/pallas_call | solution.py:410
  3.0 5.9 %all-to-all-start = ((bf16[8,144,512]{2,1,0:T(8,128)(2,1)}), bf16[8,144,512]{2,1,0:T(8,128)(2,1)S(1)}, u32[]{:S(2)}, u32[]{:S(2)}) async-start(bf16[8,144,512]{2,1,0:T(8,128)(2,1)} %get-tuple-element.16), calls=%async_computation | async-start | bytes 2359296 | tf_op jit(solution)/shard_map/all_to_all | solution.py:419
  8.9 5.5 %absorb.1 = (bf16[2,640,512]{2,1,0:T(8,128)(2,1)}, bf16[2,512,640]{2,1,0:T(8,128)(2,1)}, bf16[2,512,512]{2,1,0:T(8,128)(2,1)}, bf16[2,512,512]{2,1,0:T(8,128)(2,1)}) custom-call(bf16[128,1024]{1,0:T(8,128)(2,1)} %qn_ref.1, bf16[128,512]{1,0:T(8,128)(2,1)} %qr_ref.1, bf16[128,1024]{1,0:T(8,128)(2,1)} %go_ref.1, bf16[512,1024]{1,0:T(8,128)(2,1)} %uk_hbm.1, ...), custom_call_target="tpu_custom_call" | custom-call | flops 300000000 | bytes 8000000 | tf_op jit(solution)/shard_map/absorb/pallas_call | solution.py:425
  14.4 10.2 %all-to-all-done.first_ref = bf16[8,144,512]{2,1,0:T(8,128)(2,1)S(1)} async-done(((bf16[8,144,512]{2,1,0:T(8,128)(2,1)}), bf16[8,144,512]{2,1,0:T(8,128)(2,1)S(1)}, u32[]{:S(2)}, u32[]{:S(2)}) %all-to-all-start) | async-done | bytes 1179680 | tf_op jit(solution)/shard_map/all_to_all | solution.py:419
  24.6 0.0 copy-start.2
  24.6 0.0 collective-permute-start
  24.6 2.8 %collective-permute-done.other_ref = bf16[8,144,512]{2,1,0:T(8,128)(2,1)S(1)} collective-permute-done((bf16[8,144,512]{2,1,0:T(8,128)(2,1)S(1)}, bf16[8,144,512]{2,1,0:T(8,128)(2,1)S(1)}, u32[]{:S(2)}, u32[]{:S(2)}) %collective-permute-start) | collective-permute-done | bytes 1179680 | tf_op jit(solution)/shard_map/ppermute | solution.py:451
  27.4 0.0 copy-done.2
  27.4 11.5 %attend.1 = (bf16[9,144,512]{2,1,0:T(8,128)(2,1)S(1)}, bf16[9,144,512]{2,1,0:T(8,128)(2,1)S(1)}, bf16[9,256,512]{2,1,0:T(8,128)(2,1)}, bf16[2048,640]{1,0:T(8,128)(2,1)}) custom-call(s32[2,16]{1,0:T(2,128)S(1)} %bitcast.8, s32[1]{0:T(128)} %bitcast.1.rank_ref, bf16[8,144,512]{2,1,0:T(8,128)(2,1)S(1)} %after.1.mine_ref, ...), custom_call_target="tpu_custom_call" | custom-call | tf_op jit(solution)/shard_map/attend/pallas_call | solution.py:380
  39.0 0.2 collective-permute-start.1
  39.2 2.9 %collective-permute-done.1 = bf16[9,144,512]{2,1,0:T(8,128)(2,1)S(1)} collective-permute-done((bf16[9,144,512]{2,1,0:T(8,128)(2,1)S(1)}, bf16[9,144,512]{2,1,0:T(8,128)(2,1)S(1)}, u32[]{:S(2)}, u32[]{:S(2)}) %collective-permute-start.1) | collective-permute-done | bytes 1327136 | tf_op jit(solution)/shard_map/ppermute | solution.py:454
  42.1 1.4 %add_convert_fusion = bf16[8,144,512]{2,1,0:T(8,128)(2,1)} fusion(bf16[9,144,512]{2,1,0:T(8,128)(2,1)S(1)} %collective-permute-done.1, bf16[9,144,512]{2,1,0:T(8,128)(2,1)S(1)} %get-tuple-element.27), kind=kLoop, calls=%fused_computation | loop fusion | flops 2359296 | bytes 3538944 | tf_op jit(solution)/shard_map/convert_element_type | solution.py:455
  43.6 4.2 %all-to-all-start.1 = ((bf16[8,144,512]{2,1,0:T(8,128)(2,1)}), bf16[8,144,512]{2,1,0:T(8,128)(2,1)S(1)}, u32[]{:S(2)}, u32[]{:S(2)}) async-start(bf16[8,144,512]{2,1,0:T(8,128)(2,1)} %add_convert_fusion), calls=%async_computation.1 | async-start | bytes 2359296 | tf_op jit(solution)/shard_map/all_to_all | solution.py:456
  47.8 0.0 copy-start
  47.8 0.0 copy-start.1
  47.8 8.4 %queries.1 = (bf16[128,1024]{1,0:T(8,128)(2,1)}, bf16[128,512]{1,0:T(8,128)(2,1)}) custom-call(s32[2,16]{1,0:T(2,128)} %bitcast.7, s32[1]{0:T(128)} %bitcast.1.rank_ref, bf16[2048,640]{1,0:T(8,128)(2,1)} %get-tuple-element.23.keys_hbm, bf16[9,256,512]{2,1,0:T(8,128)(2,1)} %get-tuple-element.24.ds_hbm, bf16[512,1024]{1,0:T(8,128)(2,1)} %uk_hbm.1, ...), custom_call_target="tpu_custom_call" | custom-call | flops 4000000000 | bytes 9000000 | tf_op jit(solution)/shard_map/queries/pallas_call | solution.py:458
  56.2 7.7 %all-to-all-done.1.parts_ref = bf16[8,144,512]{2,1,0:T(8,128)(2,1)S(1)} async-done(((bf16[8,144,512]{2,1,0:T(8,128)(2,1)}), bf16[8,144,512]{2,1,0:T(8,128)(2,1)S(1)}, u32[]{:S(2)}, u32[]{:S(2)}) %all-to-all-start.1) | async-done | bytes 1179680 | tf_op jit(solution)/shard_map/all_to_all | solution.py:456
  63.9 0.0 copy-done
  63.9 0.0 copy-done.1
  63.9 0.3 chips.1
  64.1 20.1 %all_to_all.20.parts_ref = bf16[16,8,576]{2,1,0:T(8,128)(2,1)S(1)} all-to-all(bf16[16,8,576]{2,1,0:T(8,128)(2,1)S(1)} %bitcast.6), channel_id=1, replica_groups=mesh['ctx'=16,'head'=16] {'head'}, dimensions={0} | all-to-all | bytes 294912 | tf_op jit(solution)/shard_map/all_to_all | solution.py:484
  84.3 12.0 %all_to_all.21 = bf16[16,8,576]{2,1,0:T(8,128)(2,1)S(1)} all-to-all(bf16[16,8,576]{2,1,0:T(8,128)(2,1)S(1)} %heads.1), channel_id=1, replica_groups=mesh['ctx'=16,'head'=16] {'head'}, dimensions={0} | all-to-all | bytes 294912 | tf_op jit(solution)/shard_map/all_to_all | solution.py:493
  96.2 0.8 copy.13
  (2 shorter events, 0.0 us)
Async XLA Ops:
  3.0 21.6 %all-to-all-start = ((bf16[8,144,512]{2,1,0:T(8,128)(2,1)}), bf16[8,144,512]{2,1,0:T(8,128)(2,1)S(1)}, u32[]{:S(2)}, u32[]{:S(2)}) async-start(bf16[8,144,512]{2,1,0:T(8,128)(2,1)} %get-tuple-element.16), calls=%async_computation | async-start | bytes 2359296 | tf_op jit(solution)/shard_map/all_to_all | solution.py:419
  24.6 2.9 %copy-start.2 = (s32[16,2]{0,1:T(2,128)S(1)}, s32[16,2]{0,1:T(2,128)}, u32[]{:S(2)}) copy-start(s32[16,2]{0,1:T(2,128)} %param.16) | copy-start | bytes 388
  24.6 2.8 %collective-permute-start = (bf16[8,144,512]{2,1,0:T(8,128)(2,1)S(1)}, bf16[8,144,512]{2,1,0:T(8,128)(2,1)S(1)}, u32[]{:S(2)}, u32[]{:S(2)}) collective-permute-start(bf16[8,144,512]{2,1,0:T(8,128)(2,1)S(1)} %after.1.mine_ref), channel_id=1, source_target_pairs={{0,16},{16,0},{32,48},{48,32},{64,80},{80,64},{96,112},{112,96},{1... | collective-permute-start | bytes 3538952 | tf_op jit(solution)/shard_map/ppermute | solution.py:451
  39.0 3.1 %collective-permute-start.1 = (bf16[9,144,512]{2,1,0:T(8,128)(2,1)S(1)}, bf16[9,144,512]{2,1,0:T(8,128)(2,1)S(1)}, u32[]{:S(2)}, u32[]{:S(2)}) collective-permute-start(bf16[9,144,512]{2,1,0:T(8,128)(2,1)S(1)} %get-tuple-element.28), channel_id=1, source_target_pairs={{0,16},{16,0},{32,48},{48,32},{64,80},{80,64},{96,112},{112,96},{1... | collective-permute-start | bytes 3981320 | tf_op jit(solution)/shard_map/ppermute | solution.py:454
  43.6 20.3 %all-to-all-start.1 = ((bf16[8,144,512]{2,1,0:T(8,128)(2,1)}), bf16[8,144,512]{2,1,0:T(8,128)(2,1)S(1)}, u32[]{:S(2)}, u32[]{:S(2)}) async-start(bf16[8,144,512]{2,1,0:T(8,128)(2,1)} %add_convert_fusion), calls=%async_computation.1 | async-start | bytes 2359296 | tf_op jit(solution)/shard_map/all_to_all | solution.py:456
  47.8 16.1 %copy-start = (f32[128,128]{1,0:T(8,128)S(1)}, f32[128,128]{1,0:T(8,128)}, u32[]{:S(2)}) copy-start(f32[128,128]{1,0:T(8,128)} %get-tuple-element.17.cos_ref) | copy-start | bytes 196612
  47.8 16.1 %copy-start.1 = (f32[128,128]{1,0:T(8,128)S(1)}, f32[128,128]{1,0:T(8,128)}, u32[]{:S(2)}) copy-start(f32[128,128]{1,0:T(8,128)} %get-tuple-element.18.sin_ref) | copy-start | bytes 196612

commit v3 on v2

--- a/solution.py
+++ b/solution.py
@@ -41,6 +41,8 @@
 ]
 SWAP = [(c, c ^ 1) for c in range(N_CTX)]
 
+AGAINST = (((1,), (1,)), ((), ()))
+
 bf16 = jnp.bfloat16
 f32 = jnp.float32
 
@@ -142,32 +144,22 @@
 
 
 def absorb_kernel(qn_ref, qr_ref, go_ref, uk_ref, uv_ref, cos_ref, sin_ref,
-                  qt_ref, qa_ref, gt_ref, ga_ref, tall):
-    contract = (((1,), (1,)), ((), ()))
+                  both_ref):
     x = qr_ref[...].astype(f32)
     rotated = x * cos_ref[...] + swap_halves(x) * sin_ref[...]
     turned = pltpu.roll(rotated, HALF, 1)
     for h in range(2):
         cols = slice(h * D_NOPE, (h + 1) * D_NOPE)
-        q = lax.dot_general(qn_ref[:, cols], uk_ref[:, cols], contract, preferred_element_type=f32)
-        g = lax.dot_general(go_ref[:, cols], uv_ref[:, cols], contract, preferred_element_type=f32)
+        q = lax.dot_general(qn_ref[:, cols], uk_ref[:, cols], AGAINST, preferred_element_type=f32)
+        g = lax.dot_general(go_ref[:, cols], uv_ref[:, cols], AGAINST, preferred_element_type=f32)
         rope = jnp.where(lanes_of(x.shape) < D_ROPE, rotated if h == 0 else turned, 0.0)
+        dst = slice(h * HALF, (h + 1) * HALF)
         for j in range(2):
             src = slice(j * HALF, (j + 1) * HALF)
-            dst = slice(h * HALF, (h + 1) * HALF)
-            tall[j, dst, :D_LAT] = q[src]
-            tall[j, dst, D_LAT:D_PAD] = rope[src]
-            tall[j, dst, D_PAD:] = g[src]
-    for j in range(2):
-        both = tall[j, :, :D_PAD]
-        qa_ref[j] = (both * SCALE).astype(bf16)
-        ga_ref[j] = tall[j, :, D_PAD:].astype(bf16)
-        for k in range(D_PAD // 128):
-            piece = slice(k * 128, (k + 1) * 128)
-            qt_ref[j, piece, :] = (both[:, piece] * (SCALE * LOG2E)).T.astype(bf16)
-        for k in range(D_LAT // 128):
-            piece = slice(k * 128, (k + 1) * 128)
-            gt_ref[j, piece, :] = tall[j, :, D_PAD + k * 128:D_PAD + (k + 1) * 128].T.astype(bf16)
+            both_ref[j, 0, dst, :D_LAT] = (q[src] * SCALE).astype(bf16)
+            both_ref[j, 0, dst, D_LAT:] = (rope[src] * SCALE).astype(bf16)
+            both_ref[j, 1, dst, :D_LAT] = g[src].astype(bf16)
+            both_ref[j, 1, dst, D_LAT:] = jnp.zeros((HALF, 128), bf16)
 
 
 def step_places(bm_ref, rank):
@@ -175,16 +167,19 @@
     early = jnp.where(first < second, 0, 1)
     low, high = jnp.minimum(first, second), jnp.maximum(first, second)
     count = (low + PER_CHUNK) // PER_CHUNK
-    places = [(True, early, 0, low)] + [(False, 1 - early, c, high) for c in range(5)]
+    places = [(True, early, 0, 1, low)]
+    places += [(False, 1 - early, 0, 2, high), (False, 1 - early, 2, 2, high), (False, 1 - early, 4, 1, high)]
     for k in range(1, 4):
         is_early = k < count
         places.append((
             is_early,
             jnp.where(is_early, early, 1 - early),
             jnp.where(is_early, k, N_CHUNK - k),
+            1,
             jnp.where(is_early, low, high),
         ))
-    return places
+    starts = [0, 1, 3, 5, 6, 7, 8]
+    return [(slice(at * CHUNK, (at + place[3]) * CHUNK), *place) for at, place in zip(starts, places)]
 
 
 def pick(flag, first, second):
@@ -195,17 +190,13 @@
     return jnp.where(flag, first, second)
 
 
-def chunk_rows(c):
-    return pl.ds(c * CHUNK if isinstance(c, int) else pl.multiple_of(c * CHUNK, CHUNK), CHUNK)
-
-
-def attend_kernel(bm_ref, rank_ref, mine_ref, other_ref, qt_hbm, qa_hbm, gt_hbm, ga_hbm,
+def chunk_rows(c, n):
+    return pl.ds(c * CHUNK if isinstance(c, int) else pl.multiple_of(c * CHUNK, CHUNK), n * CHUNK)
+
+
+def attend_kernel(bm_ref, rank_ref, mine_ref, other_ref, both,
                   dmine_ref, dother_ref, ds_hbm, keys_hbm,
-                  qt, qa, gt, ga, probs, dprobs, tops, ds, keys, place, load_sems, key_sem, ds_sems):
-    sources = ((qt_hbm, qt), (gt_hbm, gt), (qa_hbm, qa), (ga_hbm, ga))
-    loads = [pltpu.make_async_copy(src, dst, load_sems.at[i]) for i, (src, dst) in enumerate(sources)]
-    for load in loads:
-        load.start()
+                  probs, dprobs, tops, ds, keys, dlat, drope, key_sem, ds_sems):
     rank = rank_ref[0]
     core = rank & 1
     places = step_places(bm_ref, rank)
@@ -214,7 +205,6 @@
             row = 2 * chip + (core ^ k)
             for j in range(2):
                 block = bm_ref[j, row]
-                place[block] = row * 2 + j
                 rows = pl.ds(pl.multiple_of(block * HALF, HALF), HALF)
                 keys[rows, :D_LAT] = ref[chip, j * HALF:(j + 1) * HALF, :]
                 packed = ref[chip, ROWS:, j * 256:(j + 1) * 256].astype(f32)
@@ -222,26 +212,24 @@
 
     moves = [pltpu.make_async_copy(keys, keys_hbm, key_sem)]
     moves[0].start()
-    loads[0].wait()
-    loads[1].wait()
 
     zero = jnp.zeros((1, LANES), f32)
     start = (jnp.full((1, LANES), HIDDEN, f32), zero, zero)
     state = {True: start, False: start}
-    offset = lax.broadcasted_iota(jnp.int32, (CHUNK, LANES), 0) - (
-        lax.broadcasted_iota(jnp.int32, (CHUNK, LANES), 1) & (HALF - 1)
+    offset = lax.broadcasted_iota(jnp.int32, (2 * CHUNK, LANES), 0) - (
+        lax.broadcasted_iota(jnp.int32, (2 * CHUNK, LANES), 1) & (HALF - 1)
     )
-    for i, (is_early, j, c, block) in enumerate(places):
-        rows = chunk_rows(c)
+    for i, (at, is_early, j, c, n, block) in enumerate(places):
+        rows = chunk_rows(c, n)
         top, total, weighted = (pick(is_early, a, b) for a, b in zip(state[True], state[False]))
-        scores = jnp.dot(keys[rows, :], qt[j], preferred_element_type=f32)
-        dp = jnp.dot(keys[rows, :D_LAT], gt[j], preferred_element_type=f32)
-        scores = jnp.where(offset <= block * HALF - c * CHUNK, scores, HIDDEN)
+        scores = lax.dot_general(keys[rows, :], both[j, :LANES, :], AGAINST, preferred_element_type=f32)
+        dp = lax.dot_general(keys[rows, :D_LAT], both[j, LANES:, :D_LAT], AGAINST, preferred_element_type=f32)
+        scores = jnp.where(offset[:n * CHUNK] <= block * HALF - c * CHUNK, scores * LOG2E, HIDDEN)
         new_top = jnp.maximum(top, jnp.max(scores, axis=0, keepdims=True))
         e = jnp.exp2(scores - new_top)
         keep = jnp.exp2(top - new_top)
-        probs[i] = e
-        dprobs[i] = dp
+        probs[at] = e
+        dprobs[at] = dp
         tops[i] = new_top
         new = (
             new_top,
@@ -258,43 +246,43 @@
         inverse = 1.0 / total
         stats[flag] = (top, inverse, weighted * inverse)
 
-    loads[2].wait()
-    loads[3].wait()
-
     def change(i):
-        is_early, j, c, block = places[i]
+        at, is_early, j, c, n, block = places[i]
         top, inverse, delta = (pick(is_early, a, b) for a, b in zip(stats[True], stats[False]))
-        p = probs[i] * (jnp.exp2(tops[i] - top) * inverse)
-        d = (p * (dprobs[i] - delta)).astype(bf16)
-        ds[i] = d
-        moves.append(pltpu.make_async_copy(ds.at[i], ds_hbm.at[i], ds_sems.at[i]))
+        p = probs[at] * (jnp.exp2(tops[i] - top) * inverse)
+        d = (p * (dprobs[at] - delta)).astype(bf16)
+        ds[at] = d
+        moves.append(pltpu.make_async_copy(ds.at[at], ds_hbm.at[at], ds_sems.at[i]))
         moves[-1].start()
-        values = jnp.dot(p.astype(bf16), ga[j], preferred_element_type=f32)
-        latent = jnp.dot(d, qa[j, :, :D_LAT], preferred_element_type=f32) + values
-        return latent, jnp.dot(d, qa[j, :, D_LAT:], preferred_element_type=f32)
+        pair = jnp.concatenate([d, p.astype(bf16)], axis=1)
+        latent = jnp.dot(pair, both[j, :, :D_LAT], preferred_element_type=f32)
+        rope = jnp.dot(d, both[j, :LANES, D_LAT:], preferred_element_type=f32)
+        return [(latent[k * CHUNK:(k + 1) * CHUNK], rope[k * CHUNK:(k + 1) * CHUNK]) for k in range(n)]
 
     def put(c, parts):
+        rows = slice(c * CHUNK, (c + 1) * CHUNK)
+        dlat[rows, :D_LAT] = parts[0].astype(bf16)
         for i in range(PER_CHUNK):
-            at = place[c * PER_CHUNK + i]
-            chip = at // 4
-            j = at & 1
-            ours = ((at // 2) & 1) == core
-            src = slice(i * HALF, (i + 1) * HALF)
-            latent = parts[0][src].astype(bf16)
-            rope = pack_rope(parts[1][src]).astype(bf16)
-            rows = pl.ds(pl.multiple_of(j * HALF, HALF), HALF)
-            cols = pl.ds(pl.multiple_of(j * 256, 256), 256)
-            for ref, to in ((dmine_ref, jnp.where(ours, chip, N_CHIP)), (dother_ref, jnp.where(ours, N_CHIP, chip))):
-                ref[to, rows, :] = latent
-                ref[to, ROWS:, cols] = rope
-
-    put(0, [a + b for a, b in zip(change(0), change(1))])
-    put(4, change(5))
+            part = parts[1][i * HALF:(i + 1) * HALF]
+            drope[(c * PER_CHUNK + i) * 16:(c * PER_CHUNK + i + 1) * 16, :] = pack_rope(part).astype(bf16)
+
+    early = change(0)
     for k in range(1, 4):
-        is_early = places[5 + k][0]
-        turn = change(5 + k)
-        put(k, [a + jnp.where(is_early, b, 0.0) for a, b in zip(change(1 + k), turn)])
-        put(N_CHUNK - k, [jnp.where(is_early, 0.0, b) for b in turn])
+        turn = change(3 + k)[0]
+        is_early = places[3 + k][1]
+        put(N_CHUNK - k, [jnp.where(is_early, 0.0, x) for x in turn])
+        early.append([jnp.where(is_early, x, 0.0) for x in turn])
+    late = change(1) + change(2) + change(3)
+    for c in range(4):
+        put(c, [x + y for x, y in zip(late[c], early[c])])
+    put(4, late[4])
+    for chip in range(N_CHIP):
+        for k, ref in enumerate((dmine_ref, dother_ref)):
+            row = 2 * chip + (core ^ k)
+            for j in range(2):
+                block = bm_ref[j, row]
+                ref[chip, j * HALF:(j + 1) * HALF, :] = dlat[pl.ds(pl.multiple_of(block * HALF, HALF), HALF), :]
+                ref[chip, ROWS:, j * 256:(j + 1) * 256] = drope[pl.ds(pl.multiple_of(block * 16, 16), 16), :]
     for move in moves:
         move.wait()
 
@@ -303,17 +291,18 @@
                    keys, ds, uk_ref, total, sems, ds_sems):
     first = pltpu.make_async_copy(keys_hbm, keys, sems.at[0])
     weights = pltpu.make_async_copy(uk_hbm, uk_ref, sems.at[1])
-    moves = [pltpu.make_async_copy(ds_hbm.at[i], ds.at[i], ds_sems.at[i]) for i in range(STEPS)]
+    places = step_places(bm_ref, rank_ref[0])
+    moves = [pltpu.make_async_copy(ds_hbm.at[p[0]], ds.at[p[0]], ds_sems.at[i]) for i, p in enumerate(places)]
     first.start()
     for move in moves:
         move.start()
     weights.start()
     total[...] = jnp.zeros_like(total)
     first.wait()
-    for i, (_, j, c, _) in enumerate(step_places(bm_ref, rank_ref[0])):
-        moves[i].wait()
+    for move, (at, _, j, c, n, _) in zip(moves, places):
+        move.wait()
         total[j] += lax.dot_general(
-            ds[i], keys[chunk_rows(c), :], (((0,), (0,)), ((), ())), preferred_element_type=f32
+            ds[at], keys[chunk_rows(c, n), :], (((0,), (0,)), ((), ())), preferred_element_type=f32
         )
     weights.wait()
     for pair in range(HEADS // 2):
@@ -376,24 +365,20 @@
 def attend_call(*operands):
     shape = jax.ShapeDtypeStruct
     dma = pltpu.SemaphoreType.DMA
-    piece = shape((N_CHIP + 1, PACKED, D_LAT), bf16)
+    piece = shape((N_CHIP, PACKED, D_LAT), bf16)
     return pl.pallas_call(
         attend_kernel,
-        in_specs=[SMEM, SMEM] + whole(2) + [HBM] * 4,
+        in_specs=[SMEM, SMEM] + whole(3),
         out_specs=(*whole(2), HBM, HBM),
-        out_shape=(piece, piece, pltpu.HBM((STEPS, CHUNK, LANES), bf16), pltpu.HBM((TOTAL, D_PAD), bf16)),
+        out_shape=(piece, piece, pltpu.HBM((STEPS * CHUNK, LANES), bf16), pltpu.HBM((TOTAL, D_PAD), bf16)),
         scratch_shapes=[
-            pltpu.VMEM((2, D_PAD, LANES), bf16),
-            pltpu.VMEM((2, LANES, D_PAD), bf16),
-            pltpu.VMEM((2, D_LAT, LANES), bf16),
-            pltpu.VMEM((2, LANES, D_LAT), bf16),
-            pltpu.VMEM((STEPS, CHUNK, LANES), f32),
-            pltpu.VMEM((STEPS, CHUNK, LANES), f32),
+            pltpu.VMEM((STEPS * CHUNK, LANES), f32),
+            pltpu.VMEM((STEPS * CHUNK, LANES), f32),
             pltpu.VMEM((STEPS, 1, LANES), f32),
-            pltpu.VMEM((STEPS, CHUNK, LANES), bf16),
+            pltpu.VMEM((STEPS * CHUNK, LANES), bf16),
             pltpu.VMEM((TOTAL, D_PAD), bf16),
-            pltpu.SMEM((N_BLOCK,), jnp.int32),
-            dma((4,)),
+            pltpu.VMEM((TOTAL, D_LAT), bf16),
+            pltpu.VMEM((N_BLOCK * 16, 256), bf16),
             dma,
             dma((STEPS,)),
         ],
@@ -420,20 +405,12 @@
     pair_cols = lambda width: pl.BlockSpec((ROWS, width), lambda p: (0, p))
     fixed = pl.BlockSpec((ROWS, 128), lambda p: (0, 0))
     weight = pl.BlockSpec((D_LAT, 256), lambda p: (0, p))
-    wide = lambda rows: pl.BlockSpec((2, rows, 128), lambda p: (0, 0, p))
-    tall = lambda cols: pl.BlockSpec((2, 128, cols), lambda p: (0, p, 0))
-    qt, qa, gt, ga = pl.pallas_call(
+    both = pl.pallas_call(
         absorb_kernel,
         grid=(HEADS // 2,),
         in_specs=[pair_cols(256), pair_cols(128), pair_cols(256), weight, weight, fixed, fixed],
-        out_specs=(wide(D_PAD), tall(D_PAD), wide(D_LAT), tall(D_LAT)),
-        out_shape=(
-            shape((2, D_PAD, LANES), bf16),
-            shape((2, LANES, D_PAD), bf16),
-            shape((2, D_LAT, LANES), bf16),
-            shape((2, LANES, D_LAT), bf16),
-        ),
-        scratch_shapes=[pltpu.VMEM((2, 128, D_LAT + D_PAD), f32)],
+        out_specs=pl.BlockSpec((2, 2, 128, D_PAD), lambda p: (0, 0, p, 0)),
+        out_shape=shape((2, 2, LANES, D_PAD), bf16),
         compiler_params=params(ALL_MIB),
         cost_estimate=pl.CostEstimate(flops=300_000_000, bytes_accessed=8_000_000, transcendentals=0),
         name="absorb",
@@ -447,12 +424,13 @@
         input_output_aliases={0: 0},
         compiler_params=params(8),
         name="after",
-    )(mine, in_hbm(qt))
+    )(mine, in_hbm(both))
+    both = both.reshape(2, 2 * LANES, D_PAD)
     other = lax.ppermute(mine, "ctx", SWAP)
-    dmine, dother, ds, keys = attend_call(blocks, rank, mine, other, *map(in_hbm, (qt, qa, gt, ga)))
+    dmine, dother, ds, keys = attend_call(blocks, rank, mine, other, both)
 
     theirs = lax.ppermute(dother, "ctx", SWAP)
-    summed = (dmine[:N_CHIP].astype(f32) + theirs[:N_CHIP].astype(f32)).astype(bf16)
+    summed = (dmine.astype(f32) + theirs.astype(f32)).astype(bf16)
     parts = lax.all_to_all(summed, ("ctx", "head"), 0, 0, axis_index_groups=GROUPS)
 
     grad_q_nope, grad_q_rope = pl.pallas_call(
@@ -462,7 +440,7 @@
         out_shape=(shape((ROWS, HEADS * D_NOPE), bf16), shape((ROWS, HEADS * D_ROPE), bf16)),
         scratch_shapes=[
             pltpu.VMEM((TOTAL, D_PAD), bf16),
-            pltpu.VMEM((STEPS, CHUNK, LANES), bf16),
+            pltpu.VMEM((STEPS * CHUNK, LANES), bf16),
             pltpu.VMEM((D_LAT, HEADS * D_NOPE), bf16),
             pltpu.VMEM((2, LANES, D_PAD), f32),
             pltpu.SemaphoreType.DMA((2,)),

time: 97.4 us -> 96.3 us (0.989)
  Pallas kernels: 28.1 us -> 26.2 us
  transfers between devices with their start and end apart: 4 -> 4, of which waited for: 4 -> 4; matrix products, arithmetic and copies ran while one was open for 0% -> 0% of each run, Pallas kernels for 14% -> 13%
where the time goes in v3:
time: 96.3 us; the launch traced here: 95.9 us
  blocking collectives  32.1 us (33%)
  Pallas kernels  26.2 us (27%)
  waiting for transfers between devices  24.4 us (25%)
  starting transfers between devices  10.4 us (11%)
  other arithmetic  1.38 us (1%)
    all_to_all x1, blocking collectives, on_device(): lax.all_to_all(owned.reshape(N_HEAD, ROWS // N_HEAD, D_ALL), 'head', 0, 0)  20.1 us
    all_to_all x1, blocking collectives, on_device(): grad_compressed = lax.all_to_all(slabs, 'head', 0, 0).reshape(ROWS, D_ALL)  12 us
    all_to_all x1, waiting for transfers between devices, on_device(): lax.all_to_all(shared, ('ctx', 'head'), 0, 0, axis_index_groups=GROUPS)  11 us
    pallas_call x1, Pallas kernels, attend_call(): pl.pallas_call(attend_kernel, in_specs=[SMEM, SMEM] + whole(3), out_specs...  10.7 us
    pallas_call x1, Pallas kernels, on_device(): pl.pallas_call(queries_kernel, in_specs=[SMEM, SMEM, HBM, HBM, HBM] + who...  8.24 us
    all_to_all x1, waiting for transfers between devices, on_device(): lax.all_to_all(summed, ('ctx', 'head'), 0, 0, axis_index_groups=GROUPS)  7.84 us
    all_to_all x1, starting transfers between devices, on_device(): lax.all_to_all(shared, ('ctx', 'head'), 0, 0, axis_index_groups=GROUPS)  5.93 us
    pallas_call x1, Pallas kernels, on_device(): pl.pallas_call(absorb_kernel, grid=(HEADS // 2,), in_specs=[pair_cols(256...  4.66 us
  transfers between devices with their start and end apart: 4, of which 4 were waited for; matrix products, arithmetic and copies ran while one was open for 0% of the time, Pallas kernels for 13%

profile of v3, /device:TPU:4, one launch (start us, length us, event | category | flops | bytes accessed | tf_op | source)
XLA Modules:
  0.0 95.9 jit_solution(1890088326548659253)
XLA Ops:
  0.6 2.4 %share.1 = (bf16[8,144,512]{2,1,0:T(8,128)(2,1)}, f32[128,128]{1,0:T(8,128)}, f32[128,128]{1,0:T(8,128)}) custom-call(s32[1]{0:T(128)} %bitcast.1.rank_ref, s32[1,128]{1,0:T(1,128)} %bitcast.13, f32[1,128]{1,0:T(1,128)} %constant.7.clone.inv_ref, bf16[576,128]{1,0:T(8,128)(2,1)} %bitcast.12), custom_call_target="tpu_custom_call" | custom-call | tf_op jit(solution)/shard_map/share/pallas_call | solution.py:395
  3.0 5.9 %all-to-all-start = ((bf16[8,144,512]{2,1,0:T(8,128)(2,1)}), bf16[8,144,512]{2,1,0:T(8,128)(2,1)S(1)}, u32[]{:S(2)}, u32[]{:S(2)}) async-start(bf16[8,144,512]{2,1,0:T(8,128)(2,1)} %get-tuple-element.12), calls=%async_computation | async-start | bytes 2359296 | tf_op jit(solution)/shard_map/all_to_all | solution.py:404
  8.9 4.7 %absorb.1.second_ref = bf16[2,2,512,640]{3,2,1,0:T(8,128)(2,1)} custom-call(bf16[128,1024]{1,0:T(8,128)(2,1)} %qn_ref.1, bf16[128,512]{1,0:T(8,128)(2,1)} %qr_ref.1, bf16[128,1024]{1,0:T(8,128)(2,1)} %go_ref.1, bf16[512,1024]{1,0:T(8,128)(2,1)} %uk_hbm.1, bf16[512,1024]{1,0:T(8,128)(2,1)} %uv_ref.1, f32[128,128]{1,0:T(8,128)} %get-tuple-element.13.cos_ref, ...), custom_call_target="tpu_custom_call" | custom-call | flops 300000000 | bytes 8000000 | tf_op jit(solution)/shard_map/absorb/pallas_call | solution.py:408
  13.6 0.0 copy-start.3
  13.6 11.0 %all-to-all-done.first_ref = bf16[8,144,512]{2,1,0:T(8,128)(2,1)S(1)} async-done(((bf16[8,144,512]{2,1,0:T(8,128)(2,1)}), bf16[8,144,512]{2,1,0:T(8,128)(2,1)S(1)}, u32[]{:S(2)}, u32[]{:S(2)}) %all-to-all-start) | async-done | bytes 1179680 | tf_op jit(solution)/shard_map/all_to_all | solution.py:404
  24.6 0.0 copy-start
  24.6 0.0 collective-permute-start
  24.6 2.8 %collective-permute-done.other_ref = bf16[8,144,512]{2,1,0:T(8,128)(2,1)S(1)} collective-permute-done((bf16[8,144,512]{2,1,0:T(8,128)(2,1)S(1)}, bf16[8,144,512]{2,1,0:T(8,128)(2,1)S(1)}, u32[]{:S(2)}, u32[]{:S(2)}) %collective-permute-start) | collective-permute-done | bytes 1179680 | tf_op jit(solution)/shard_map/ppermute | solution.py:429
  27.4 0.0 copy-done.3
  27.4 0.0 copy-done
  27.4 10.7 %attend.1 = (bf16[8,144,512]{2,1,0:T(8,128)(2,1)S(1)}, bf16[8,144,512]{2,1,0:T(8,128)(2,1)S(1)}, bf16[2304,512]{1,0:T(8,128)(2,1)}, bf16[2048,640]{1,0:T(8,128)(2,1)}) custom-call(s32[2,16]{1,0:T(2,128)S(1)} %bitcast.10, s32[1]{0:T(128)} %bitcast.1.rank_ref, bf16[8,144,512]{2,1,0:T(8,128)(2,1)S(1)} %after.1.mine_ref, ...), custom_call_target="tpu_custom_call" | custom-call | tf_op jit(solution)/shard_map/attend/pallas_call | solution.py:369
  38.1 0.2 collective-permute-start.1
  38.3 2.7 %collective-permute-done.1 = bf16[8,144,512]{2,1,0:T(8,128)(2,1)S(1)} collective-permute-done((bf16[8,144,512]{2,1,0:T(8,128)(2,1)S(1)}, bf16[8,144,512]{2,1,0:T(8,128)(2,1)S(1)}, u32[]{:S(2)}, u32[]{:S(2)}) %collective-permute-start.1) | collective-permute-done | bytes 1179680 | tf_op jit(solution)/shard_map/ppermute | solution.py:432
  41.0 1.4 %add_convert_fusion = bf16[8,144,512]{2,1,0:T(8,128)(2,1)} fusion(bf16[8,144,512]{2,1,0:T(8,128)(2,1)S(1)} %collective-permute-done.1, bf16[8,144,512]{2,1,0:T(8,128)(2,1)S(1)} %get-tuple-element.19), kind=kLoop, calls=%fused_computation | loop fusion | flops 2359296 | bytes 3538944 | tf_op jit(solution)/shard_map/convert_element_type | solution.py:433
  42.4 4.2 %all-to-all-start.1 = ((bf16[8,144,512]{2,1,0:T(8,128)(2,1)}), bf16[8,144,512]{2,1,0:T(8,128)(2,1)S(1)}, u32[]{:S(2)}, u32[]{:S(2)}) async-start(bf16[8,144,512]{2,1,0:T(8,128)(2,1)} %add_convert_fusion), calls=%async_computation.1 | async-start | bytes 2359296 | tf_op jit(solution)/shard_map/all_to_all | solution.py:434
  46.6 0.0 copy-start.1
  46.6 0.0 copy-start.2
  46.6 8.2 %queries.1 = (bf16[128,1024]{1,0:T(8,128)(2,1)}, bf16[128,512]{1,0:T(8,128)(2,1)}) custom-call(s32[2,16]{1,0:T(2,128)} %bitcast.9, s32[1]{0:T(128)} %bitcast.1.rank_ref, bf16[2048,640]{1,0:T(8,128)(2,1)} %get-tuple-element.15.keys_hbm, bf16[2304,512]{1,0:T(8,128)(2,1)} %get-tuple-element.16.ds_hbm, bf16[512,1024]{1,0:T(8,128)(2,1)} %uk_hbm.1, ...), custom_call_target="tpu_custom_call" | custom-call | flops 4000000000 | bytes 9000000 | tf_op jit(solution)/shard_map/queries/pallas_call | solution.py:436
  54.9 7.8 %all-to-all-done.1.parts_ref = bf16[8,144,512]{2,1,0:T(8,128)(2,1)S(1)} async-done(((bf16[8,144,512]{2,1,0:T(8,128)(2,1)}), bf16[8,144,512]{2,1,0:T(8,128)(2,1)S(1)}, u32[]{:S(2)}, u32[]{:S(2)}) %all-to-all-start.1) | async-done | bytes 1179680 | tf_op jit(solution)/shard_map/all_to_all | solution.py:434
  62.7 0.0 copy-done.1
  62.7 0.0 copy-done.2
  62.7 0.3 chips.1
  63.0 20.1 %all_to_all.20.parts_ref = bf16[16,8,576]{2,1,0:T(8,128)(2,1)S(1)} all-to-all(bf16[16,8,576]{2,1,0:T(8,128)(2,1)S(1)} %bitcast.8), channel_id=1, replica_groups=mesh['ctx'=16,'head'=16] {'head'}, dimensions={0} | all-to-all | bytes 294912 | tf_op jit(solution)/shard_map/all_to_all | solution.py:462
  83.1 12.0 %all_to_all.21 = bf16[16,8,576]{2,1,0:T(8,128)(2,1)S(1)} all-to-all(bf16[16,8,576]{2,1,0:T(8,128)(2,1)S(1)} %heads.1), channel_id=1, replica_groups=mesh['ctx'=16,'head'=16] {'head'}, dimensions={0} | all-to-all | bytes 294912 | tf_op jit(solution)/shard_map/all_to_all | solution.py:471
  95.1 0.8 copy.13
  (2 shorter events, 0.0 us)
Async XLA Ops:
  3.0 21.6 %all-to-all-start = ((bf16[8,144,512]{2,1,0:T(8,128)(2,1)}), bf16[8,144,512]{2,1,0:T(8,128)(2,1)S(1)}, u32[]{:S(2)}, u32[]{:S(2)}) async-start(bf16[8,144,512]{2,1,0:T(8,128)(2,1)} %get-tuple-element.12), calls=%async_computation | async-start | bytes 2359296 | tf_op jit(solution)/shard_map/all_to_all | solution.py:404
  13.6 13.8 %copy-start.3 = (s32[16,2]{0,1:T(2,128)S(1)}, s32[16,2]{0,1:T(2,128)}, u32[]{:S(2)}) copy-start(s32[16,2]{0,1:T(2,128)} %param.16) | copy-start | bytes 388
  24.6 2.9 %copy-start = (bf16[2,2,512,640]{3,2,1,0:T(8,128)(2,1)S(1)}, bf16[2,2,512,640]{3,2,1,0:T(8,128)(2,1)}, u32[]{:S(2)}) copy-start(bf16[2,2,512,640]{3,2,1,0:T(8,128)(2,1)} %absorb.1.second_ref) | copy-start | bytes 7864324
  24.6 2.8 %collective-permute-start = (bf16[8,144,512]{2,1,0:T(8,128)(2,1)S(1)}, bf16[8,144,512]{2,1,0:T(8,128)(2,1)S(1)}, u32[]{:S(2)}, u32[]{:S(2)}) collective-permute-start(bf16[8,144,512]{2,1,0:T(8,128)(2,1)S(1)} %after.1.mine_ref), channel_id=1, source_target_pairs={{0,16},{16,0},{32,48},{48,32},{64,80},{80,64},{96,112},{112,96},{1... | collective-permute-start | bytes 3538952 | tf_op jit(solution)/shard_map/ppermute | solution.py:429
  38.1 2.9 %collective-permute-start.1 = (bf16[8,144,512]{2,1,0:T(8,128)(2,1)S(1)}, bf16[8,144,512]{2,1,0:T(8,128)(2,1)S(1)}, u32[]{:S(2)}, u32[]{:S(2)}) collective-permute-start(bf16[8,144,512]{2,1,0:T(8,128)(2,1)S(1)} %get-tuple-element.20), channel_id=1, source_target_pairs={{0,16},{16,0},{32,48},{48,32},{64,80},{80,64},{96,112},{112,96},{1... | collective-permute-start | bytes 3538952 | tf_op jit(solution)/shard_map/ppermute | solution.py:432
  42.4 20.3 %all-to-all-start.1 = ((bf16[8,144,512]{2,1,0:T(8,128)(2,1)}), bf16[8,144,512]{2,1,0:T(8,128)(2,1)S(1)}, u32[]{:S(2)}, u32[]{:S(2)}) async-start(bf16[8,144,512]{2,1,0:T(8,128)(2,1)} %add_convert_fusion), calls=%async_computation.1 | async-start | bytes 2359296 | tf_op jit(solution)/shard_map/all_to_all | solution.py:434
  46.6 16.1 %copy-start.1 = (f32[128,128]{1,0:T(8,128)S(1)}, f32[128,128]{1,0:T(8,128)}, u32[]{:S(2)}) copy-start(f32[128,128]{1,0:T(8,128)} %get-tuple-element.13.cos_ref) | copy-start | bytes 196612
  46.6 16.1 %copy-start.2 = (f32[128,128]{1,0:T(8,128)S(1)}, f32[128,128]{1,0:T(8,128)}, u32[]{:S(2)}) copy-start(f32[128,128]{1,0:T(8,128)} %get-tuple-element.14.sin_ref) | copy-start | bytes 196612

commit v4 on v3

--- a/solution.py
+++ b/solution.py
@@ -39,6 +39,10 @@
     for side in range(2)
     for z in range(8)
 ]
+ALONG_X = [(i, i ^ (8 * N_HEAD + 8)) for i in range(N_CTX * N_HEAD)]
+ALONG_Y1 = [(c, c ^ 2) for c in range(N_CTX)]
+ALONG_Y3 = [(c, c ^ 6) for c in range(N_CTX)]
+OWNERS = (0, 2, 4, 6, 8, 10, 12, 14)
 SWAP = [(c, c ^ 1) for c in range(N_CTX)]
 
 AGAINST = (((1,), (1,)), ((), ()))
@@ -125,7 +129,7 @@
     return jnp.concatenate(pieces, axis=0)
 
 
-def share_kernel(rank_ref, pos_ref, inv_ref, comp_ref, out_ref, cos_ref, sin_ref, tile):
+def share_kernel(rank_ref, pos_ref, inv_ref, comp_ref, tile, cos_ref, sin_ref):
     pos = jnp.broadcast_to(pos_ref[...].astype(f32), (ROWS, ROWS)).T
     cosine, sine = cos_sin(pos * inv_ref[...])
     sine = jnp.where((lanes_of(sine.shape) & 63) < 32, -sine, sine)
@@ -137,8 +141,6 @@
     rotated = x * cosine + pltpu.roll(x, 32, 1) * sine
     for j in range(2):
         tile[ROWS:, j * 256:(j + 1) * 256] = pack_rope(rotated[j * HALF:(j + 1) * HALF]).astype(bf16)
-    for i in range(N_CHIP):
-        out_ref[i] = tile[...]
     cos_ref[...] = cosine
     sin_ref[...] = sine
 
@@ -194,24 +196,19 @@
     return pl.ds(c * CHUNK if isinstance(c, int) else pl.multiple_of(c * CHUNK, CHUNK), n * CHUNK)
 
 
-def attend_kernel(bm_ref, rank_ref, mine_ref, other_ref, both,
-                  dmine_ref, dother_ref, ds_hbm, keys_hbm,
-                  probs, dprobs, tops, ds, keys, dlat, drope, key_sem, ds_sems):
+def attend_kernel(bm_ref, rank_ref, both, *refs):
+    shares, refs = refs[:2 * N_CHIP], refs[2 * N_CHIP:]
+    dmine_ref, dother_ref, ds, keys, probs, dprobs, tops, dlat, drope = refs
     rank = rank_ref[0]
     core = rank & 1
     places = step_places(bm_ref, rank)
-    for chip in range(N_CHIP):
-        for k, ref in enumerate((mine_ref, other_ref)):
-            row = 2 * chip + (core ^ k)
-            for j in range(2):
-                block = bm_ref[j, row]
-                rows = pl.ds(pl.multiple_of(block * HALF, HALF), HALF)
-                keys[rows, :D_LAT] = ref[chip, j * HALF:(j + 1) * HALF, :]
-                packed = ref[chip, ROWS:, j * 256:(j + 1) * 256].astype(f32)
-                keys[rows, D_LAT:] = unpack_rope(packed).astype(bf16)
-
-    moves = [pltpu.make_async_copy(keys, keys_hbm, key_sem)]
-    moves[0].start()
+    for i, ref in enumerate(shares):
+        row = rank ^ (OWNERS[i % N_CHIP] ^ (i // N_CHIP))
+        for j in range(2):
+            rows = pl.ds(pl.multiple_of(bm_ref[j, row] * HALF, HALF), HALF)
+            keys[rows, :D_LAT] = ref[j * HALF:(j + 1) * HALF, :]
+            packed = ref[ROWS:, j * 256:(j + 1) * 256].astype(f32)
+            keys[rows, D_LAT:] = unpack_rope(packed).astype(bf16)
 
     zero = jnp.zeros((1, LANES), f32)
     start = (jnp.full((1, LANES), HIDDEN, f32), zero, zero)
@@ -252,8 +249,6 @@
         p = probs[at] * (jnp.exp2(tops[i] - top) * inverse)
         d = (p * (dprobs[at] - delta)).astype(bf16)
         ds[at] = d
-        moves.append(pltpu.make_async_copy(ds.at[at], ds_hbm.at[at], ds_sems.at[i]))
-        moves[-1].start()
         pair = jnp.concatenate([d, p.astype(bf16)], axis=1)
         latent = jnp.dot(pair, both[j, :, :D_LAT], preferred_element_type=f32)
         rope = jnp.dot(d, both[j, :LANES, D_LAT:], preferred_element_type=f32)
@@ -283,8 +278,14 @@
                 block = bm_ref[j, row]
                 ref[chip, j * HALF:(j + 1) * HALF, :] = dlat[pl.ds(pl.multiple_of(block * HALF, HALF), HALF), :]
                 ref[chip, ROWS:, j * 256:(j + 1) * 256] = drope[pl.ds(pl.multiple_of(block * 16, 16), 16), :]
-    for move in moves:
-        move.wait()
+
+
+def spill_kernel(ds, keys, ds_hbm, keys_hbm, sems):
+    copies = [pltpu.make_async_copy(ds, ds_hbm, sems.at[0]), pltpu.make_async_copy(keys, keys_hbm, sems.at[1])]
+    for copy in copies:
+        copy.start()
+    for copy in copies:
+        copy.wait()
 
 
 def queries_kernel(bm_ref, rank_ref, keys_hbm, ds_hbm, uk_hbm, cos_ref, sin_ref, gqn_ref, gqr_ref,
@@ -324,6 +325,11 @@
     pass
 
 
+def pair_kernel(ours_ref, theirs_ref, later_ref, out_ref):
+    for i in range(N_CHIP):
+        out_ref[i] = (ours_ref[i].astype(f32) + theirs_ref[i].astype(f32)).astype(bf16)
+
+
 def chips_kernel(parts_ref, cos_ref, sin_ref, later_ref, out_ref):
     total = parts_ref[0].astype(f32)
     for i in range(1, N_CHIP):
@@ -364,23 +370,18 @@
 
 def attend_call(*operands):
     shape = jax.ShapeDtypeStruct
-    dma = pltpu.SemaphoreType.DMA
     piece = shape((N_CHIP, PACKED, D_LAT), bf16)
     return pl.pallas_call(
         attend_kernel,
-        in_specs=[SMEM, SMEM] + whole(3),
-        out_specs=(*whole(2), HBM, HBM),
-        out_shape=(piece, piece, pltpu.HBM((STEPS * CHUNK, LANES), bf16), pltpu.HBM((TOTAL, D_PAD), bf16)),
+        in_specs=[SMEM, SMEM] + whole(1 + 2 * N_CHIP),
+        out_specs=tuple(whole(4)),
+        out_shape=(piece, piece, shape((STEPS * CHUNK, LANES), bf16), shape((TOTAL, D_PAD), bf16)),
         scratch_shapes=[
             pltpu.VMEM((STEPS * CHUNK, LANES), f32),
             pltpu.VMEM((STEPS * CHUNK, LANES), f32),
             pltpu.VMEM((STEPS, 1, LANES), f32),
-            pltpu.VMEM((STEPS * CHUNK, LANES), bf16),
-            pltpu.VMEM((TOTAL, D_PAD), bf16),
             pltpu.VMEM((TOTAL, D_LAT), bf16),
             pltpu.VMEM((N_BLOCK * 16, 256), bf16),
-            dma,
-            dma((STEPS,)),
         ],
         compiler_params=params(36),
         name="attend",
@@ -396,12 +397,16 @@
         share_kernel,
         in_specs=[SMEM] + whole(3),
         out_specs=tuple(whole(3)),
-        out_shape=(shape((N_CHIP, PACKED, D_LAT), bf16), table, table),
-        scratch_shapes=[pltpu.VMEM((PACKED, D_LAT), bf16)],
+        out_shape=(shape((PACKED, D_LAT), bf16), table, table),
         compiler_params=params(ALL_MIB),
         name="share",
     )(rank, positions.reshape(1, ROWS), jnp.asarray(frequencies()), compressed.T)
-    mine = lax.all_to_all(shared, ("ctx", "head"), 0, 0, axis_index_groups=GROUPS)
+    x = lambda a: lax.ppermute(a, ("ctx", "head"), ALONG_X)
+    y1 = lambda a: lax.ppermute(a, "ctx", ALONG_Y1)
+    y3 = lambda a: lax.ppermute(a, "ctx", ALONG_Y3)
+    swap = lambda a: lax.ppermute(a, "ctx", SWAP)
+    held = {0: shared, 8: x(shared), 2: y1(shared), 6: y3(shared)}
+    held.update({10: y1(held[8]), 4: y3(held[2]), 14: x(held[6])})
     pair_cols = lambda width: pl.BlockSpec((ROWS, width), lambda p: (0, p))
     fixed = pl.BlockSpec((ROWS, 128), lambda p: (0, 0))
     weight = pl.BlockSpec((D_LAT, 256), lambda p: (0, p))
@@ -411,26 +416,45 @@
         in_specs=[pair_cols(256), pair_cols(128), pair_cols(256), weight, weight, fixed, fixed],
         out_specs=pl.BlockSpec((2, 2, 128, D_PAD), lambda p: (0, 0, p, 0)),
         out_shape=shape((2, 2, LANES, D_PAD), bf16),
-        compiler_params=params(ALL_MIB),
+        compiler_params=params(16),
         cost_estimate=pl.CostEstimate(flops=300_000_000, bytes_accessed=8_000_000, transcendentals=0),
         name="absorb",
-    )(q_nope, q_rope, grad_out, w_uk, w_uv, cosine, sine)
-
-    mine = pl.pallas_call(
+    )(*map(in_hbm, (q_nope, q_rope, grad_out, w_uk, w_uv, cosine, sine)))
+
+    held[4] = pl.pallas_call(
         after_kernel,
         in_specs=[ANY, ANY],
         out_specs=ANY,
-        out_shape=shape(mine.shape, bf16),
+        out_shape=shape((PACKED, D_LAT), bf16),
         input_output_aliases={0: 0},
         compiler_params=params(8),
         name="after",
-    )(mine, in_hbm(both))
+    )(held[4], both)
+    held[12] = x(held[4])
+    mine = [held[owner] for owner in OWNERS]
+    other = [swap(share) for share in mine]
     both = both.reshape(2, 2 * LANES, D_PAD)
-    other = lax.ppermute(mine, "ctx", SWAP)
-    dmine, dother, ds, keys = attend_call(blocks, rank, mine, other, both)
+    dmine, dother, ds, keys = attend_call(blocks, rank, both, *mine, *other)
+    ds, keys = pl.pallas_call(
+        spill_kernel,
+        in_specs=[ANY, ANY],
+        out_specs=(HBM, HBM),
+        out_shape=(pltpu.HBM(ds.shape, bf16), pltpu.HBM(keys.shape, bf16)),
+        scratch_shapes=[pltpu.SemaphoreType.DMA((2,))],
+        compiler_params=params(8),
+        cost_estimate=pl.CostEstimate(flops=0, bytes_accessed=10_000_000, transcendentals=0),
+        name="spill",
+    )(ds, keys)
 
     theirs = lax.ppermute(dother, "ctx", SWAP)
-    summed = (dmine.astype(f32) + theirs.astype(f32)).astype(bf16)
+    summed = pl.pallas_call(
+        pair_kernel,
+        in_specs=whole(2) + [HBM],
+        out_specs=whole(1)[0],
+        out_shape=shape(dmine.shape, bf16),
+        compiler_params=params(16),
+        name="pair",
+    )(dmine, theirs, in_hbm(ds))
     parts = lax.all_to_all(summed, ("ctx", "head"), 0, 0, axis_index_groups=GROUPS)
 
     grad_q_nope, grad_q_rope = pl.pallas_call(

time: 96.3 us -> 93.6 us (0.972)
  waiting for transfers between devices: 24.4 us -> 17.8 us
  starting transfers between devices: 10.4 us -> 15.5 us
  other arithmetic: 1.38 us -> 0 us
    all_to_all x1 -> x0, waiting for transfers between devices: 11 us -> none  [on_device(): lax.all_to_all(shared, ('ctx', 'head'), 0, 0, axis_index_groups=GROUPS)]
    ppermute x1 -> x15, starting transfers between devices: 0.01 us -> 10.7 us  [the longest x2 5.2 us: on_device(): y3 = lambda a: lax.ppermute(a, 'ctx', ALONG_Y3)]
    ppermute x1 -> x15, waiting for transfers between devices: 2.84 us -> 9.66 us  [the longest x2 5.08 us: on_device(): y1 = lambda a: lax.ppermute(a, 'ctx', ALONG_Y1)]
    all_to_all x1 -> x0, starting transfers between devices: 5.93 us -> none  [on_device(): lax.all_to_all(shared, ('ctx', 'head'), 0, 0, axis_index_groups=GROUPS)]
    ppermute x1, waiting for transfers between devices: 2.71 us -> 0.46 us  [on_device(): theirs = lax.ppermute(dother, 'ctx', SWAP)]
    pallas_call x1 -> x3, Pallas kernels: 10.7 us -> 12.2 us  [the longest x1 8.63 us: attend_call(): pl.pallas_call(attend_kernel, in_specs=[SMEM, SMEM] + whole(1 + 2 * N_CHI...]
    convert_element_type x1 -> x0, other arithmetic: 1.38 us -> none  [on_device(): summed = (dmine.astype(f32) + theirs.astype(f32)).astype(bf16)]
    pallas_call x1, Pallas kernels: 4.66 us -> 3.45 us  [on_device(): pl.pallas_call(absorb_kernel, grid=(HEADS // 2,), in_specs=[pair_cols(256...]
  transfers between devices with their start and end apart: 4 -> 17, of which waited for: 4 -> 7; matrix products, arithmetic and copies ran while one was open for 0% -> 0% of each run, Pallas kernels for 13% -> 15%
where the time goes in v4:
time: 93.6 us; the launch traced here: 93.2 us
  blocking collectives  32.2 us (34%)
  Pallas kernels  26.1 us (28%)
  waiting for transfers between devices  17.8 us (19%)
  starting transfers between devices  15.5 us (17%)
    all_to_all x1, blocking collectives, on_device(): lax.all_to_all(owned.reshape(N_HEAD, ROWS // N_HEAD, D_ALL), 'head', 0, 0)  20.3 us
    all_to_all x1, blocking collectives, on_device(): grad_compressed = lax.all_to_all(slabs, 'head', 0, 0).reshape(ROWS, D_ALL)  12 us
    pallas_call x1, Pallas kernels, attend_call(): pl.pallas_call(attend_kernel, in_specs=[SMEM, SMEM] + whole(1 + 2 * N_CHI...  8.63 us
    pallas_call x1, Pallas kernels, on_device(): pl.pallas_call(queries_kernel, in_specs=[SMEM, SMEM, HBM, HBM, HBM] + who...  8.23 us
    all_to_all x1, waiting for transfers between devices, on_device(): lax.all_to_all(summed, ('ctx', 'head'), 0, 0, axis_index_groups=GROUPS)  7.72 us
    ppermute x2, starting transfers between devices, on_device(): y3 = lambda a: lax.ppermute(a, 'ctx', ALONG_Y3)  5.2 us
    ppermute x2, waiting for transfers between devices, on_device(): y1 = lambda a: lax.ppermute(a, 'ctx', ALONG_Y1)  5.08 us
    all_to_all x1, starting transfers between devices, on_device(): lax.all_to_all(summed, ('ctx', 'head'), 0, 0, axis_index_groups=GROUPS)  4.62 us
  transfers between devices with their start and end apart: 17, of which 7 were waited for; matrix products, arithmetic and copies ran while one was open for 0% of the time, Pallas kernels for 15%

profile of v4, /device:TPU:4, one launch (start us, length us, event | category | flops | bytes accessed | tf_op | source)
XLA Modules:
  0.0 93.2 jit_solution(16296845090634266864)
XLA Ops:
  0.6 1.9 %share.1 = (bf16[144,512]{1,0:T(8,128)(2,1)}, f32[128,128]{1,0:T(8,128)}, f32[128,128]{1,0:T(8,128)}) custom-call(s32[1]{0:T(128)} %bitcast.1.rank_ref, s32[1,128]{1,0:T(1,128)} %bitcast.13, f32[1,128]{1,0:T(1,128)} %constant.7.clone.inv_ref, bf16[576,128]{1,0:T(8,128)(2,1)} %bitcast.12), custom_call_target="tpu_custom_call" | custom-call | tf_op jit(solution)/shard_map/share/pallas_call | solution.py:396
  2.6 1.6 %collective-permute-start = (bf16[144,512]{1,0:T(8,128)(2,1)}, bf16[144,512]{1,0:T(8,128)(2,1)S(1)}, u32[]{:S(2)}, u32[]{:S(2)}) collective-permute-start(bf16[144,512]{1,0:T(8,128)(2,1)} %get-tuple-element.16.refs_0_), channel_id=1, source_target_pairs={{0,32},{16,48},{32,0},{48,16},{64,96},{80,112},{96,64},{112,80},{1... | collective-permute-start | bytes 442376 | tf_op jit(solution)/shard_map/ppermute | solution.py:405
  4.1 0.5 collective-permute-start.3
  4.7 2.2 %collective-permute-start.2 = (bf16[144,512]{1,0:T(8,128)(2,1)}, bf16[144,512]{1,0:T(8,128)(2,1)S(1)}, u32[]{:S(2)}, u32[]{:S(2)}) collective-permute-start(bf16[144,512]{1,0:T(8,128)(2,1)} %get-tuple-element.16.refs_0_), channel_id=1, source_target_pairs={{0,96},{16,112},{32,64},{48,80},{64,32},{80,48},{96,0},{112,16},{1... | collective-permute-start | bytes 442376 | tf_op jit(solution)/shard_map/ppermute | solution.py:406
  6.9 1.5 %collective-permute-done.refs_1_ = bf16[144,512]{1,0:T(8,128)(2,1)S(1)} collective-permute-done((bf16[144,512]{1,0:T(8,128)(2,1)}, bf16[144,512]{1,0:T(8,128)(2,1)S(1)}, u32[]{:S(2)}, u32[]{:S(2)}) %collective-permute-start) | collective-permute-done | bytes 147488 | tf_op jit(solution)/shard_map/ppermute | solution.py:405
  8.4 3.0 %collective-permute-start.1 = (bf16[144,512]{1,0:T(8,128)(2,1)S(1)}, bf16[144,512]{1,0:T(8,128)(2,1)S(1)}, u32[]{:S(2)}, u32[]{:S(2)}) collective-permute-start(bf16[144,512]{1,0:T(8,128)(2,1)S(1)} %collective-permute-done.refs_1_), channel_id=1, source_target_pairs={{0,96},{16,112},{32,64},{48,80},{64,32},{80,48},{96,0},{112,16},{1... | collective-permute-start | bytes 442376 | tf_op jit(solution)/shard_map/ppermute | solution.py:406
  11.4 3.5 %absorb.1.second_ref = bf16[2,2,512,640]{3,2,1,0:T(8,128)(2,1)S(1)} custom-call(bf16[128,1024]{1,0:T(8,128)(2,1)} %qn_ref.1, bf16[128,512]{1,0:T(8,128)(2,1)} %qr_ref.1, bf16[128,1024]{1,0:T(8,128)(2,1)} %go_ref.1, bf16[512,1024]{1,0:T(8,128)(2,1)} %uk_hbm.1, bf16[512,1024]{1,0:T(8,128)(2,1)} %uv_ref.1, f32[128,128]{1,0:T(8,128)} %get-tuple-element.14.cos_ref, ...), custom_call_target="tpu_custom_call" | custom-call | flops 300000000 | bytes 8000000 | tf_op jit(solution)/shard_map/absorb/pallas_call | solution.py:413
  14.8 0.0 copy-start.2
  14.8 0.0 copy-start.3
  14.9 0.6 collective-permute-start.11
  15.5 0.1 collective-permute-start.4
  15.6 0.1 collective-permute-start.10
  15.7 0.6 collective-permute-start.6
  16.2 1.5 %collective-permute-start.5 = (bf16[144,512]{1,0:T(8,128)(2,1)S(1)}, bf16[144,512]{1,0:T(8,128)(2,1)S(1)}, u32[]{:S(2)}, u32[]{:S(2)}) collective-permute-start(bf16[144,512]{1,0:T(8,128)(2,1)S(1)} %after.1.refs_2_), channel_id=1, source_target_pairs={{0,136},{1,137},{2,138},{3,139},{4,140},{5,141},{6,142},{7,143},{8... | collective-permute-start | bytes 442376 | tf_op jit(solution)/shard_map/ppermute | solution.py:404
  17.7 3.6 %collective-permute-done.4.refs_5_ = bf16[144,512]{1,0:T(8,128)(2,1)S(1)} collective-permute-done((bf16[144,512]{1,0:T(8,128)(2,1)S(1)}, bf16[144,512]{1,0:T(8,128)(2,1)S(1)}, u32[]{:S(2)}, u32[]{:S(2)}) %collective-permute-start.4) | collective-permute-done | bytes 147488 | tf_op jit(solution)/shard_map/ppermute | solution.py:405
  21.3 0.5 collective-permute-start.12
  21.8 0.5 collective-permute-done.6.refs_7_
  22.4 2.7 %collective-permute-done.5.refs_6_ = bf16[144,512]{1,0:T(8,128)(2,1)S(1)} collective-permute-done((bf16[144,512]{1,0:T(8,128)(2,1)S(1)}, bf16[144,512]{1,0:T(8,128)(2,1)S(1)}, u32[]{:S(2)}, u32[]{:S(2)}) %collective-permute-start.5) | collective-permute-done | bytes 147488 | tf_op jit(solution)/shard_map/ppermute | solution.py:404
  25.1 0.0 collective-permute-start.13
  25.1 1.3 %collective-permute-done.13.refs_14_ = bf16[144,512]{1,0:T(8,128)(2,1)S(1)} collective-permute-done((bf16[144,512]{1,0:T(8,128)(2,1)S(1)}, bf16[144,512]{1,0:T(8,128)(2,1)S(1)}, u32[]{:S(2)}, u32[]{:S(2)}) %collective-permute-start.13) | collective-permute-done | bytes 147488 | tf_op jit(solution)/shard_map/ppermute | solution.py:407
  26.4 8.6 %attend.1 = (bf16[8,144,512]{2,1,0:T(8,128)(2,1)S(1)}, bf16[8,144,512]{2,1,0:T(8,128)(2,1)S(1)}, bf16[2304,512]{1,0:T(8,128)(2,1)S(1)}, bf16[2048,640]{1,0:T(8,128)(2,1)S(1)}) custom-call(s32[2,16]{1,0:T(2,128)S(1)} %bitcast.10, s32[1]{0:T(128)} %bitcast.1.rank_ref, bf16[2,1024,640]{2,1,0:T(8,128)(2,1)S(1)} %bitcast.7, bf16[144,512]{1,0:T(8,128)(2,1)S(1)} %copy-done.2, ...), custom_call_target="tpu_custom_call" | custom-call | tf_op jit(solution)/shard_map/attend/pallas_call | solution.py:374
  35.1 0.2 collective-permute-start.15
  35.3 2.2 %spill.1 = (bf16[2304,512]{1,0:T(8,128)(2,1)}, bf16[2048,640]{1,0:T(8,128)(2,1)}) custom-call(bf16[2304,512]{1,0:T(8,128)(2,1)S(1)} %get-tuple-element.17.ds, bf16[2048,640]{1,0:T(8,128)(2,1)S(1)} %get-tuple-element.18.keys), custom_call_target="tpu_custom_call" | custom-call | bytes 10000000 | tf_op jit(solution)/shard_map/spill/pallas_call | solution.py:438
  37.5 0.5 collective-permute-done.15.theirs_ref
  38.0 1.3 %pair.1 = bf16[8,144,512]{2,1,0:T(8,128)(2,1)} custom-call(bf16[8,144,512]{2,1,0:T(8,128)(2,1)S(1)} %get-tuple-element.23.ours_ref, bf16[8,144,512]{2,1,0:T(8,128)(2,1)S(1)} %collective-permute-done.15.theirs_ref, bf16[2304,512]{1,0:T(8,128)(2,1)} %get-tuple-element.20.ds_hbm.later_ref), custom_call_target="tpu_custom_call" | custom-call | tf_op jit(solution)/shard_map/pair/pallas_call | solution.py:450
  39.3 4.6 %all-to-all-start = ((bf16[8,144,512]{2,1,0:T(8,128)(2,1)}), bf16[8,144,512]{2,1,0:T(8,128)(2,1)S(1)}, u32[]{:S(2)}, u32[]{:S(2)}) async-start(bf16[8,144,512]{2,1,0:T(8,128)(2,1)} %pair.1), calls=%async_computation | async-start | bytes 2359296 | tf_op jit(solution)/shard_map/all_to_all | solution.py:458
  44.0 8.2 %queries.1 = (bf16[128,1024]{1,0:T(8,128)(2,1)}, bf16[128,512]{1,0:T(8,128)(2,1)}) custom-call(s32[2,16]{1,0:T(2,128)} %bitcast.9, s32[1]{0:T(128)} %bitcast.1.rank_ref, bf16[2048,640]{1,0:T(8,128)(2,1)} %get-tuple-element.19.keys_hbm, bf16[2304,512]{1,0:T(8,128)(2,1)} %get-tuple-element.20.ds_hbm.later_ref, bf16[512,1024]{1,0:T(8,128)(2,1)} %uk_hbm.1, ...), custom_call_target="tpu_custom_call" | custom-call | flops 4000000000 | bytes 9000000 | tf_op jit(solution)/shard_map/queries/pallas_call | solution.py:460
  52.2 7.7 %all-to-all-done.parts_ref = bf16[8,144,512]{2,1,0:T(8,128)(2,1)S(1)} async-done(((bf16[8,144,512]{2,1,0:T(8,128)(2,1)}), bf16[8,144,512]{2,1,0:T(8,128)(2,1)S(1)}, u32[]{:S(2)}, u32[]{:S(2)}) %all-to-all-start) | async-done | bytes 1179680 | tf_op jit(solution)/shard_map/all_to_all | solution.py:458
  59.9 0.3 chips.1
  60.2 20.3 %all_to_all.15.parts_ref = bf16[16,8,576]{2,1,0:T(8,128)(2,1)S(1)} all-to-all(bf16[16,8,576]{2,1,0:T(8,128)(2,1)S(1)} %bitcast.8), channel_id=1, replica_groups=mesh['ctx'=16,'head'=16] {'head'}, dimensions={0} | all-to-all | bytes 294912 | tf_op jit(solution)/shard_map/all_to_all | solution.py:486
  80.5 12.0 %all_to_all.16 = bf16[16,8,576]{2,1,0:T(8,128)(2,1)S(1)} all-to-all(bf16[16,8,576]{2,1,0:T(8,128)(2,1)S(1)} %heads.1), channel_id=1, replica_groups=mesh['ctx'=16,'head'=16] {'head'}, dimensions={0} | all-to-all | bytes 294912 | tf_op jit(solution)/shard_map/all_to_all | solution.py:495
  92.5 0.8 copy.13
  (22 shorter events, 0.1 us)
Async XLA Ops:
  2.6 5.8 %collective-permute-start = (bf16[144,512]{1,0:T(8,128)(2,1)}, bf16[144,512]{1,0:T(8,128)(2,1)S(1)}, u32[]{:S(2)}, u32[]{:S(2)}) collective-permute-start(bf16[144,512]{1,0:T(8,128)(2,1)} %get-tuple-element.16.refs_0_), channel_id=1, source_target_pairs={{0,32},{16,48},{32,0},{48,16},{64,96},{80,112},{96,64},{112,80},{1... | collective-permute-start | bytes 442376 | tf_op jit(solution)/shard_map/ppermute | solution.py:405
  4.1 10.7 %collective-permute-start.3 = (bf16[144,512]{1,0:T(8,128)(2,1)}, bf16[144,512]{1,0:T(8,128)(2,1)S(1)}, u32[]{:S(2)}, u32[]{:S(2)}) collective-permute-start(bf16[144,512]{1,0:T(8,128)(2,1)} %get-tuple-element.16.refs_0_), channel_id=1, source_target_pairs={{0,136},{1,137},{2,138},{3,139},{4,140},{5,141},{6,142},{7,143},{8... | collective-permute-start | bytes 442376 | tf_op jit(solution)/shard_map/ppermute | solution.py:404
  4.7 10.9 %collective-permute-start.2 = (bf16[144,512]{1,0:T(8,128)(2,1)}, bf16[144,512]{1,0:T(8,128)(2,1)S(1)}, u32[]{:S(2)}, u32[]{:S(2)}) collective-permute-start(bf16[144,512]{1,0:T(8,128)(2,1)} %get-tuple-element.16.refs_0_), channel_id=1, source_target_pairs={{0,96},{16,112},{32,64},{48,80},{64,32},{80,48},{96,0},{112,16},{1... | collective-permute-start | bytes 442376 | tf_op jit(solution)/shard_map/ppermute | solution.py:406
  8.4 7.3 %collective-permute-start.1 = (bf16[144,512]{1,0:T(8,128)(2,1)S(1)}, bf16[144,512]{1,0:T(8,128)(2,1)S(1)}, u32[]{:S(2)}, u32[]{:S(2)}) collective-permute-start(bf16[144,512]{1,0:T(8,128)(2,1)S(1)} %collective-permute-done.refs_1_), channel_id=1, source_target_pairs={{0,96},{16,112},{32,64},{48,80},{64,32},{80,48},{96,0},{112,16},{1... | collective-permute-start | bytes 442376 | tf_op jit(solution)/shard_map/ppermute | solution.py:406
  11.4 4.9 %collective-permute-start.7 = (bf16[144,512]{1,0:T(8,128)(2,1)}, bf16[144,512]{1,0:T(8,128)(2,1)S(1)}, u32[]{:S(2)}, u32[]{:S(2)}) collective-permute-start(bf16[144,512]{1,0:T(8,128)(2,1)} %get-tuple-element.16.refs_0_), channel_id=1, source_target_pairs={{0,16},{16,0},{32,48},{48,32},{64,80},{80,64},{96,112},{112,96},{1... | collective-permute-start | bytes 442376 | tf_op jit(solution)/shard_map/ppermute | solution.py:407
  14.8 11.6 %copy-start.2 = (bf16[144,512]{1,0:T(8,128)(2,1)S(1)}, bf16[144,512]{1,0:T(8,128)(2,1)}, u32[]{:S(2)}) copy-start(bf16[144,512]{1,0:T(8,128)(2,1)} %get-tuple-element.16.refs_0_) | copy-start | bytes 442372
  14.8 11.6 %copy-start.3 = (s32[16,2]{0,1:T(2,128)S(1)}, s32[16,2]{0,1:T(2,128)}, u32[]{:S(2)}) copy-start(s32[16,2]{0,1:T(2,128)} %param.16) | copy-start | bytes 388
  14.9 2.9 %collective-permute-start.11 = (bf16[144,512]{1,0:T(8,128)(2,1)S(1)}, bf16[144,512]{1,0:T(8,128)(2,1)S(1)}, u32[]{:S(2)}, u32[]{:S(2)}) collective-permute-start(bf16[144,512]{1,0:T(8,128)(2,1)S(1)} %collective-permute-done.3.refs_4_), channel_id=1, source_target_pairs={{0,16},{16,0},{32,48},{48,32},{64,80},{80,64},{96,112},{112,96},{1... | collective-permute-start | bytes 442376 | tf_op jit(solution)/shard_map/ppermute | solution.py:407
  15.5 5.9 %collective-permute-start.4 = (bf16[144,512]{1,0:T(8,128)(2,1)S(1)}, bf16[144,512]{1,0:T(8,128)(2,1)S(1)}, u32[]{:S(2)}, u32[]{:S(2)}) collective-permute-start(bf16[144,512]{1,0:T(8,128)(2,1)S(1)} %collective-permute-done.3.refs_4_), channel_id=1, source_target_pairs={{0,32},{16,48},{32,0},{48,16},{64,96},{80,112},{96,64},{112,80},{1... | collective-permute-start | bytes 442376 | tf_op jit(solution)/shard_map/ppermute | solution.py:405
  15.6 5.7 %collective-permute-start.10 = (bf16[144,512]{1,0:T(8,128)(2,1)S(1)}, bf16[144,512]{1,0:T(8,128)(2,1)S(1)}, u32[]{:S(2)}, u32[]{:S(2)}) collective-permute-start(bf16[144,512]{1,0:T(8,128)(2,1)S(1)} %collective-permute-done.2.refs_3_), channel_id=1, source_target_pairs={{0,16},{16,0},{32,48},{48,32},{64,80},{80,64},{96,112},{112,96},{1... | collective-permute-start | bytes 442376 | tf_op jit(solution)/shard_map/ppermute | solution.py:407
  15.7 6.7 %collective-permute-start.6 = (bf16[144,512]{1,0:T(8,128)(2,1)S(1)}, bf16[144,512]{1,0:T(8,128)(2,1)S(1)}, u32[]{:S(2)}, u32[]{:S(2)}) collective-permute-start(bf16[144,512]{1,0:T(8,128)(2,1)S(1)} %collective-permute-done.2.refs_3_), channel_id=1, source_target_pairs={{0,136},{1,137},{2,138},{3,139},{4,140},{5,141},{6,142},{7,143},{8... | collective-permute-start | bytes 442376 | tf_op jit(solution)/shard_map/ppermute | solution.py:404
  16.2 8.8 %collective-permute-start.5 = (bf16[144,512]{1,0:T(8,128)(2,1)S(1)}, bf16[144,512]{1,0:T(8,128)(2,1)S(1)}, u32[]{:S(2)}, u32[]{:S(2)}) collective-permute-start(bf16[144,512]{1,0:T(8,128)(2,1)S(1)} %after.1.refs_2_), channel_id=1, source_target_pairs={{0,136},{1,137},{2,138},{3,139},{4,140},{5,141},{6,142},{7,143},{8... | collective-permute-start | bytes 442376 | tf_op jit(solution)/shard_map/ppermute | solution.py:404
  17.7 7.3 %collective-permute-start.8 = (bf16[144,512]{1,0:T(8,128)(2,1)S(1)}, bf16[144,512]{1,0:T(8,128)(2,1)S(1)}, u32[]{:S(2)}, u32[]{:S(2)}) collective-permute-start(bf16[144,512]{1,0:T(8,128)(2,1)S(1)} %collective-permute-done.refs_1_), channel_id=1, source_target_pairs={{0,16},{16,0},{32,48},{48,32},{64,80},{80,64},{96,112},{112,96},{1... | collective-permute-start | bytes 442376 | tf_op jit(solution)/shard_map/ppermute | solution.py:407
  21.3 3.8 %collective-permute-start.9 = (bf16[144,512]{1,0:T(8,128)(2,1)S(1)}, bf16[144,512]{1,0:T(8,128)(2,1)S(1)}, u32[]{:S(2)}, u32[]{:S(2)}) collective-permute-start(bf16[144,512]{1,0:T(8,128)(2,1)S(1)} %after.1.refs_2_), channel_id=1, source_target_pairs={{0,16},{16,0},{32,48},{48,32},{64,80},{80,64},{96,112},{112,96},{1... | collective-permute-start | bytes 442376 | tf_op jit(solution)/shard_map/ppermute | solution.py:407
  21.3 3.7 %collective-permute-start.12 = (bf16[144,512]{1,0:T(8,128)(2,1)S(1)}, bf16[144,512]{1,0:T(8,128)(2,1)S(1)}, u32[]{:S(2)}, u32[]{:S(2)}) collective-permute-start(bf16[144,512]{1,0:T(8,128)(2,1)S(1)} %collective-permute-done.4.refs_5_), channel_id=1, source_target_pairs={{0,16},{16,0},{32,48},{48,32},{64,80},{80,64},{96,112},{112,96},{1... | collective-permute-start | bytes 442376 | tf_op jit(solution)/shard_map/ppermute | solution.py:407
  22.4 2.7 %collective-permute-start.14 = (bf16[144,512]{1,0:T(8,128)(2,1)S(1)}, bf16[144,512]{1,0:T(8,128)(2,1)S(1)}, u32[]{:S(2)}, u32[]{:S(2)}) collective-permute-start(bf16[144,512]{1,0:T(8,128)(2,1)S(1)} %collective-permute-done.6.refs_7_), channel_id=1, source_target_pairs={{0,16},{16,0},{32,48},{48,32},{64,80},{80,64},{96,112},{112,96},{1... | collective-permute-start | bytes 442376 | tf_op jit(solution)/shard_map/ppermute | solution.py:407
  25.1 1.4 %collective-permute-start.13 = (bf16[144,512]{1,0:T(8,128)(2,1)S(1)}, bf16[144,512]{1,0:T(8,128)(2,1)S(1)}, u32[]{:S(2)}, u32[]{:S(2)}) collective-permute-start(bf16[144,512]{1,0:T(8,128)(2,1)S(1)} %collective-permute-done.5.refs_6_), channel_id=1, source_target_pairs={{0,16},{16,0},{32,48},{48,32},{64,80},{80,64},{96,112},{112,96},{1... | collective-permute-start | bytes 442376 | tf_op jit(solution)/shard_map/ppermute | solution.py:407
  35.1 2.9 %collective-permute-start.15 = (bf16[8,144,512]{2,1,0:T(8,128)(2,1)S(1)}, bf16[8,144,512]{2,1,0:T(8,128)(2,1)S(1)}, u32[]{:S(2)}, u32[]{:S(2)}) collective-permute-start(bf16[8,144,512]{2,1,0:T(8,128)(2,1)S(1)} %get-tuple-element.24), channel_id=1, source_target_pairs={{0,16},{16,0},{32,48},{48,32},{64,80},{80,64},{96,112},{112,96},{1... | collective-permute-start | bytes 3538952 | tf_op jit(solution)/shard_map/ppermute | solution.py:449
  39.3 20.6 %all-to-all-start = ((bf16[8,144,512]{2,1,0:T(8,128)(2,1)}), bf16[8,144,512]{2,1,0:T(8,128)(2,1)S(1)}, u32[]{:S(2)}, u32[]{:S(2)}) async-start(bf16[8,144,512]{2,1,0:T(8,128)(2,1)} %pair.1), calls=%async_computation | async-start | bytes 2359296 | tf_op jit(solution)/shard_map/all_to_all | solution.py:458
  44.0 16.0 %copy-start = (f32[128,128]{1,0:T(8,128)S(1)}, f32[128,128]{1,0:T(8,128)}, u32[]{:S(2)}) copy-start(f32[128,128]{1,0:T(8,128)} %get-tuple-element.14.cos_ref) | copy-start | bytes 196612
  44.0 16.0 %copy-start.1 = (f32[128,128]{1,0:T(8,128)S(1)}, f32[128,128]{1,0:T(8,128)}, u32[]{:S(2)}) copy-start(f32[128,128]{1,0:T(8,128)} %get-tuple-element.15.sin_ref) | copy-start | bytes 196612

commit v5 on v4

--- a/solution.py
+++ b/solution.py
@@ -147,21 +147,22 @@
 
 def absorb_kernel(qn_ref, qr_ref, go_ref, uk_ref, uv_ref, cos_ref, sin_ref,
                   both_ref):
-    x = qr_ref[...].astype(f32)
-    rotated = x * cos_ref[...] + swap_halves(x) * sin_ref[...]
-    turned = pltpu.roll(rotated, HALF, 1)
-    for h in range(2):
-        cols = slice(h * D_NOPE, (h + 1) * D_NOPE)
-        q = lax.dot_general(qn_ref[:, cols], uk_ref[:, cols], AGAINST, preferred_element_type=f32)
-        g = lax.dot_general(go_ref[:, cols], uv_ref[:, cols], AGAINST, preferred_element_type=f32)
-        rope = jnp.where(lanes_of(x.shape) < D_ROPE, rotated if h == 0 else turned, 0.0)
-        dst = slice(h * HALF, (h + 1) * HALF)
-        for j in range(2):
-            src = slice(j * HALF, (j + 1) * HALF)
-            both_ref[j, 0, dst, :D_LAT] = (q[src] * SCALE).astype(bf16)
-            both_ref[j, 0, dst, D_LAT:] = (rope[src] * SCALE).astype(bf16)
-            both_ref[j, 1, dst, :D_LAT] = g[src].astype(bf16)
-            both_ref[j, 1, dst, D_LAT:] = jnp.zeros((HALF, 128), bf16)
+    for pair in range(2):
+        x = qr_ref[:, pair * 128:(pair + 1) * 128].astype(f32)
+        rotated = x * cos_ref[...] + swap_halves(x) * sin_ref[...]
+        turned = pltpu.roll(rotated, HALF, 1)
+        for h in (2 * pair, 2 * pair + 1):
+            cols = slice(h * D_NOPE, (h + 1) * D_NOPE)
+            q = lax.dot_general(qn_ref[:, cols], uk_ref[:, cols], AGAINST, preferred_element_type=f32)
+            g = lax.dot_general(go_ref[:, cols], uv_ref[:, cols], AGAINST, preferred_element_type=f32)
+            rope = jnp.where(lanes_of(x.shape) < D_ROPE, turned if h % 2 else rotated, 0.0)
+            dst = slice(h * HALF, (h + 1) * HALF)
+            for j in range(2):
+                src = slice(j * HALF, (j + 1) * HALF)
+                both_ref[j, 0, dst, :D_LAT] = (q[src] * SCALE).astype(bf16)
+                both_ref[j, 0, dst, D_LAT:] = (rope[src] * SCALE).astype(bf16)
+                both_ref[j, 1, dst, :D_LAT] = g[src].astype(bf16)
+                both_ref[j, 1, dst, D_LAT:] = jnp.zeros((HALF, 128), bf16)
 
 
 def step_places(bm_ref, rank):
@@ -213,15 +214,17 @@
     zero = jnp.zeros((1, LANES), f32)
     start = (jnp.full((1, LANES), HIDDEN, f32), zero, zero)
     state = {True: start, False: start}
-    offset = lax.broadcasted_iota(jnp.int32, (2 * CHUNK, LANES), 0) - (
-        lax.broadcasted_iota(jnp.int32, (2 * CHUNK, LANES), 1) & (HALF - 1)
+    offset = lax.broadcasted_iota(jnp.int32, (CHUNK, LANES), 0) - (
+        lax.broadcasted_iota(jnp.int32, (CHUNK, LANES), 1) & (HALF - 1)
     )
     for i, (at, is_early, j, c, n, block) in enumerate(places):
         rows = chunk_rows(c, n)
         top, total, weighted = (pick(is_early, a, b) for a, b in zip(state[True], state[False]))
         scores = lax.dot_general(keys[rows, :], both[j, :LANES, :], AGAINST, preferred_element_type=f32)
         dp = lax.dot_general(keys[rows, :D_LAT], both[j, LANES:, :D_LAT], AGAINST, preferred_element_type=f32)
-        scores = jnp.where(offset[:n * CHUNK] <= block * HALF - c * CHUNK, scores * LOG2E, HIDDEN)
+        scores = scores * LOG2E
+        if n == 1:
+            scores = jnp.where(offset <= block * HALF - c * CHUNK, scores, HIDDEN)
         new_top = jnp.maximum(top, jnp.max(scores, axis=0, keepdims=True))
         e = jnp.exp2(scores - new_top)
         keep = jnp.exp2(top - new_top)
@@ -409,12 +412,12 @@
     held.update({10: y1(held[8]), 4: y3(held[2]), 14: x(held[6])})
     pair_cols = lambda width: pl.BlockSpec((ROWS, width), lambda p: (0, p))
     fixed = pl.BlockSpec((ROWS, 128), lambda p: (0, 0))
-    weight = pl.BlockSpec((D_LAT, 256), lambda p: (0, p))
+    weight = pl.BlockSpec((D_LAT, 512), lambda p: (0, p))
     both = pl.pallas_call(
         absorb_kernel,
-        grid=(HEADS // 2,),
-        in_specs=[pair_cols(256), pair_cols(128), pair_cols(256), weight, weight, fixed, fixed],
-        out_specs=pl.BlockSpec((2, 2, 128, D_PAD), lambda p: (0, 0, p, 0)),
+        grid=(HEADS // 4,),
+        in_specs=[pair_cols(512), pair_cols(256), pair_cols(512), weight, weight, fixed, fixed],
+        out_specs=pl.BlockSpec((2, 2, 256, D_PAD), lambda p: (0, 0, p, 0)),
         out_shape=shape((2, 2, LANES, D_PAD), bf16),
         compiler_params=params(16),
         cost_estimate=pl.CostEstimate(flops=300_000_000, bytes_accessed=8_000_000, transcendentals=0),

time: 93.6 us -> 92.7 us (level)
  transfers between devices with their start and end apart: 17 -> 17, of which waited for: 7 -> 7; matrix products, arithmetic and copies ran while one was open for 0% -> 0% of each run, Pallas kernels for 15% -> 14%
where the time goes in v5:
time: 92.7 us; the launch traced here: 92.4 us
  blocking collectives  32.2 us (35%)
  Pallas kernels  25.2 us (27%)
  waiting for transfers between devices  17.9 us (19%)
  starting transfers between devices  15.5 us (17%)
    all_to_all x1, blocking collectives, on_device(): lax.all_to_all(owned.reshape(N_HEAD, ROWS // N_HEAD, D_ALL), 'head', 0, 0)  20.3 us
    all_to_all x1, blocking collectives, on_device(): grad_compressed = lax.all_to_all(slabs, 'head', 0, 0).reshape(ROWS, D_ALL)  12 us
    pallas_call x1, Pallas kernels, attend_call(): pl.pallas_call(attend_kernel, in_specs=[SMEM, SMEM] + whole(1 + 2 * N_CHI...  8.62 us
    pallas_call x1, Pallas kernels, on_device(): pl.pallas_call(queries_kernel, in_specs=[SMEM, SMEM, HBM, HBM, HBM] + who...  8.23 us
    all_to_all x1, waiting for transfers between devices, on_device(): lax.all_to_all(summed, ('ctx', 'head'), 0, 0, axis_index_groups=GROUPS)  7.73 us
    ppermute x2, starting transfers between devices, on_device(): y3 = lambda a: lax.ppermute(a, 'ctx', ALONG_Y3)  5.2 us
    ppermute x2, waiting for transfers between devices, on_device(): y1 = lambda a: lax.ppermute(a, 'ctx', ALONG_Y1)  5.08 us
    all_to_all x1, starting transfers between devices, on_device(): lax.all_to_all(summed, ('ctx', 'head'), 0, 0, axis_index_groups=GROUPS)  4.61 us
  transfers between devices with their start and end apart: 17, of which 7 were waited for; matrix products, arithmetic and copies ran while one was open for 0% of the time, Pallas kernels for 14%

profile of v5, /device:TPU:4, one launch (start us, length us, event | category | flops | bytes accessed | tf_op | source)
XLA Modules:
  0.0 92.4 jit_solution(8765057332520185196)
XLA Ops:
  0.6 1.9 %share.1 = (bf16[144,512]{1,0:T(8,128)(2,1)}, f32[128,128]{1,0:T(8,128)}, f32[128,128]{1,0:T(8,128)}) custom-call(s32[1]{0:T(128)} %bitcast.1.rank_ref, s32[1,128]{1,0:T(1,128)} %bitcast.13, f32[1,128]{1,0:T(1,128)} %constant.7.clone.inv_ref, bf16[576,128]{1,0:T(8,128)(2,1)} %bitcast.12), custom_call_target="tpu_custom_call" | custom-call | tf_op jit(solution)/shard_map/share/pallas_call | solution.py:399
  2.6 1.6 %collective-permute-start = (bf16[144,512]{1,0:T(8,128)(2,1)}, bf16[144,512]{1,0:T(8,128)(2,1)S(1)}, u32[]{:S(2)}, u32[]{:S(2)}) collective-permute-start(bf16[144,512]{1,0:T(8,128)(2,1)} %get-tuple-element.16.refs_0_), channel_id=1, source_target_pairs={{0,32},{16,48},{32,0},{48,16},{64,96},{80,112},{96,64},{112,80},{1... | collective-permute-start | bytes 442376 | tf_op jit(solution)/shard_map/ppermute | solution.py:408
  4.1 0.5 collective-permute-start.3
  4.7 2.2 %collective-permute-start.2 = (bf16[144,512]{1,0:T(8,128)(2,1)}, bf16[144,512]{1,0:T(8,128)(2,1)S(1)}, u32[]{:S(2)}, u32[]{:S(2)}) collective-permute-start(bf16[144,512]{1,0:T(8,128)(2,1)} %get-tuple-element.16.refs_0_), channel_id=1, source_target_pairs={{0,96},{16,112},{32,64},{48,80},{64,32},{80,48},{96,0},{112,16},{1... | collective-permute-start | bytes 442376 | tf_op jit(solution)/shard_map/ppermute | solution.py:409
  6.9 1.5 %collective-permute-done.refs_1_ = bf16[144,512]{1,0:T(8,128)(2,1)S(1)} collective-permute-done((bf16[144,512]{1,0:T(8,128)(2,1)}, bf16[144,512]{1,0:T(8,128)(2,1)S(1)}, u32[]{:S(2)}, u32[]{:S(2)}) %collective-permute-start) | collective-permute-done | bytes 147488 | tf_op jit(solution)/shard_map/ppermute | solution.py:408
  8.4 3.0 %collective-permute-start.1 = (bf16[144,512]{1,0:T(8,128)(2,1)S(1)}, bf16[144,512]{1,0:T(8,128)(2,1)S(1)}, u32[]{:S(2)}, u32[]{:S(2)}) collective-permute-start(bf16[144,512]{1,0:T(8,128)(2,1)S(1)} %collective-permute-done.refs_1_), channel_id=1, source_target_pairs={{0,96},{16,112},{32,64},{48,80},{64,32},{80,48},{96,0},{112,16},{1... | collective-permute-start | bytes 442376 | tf_op jit(solution)/shard_map/ppermute | solution.py:409
  11.4 2.6 %absorb.1.second_ref = bf16[2,2,512,640]{3,2,1,0:T(8,128)(2,1)S(1)} custom-call(bf16[128,1024]{1,0:T(8,128)(2,1)} %qn_ref.1, bf16[128,512]{1,0:T(8,128)(2,1)} %qr_ref.1, bf16[128,1024]{1,0:T(8,128)(2,1)} %go_ref.1, bf16[512,1024]{1,0:T(8,128)(2,1)} %uk_hbm.1, bf16[512,1024]{1,0:T(8,128)(2,1)} %uv_ref.1, f32[128,128]{1,0:T(8,128)} %get-tuple-element.14.cos_ref, ...), custom_call_target="tpu_custom_call" | custom-call | flops 300000000 | bytes 8000000 | tf_op jit(solution)/shard_map/absorb/pallas_call | solution.py:416
  14.0 0.0 copy-start.2
  14.0 0.0 copy-start.3
  14.0 0.6 collective-permute-start.11
  14.6 0.1 collective-permute-start.4
  14.8 0.1 collective-permute-start.10
  14.8 1.1 %collective-permute-start.6 = (bf16[144,512]{1,0:T(8,128)(2,1)S(1)}, bf16[144,512]{1,0:T(8,128)(2,1)S(1)}, u32[]{:S(2)}, u32[]{:S(2)}) collective-permute-start(bf16[144,512]{1,0:T(8,128)(2,1)S(1)} %collective-permute-done.2.refs_3_), channel_id=1, source_target_pairs={{0,136},{1,137},{2,138},{3,139},{4,140},{5,141},{6,142},{7,143},{8... | collective-permute-start | bytes 442376 | tf_op jit(solution)/shard_map/ppermute | solution.py:407
  15.9 1.0 %collective-permute-start.5 = (bf16[144,512]{1,0:T(8,128)(2,1)S(1)}, bf16[144,512]{1,0:T(8,128)(2,1)S(1)}, u32[]{:S(2)}, u32[]{:S(2)}) collective-permute-start(bf16[144,512]{1,0:T(8,128)(2,1)S(1)} %after.1.refs_2_), channel_id=1, source_target_pairs={{0,136},{1,137},{2,138},{3,139},{4,140},{5,141},{6,142},{7,143},{8... | collective-permute-start | bytes 442376 | tf_op jit(solution)/shard_map/ppermute | solution.py:407
  16.9 3.6 %collective-permute-done.4.refs_5_ = bf16[144,512]{1,0:T(8,128)(2,1)S(1)} collective-permute-done((bf16[144,512]{1,0:T(8,128)(2,1)S(1)}, bf16[144,512]{1,0:T(8,128)(2,1)S(1)}, u32[]{:S(2)}, u32[]{:S(2)}) %collective-permute-start.4) | collective-permute-done | bytes 147488 | tf_op jit(solution)/shard_map/ppermute | solution.py:408
  20.5 0.5 collective-permute-start.12
  21.0 0.5 collective-permute-done.6.refs_7_
  21.5 2.7 %collective-permute-done.5.refs_6_ = bf16[144,512]{1,0:T(8,128)(2,1)S(1)} collective-permute-done((bf16[144,512]{1,0:T(8,128)(2,1)S(1)}, bf16[144,512]{1,0:T(8,128)(2,1)S(1)}, u32[]{:S(2)}, u32[]{:S(2)}) %collective-permute-start.5) | collective-permute-done | bytes 147488 | tf_op jit(solution)/shard_map/ppermute | solution.py:407
  24.2 0.0 collective-permute-start.13
  24.2 1.3 %collective-permute-done.13.refs_14_ = bf16[144,512]{1,0:T(8,128)(2,1)S(1)} collective-permute-done((bf16[144,512]{1,0:T(8,128)(2,1)S(1)}, bf16[144,512]{1,0:T(8,128)(2,1)S(1)}, u32[]{:S(2)}, u32[]{:S(2)}) %collective-permute-start.13) | collective-permute-done | bytes 147488 | tf_op jit(solution)/shard_map/ppermute | solution.py:410
  25.6 8.6 %attend.1 = (bf16[8,144,512]{2,1,0:T(8,128)(2,1)S(1)}, bf16[8,144,512]{2,1,0:T(8,128)(2,1)S(1)}, bf16[2304,512]{1,0:T(8,128)(2,1)S(1)}, bf16[2048,640]{1,0:T(8,128)(2,1)S(1)}) custom-call(s32[2,16]{1,0:T(2,128)S(1)} %bitcast.10, s32[1]{0:T(128)} %bitcast.1.rank_ref, bf16[2,1024,640]{2,1,0:T(8,128)(2,1)S(1)} %bitcast.7, bf16[144,512]{1,0:T(8,128)(2,1)S(1)} %copy-done.2, ...), custom_call_target="tpu_custom_call" | custom-call | tf_op jit(solution)/shard_map/attend/pallas_call | solution.py:377
  34.2 0.2 collective-permute-start.15
  34.4 2.2 %spill.1 = (bf16[2304,512]{1,0:T(8,128)(2,1)}, bf16[2048,640]{1,0:T(8,128)(2,1)}) custom-call(bf16[2304,512]{1,0:T(8,128)(2,1)S(1)} %get-tuple-element.17.ds, bf16[2048,640]{1,0:T(8,128)(2,1)S(1)} %get-tuple-element.18.keys), custom_call_target="tpu_custom_call" | custom-call | bytes 10000000 | tf_op jit(solution)/shard_map/spill/pallas_call | solution.py:441
  36.7 0.5 collective-permute-done.15.theirs_ref
  37.1 1.3 %pair.1 = bf16[8,144,512]{2,1,0:T(8,128)(2,1)} custom-call(bf16[8,144,512]{2,1,0:T(8,128)(2,1)S(1)} %get-tuple-element.23.ours_ref, bf16[8,144,512]{2,1,0:T(8,128)(2,1)S(1)} %collective-permute-done.15.theirs_ref, bf16[2304,512]{1,0:T(8,128)(2,1)} %get-tuple-element.20.ds_hbm.later_ref), custom_call_target="tpu_custom_call" | custom-call | tf_op jit(solution)/shard_map/pair/pallas_call | solution.py:453
  38.5 4.6 %all-to-all-start = ((bf16[8,144,512]{2,1,0:T(8,128)(2,1)}), bf16[8,144,512]{2,1,0:T(8,128)(2,1)S(1)}, u32[]{:S(2)}, u32[]{:S(2)}) async-start(bf16[8,144,512]{2,1,0:T(8,128)(2,1)} %pair.1), calls=%async_computation | async-start | bytes 2359296 | tf_op jit(solution)/shard_map/all_to_all | solution.py:461
  43.1 8.2 %queries.1 = (bf16[128,1024]{1,0:T(8,128)(2,1)}, bf16[128,512]{1,0:T(8,128)(2,1)}) custom-call(s32[2,16]{1,0:T(2,128)} %bitcast.9, s32[1]{0:T(128)} %bitcast.1.rank_ref, bf16[2048,640]{1,0:T(8,128)(2,1)} %get-tuple-element.19.keys_hbm, bf16[2304,512]{1,0:T(8,128)(2,1)} %get-tuple-element.20.ds_hbm.later_ref, bf16[512,1024]{1,0:T(8,128)(2,1)} %uk_hbm.1, ...), custom_call_target="tpu_custom_call" | custom-call | flops 4000000000 | bytes 9000000 | tf_op jit(solution)/shard_map/queries/pallas_call | solution.py:463
  51.3 7.7 %all-to-all-done.parts_ref = bf16[8,144,512]{2,1,0:T(8,128)(2,1)S(1)} async-done(((bf16[8,144,512]{2,1,0:T(8,128)(2,1)}), bf16[8,144,512]{2,1,0:T(8,128)(2,1)S(1)}, u32[]{:S(2)}, u32[]{:S(2)}) %all-to-all-start) | async-done | bytes 1179680 | tf_op jit(solution)/shard_map/all_to_all | solution.py:461
  59.1 0.3 chips.1
  59.3 20.3 %all_to_all.15.parts_ref = bf16[16,8,576]{2,1,0:T(8,128)(2,1)S(1)} all-to-all(bf16[16,8,576]{2,1,0:T(8,128)(2,1)S(1)} %bitcast.8), channel_id=1, replica_groups=mesh['ctx'=16,'head'=16] {'head'}, dimensions={0} | all-to-all | bytes 294912 | tf_op jit(solution)/shard_map/all_to_all | solution.py:489
  79.6 12.0 %all_to_all.16 = bf16[16,8,576]{2,1,0:T(8,128)(2,1)S(1)} all-to-all(bf16[16,8,576]{2,1,0:T(8,128)(2,1)S(1)} %heads.1), channel_id=1, replica_groups=mesh['ctx'=16,'head'=16] {'head'}, dimensions={0} | all-to-all | bytes 294912 | tf_op jit(solution)/shard_map/all_to_all | solution.py:498
  91.6 0.8 copy.13
  (22 shorter events, 0.1 us)
Async XLA Ops:
  2.6 5.8 %collective-permute-start = (bf16[144,512]{1,0:T(8,128)(2,1)}, bf16[144,512]{1,0:T(8,128)(2,1)S(1)}, u32[]{:S(2)}, u32[]{:S(2)}) collective-permute-start(bf16[144,512]{1,0:T(8,128)(2,1)} %get-tuple-element.16.refs_0_), channel_id=1, source_target_pairs={{0,32},{16,48},{32,0},{48,16},{64,96},{80,112},{96,64},{112,80},{1... | collective-permute-start | bytes 442376 | tf_op jit(solution)/shard_map/ppermute | solution.py:408
  4.1 9.9 %collective-permute-start.3 = (bf16[144,512]{1,0:T(8,128)(2,1)}, bf16[144,512]{1,0:T(8,128)(2,1)S(1)}, u32[]{:S(2)}, u32[]{:S(2)}) collective-permute-start(bf16[144,512]{1,0:T(8,128)(2,1)} %get-tuple-element.16.refs_0_), channel_id=1, source_target_pairs={{0,136},{1,137},{2,138},{3,139},{4,140},{5,141},{6,142},{7,143},{8... | collective-permute-start | bytes 442376 | tf_op jit(solution)/shard_map/ppermute | solution.py:407
  4.7 10.1 %collective-permute-start.2 = (bf16[144,512]{1,0:T(8,128)(2,1)}, bf16[144,512]{1,0:T(8,128)(2,1)S(1)}, u32[]{:S(2)}, u32[]{:S(2)}) collective-permute-start(bf16[144,512]{1,0:T(8,128)(2,1)} %get-tuple-element.16.refs_0_), channel_id=1, source_target_pairs={{0,96},{16,112},{32,64},{48,80},{64,32},{80,48},{96,0},{112,16},{1... | collective-permute-start | bytes 442376 | tf_op jit(solution)/shard_map/ppermute | solution.py:409
  8.4 6.5 %collective-permute-start.1 = (bf16[144,512]{1,0:T(8,128)(2,1)S(1)}, bf16[144,512]{1,0:T(8,128)(2,1)S(1)}, u32[]{:S(2)}, u32[]{:S(2)}) collective-permute-start(bf16[144,512]{1,0:T(8,128)(2,1)S(1)} %collective-permute-done.refs_1_), channel_id=1, source_target_pairs={{0,96},{16,112},{32,64},{48,80},{64,32},{80,48},{96,0},{112,16},{1... | collective-permute-start | bytes 442376 | tf_op jit(solution)/shard_map/ppermute | solution.py:409
  11.4 4.5 %collective-permute-start.7 = (bf16[144,512]{1,0:T(8,128)(2,1)}, bf16[144,512]{1,0:T(8,128)(2,1)S(1)}, u32[]{:S(2)}, u32[]{:S(2)}) collective-permute-start(bf16[144,512]{1,0:T(8,128)(2,1)} %get-tuple-element.16.refs_0_), channel_id=1, source_target_pairs={{0,16},{16,0},{32,48},{48,32},{64,80},{80,64},{96,112},{112,96},{1... | collective-permute-start | bytes 442376 | tf_op jit(solution)/shard_map/ppermute | solution.py:410
  14.0 11.6 %copy-start.2 = (bf16[144,512]{1,0:T(8,128)(2,1)S(1)}, bf16[144,512]{1,0:T(8,128)(2,1)}, u32[]{:S(2)}) copy-start(bf16[144,512]{1,0:T(8,128)(2,1)} %get-tuple-element.16.refs_0_) | copy-start | bytes 442372
  14.0 11.6 %copy-start.3 = (s32[16,2]{0,1:T(2,128)S(1)}, s32[16,2]{0,1:T(2,128)}, u32[]{:S(2)}) copy-start(s32[16,2]{0,1:T(2,128)} %param.16) | copy-start | bytes 388
  14.0 2.9 %collective-permute-start.11 = (bf16[144,512]{1,0:T(8,128)(2,1)S(1)}, bf16[144,512]{1,0:T(8,128)(2,1)S(1)}, u32[]{:S(2)}, u32[]{:S(2)}) collective-permute-start(bf16[144,512]{1,0:T(8,128)(2,1)S(1)} %collective-permute-done.3.refs_4_), channel_id=1, source_target_pairs={{0,16},{16,0},{32,48},{48,32},{64,80},{80,64},{96,112},{112,96},{1... | collective-permute-start | bytes 442376 | tf_op jit(solution)/shard_map/ppermute | solution.py:410
  14.6 5.9 %collective-permute-start.4 = (bf16[144,512]{1,0:T(8,128)(2,1)S(1)}, bf16[144,512]{1,0:T(8,128)(2,1)S(1)}, u32[]{:S(2)}, u32[]{:S(2)}) collective-permute-start(bf16[144,512]{1,0:T(8,128)(2,1)S(1)} %collective-permute-done.3.refs_4_), channel_id=1, source_target_pairs={{0,32},{16,48},{32,0},{48,16},{64,96},{80,112},{96,64},{112,80},{1... | collective-permute-start | bytes 442376 | tf_op jit(solution)/shard_map/ppermute | solution.py:408
  14.8 5.7 %collective-permute-start.10 = (bf16[144,512]{1,0:T(8,128)(2,1)S(1)}, bf16[144,512]{1,0:T(8,128)(2,1)S(1)}, u32[]{:S(2)}, u32[]{:S(2)}) collective-permute-start(bf16[144,512]{1,0:T(8,128)(2,1)S(1)} %collective-permute-done.2.refs_3_), channel_id=1, source_target_pairs={{0,16},{16,0},{32,48},{48,32},{64,80},{80,64},{96,112},{112,96},{1... | collective-permute-start | bytes 442376 | tf_op jit(solution)/shard_map/ppermute | solution.py:410
  14.8 6.7 %collective-permute-start.6 = (bf16[144,512]{1,0:T(8,128)(2,1)S(1)}, bf16[144,512]{1,0:T(8,128)(2,1)S(1)}, u32[]{:S(2)}, u32[]{:S(2)}) collective-permute-start(bf16[144,512]{1,0:T(8,128)(2,1)S(1)} %collective-permute-done.2.refs_3_), channel_id=1, source_target_pairs={{0,136},{1,137},{2,138},{3,139},{4,140},{5,141},{6,142},{7,143},{8... | collective-permute-start | bytes 442376 | tf_op jit(solution)/shard_map/ppermute | solution.py:407
  15.9 8.3 %collective-permute-start.5 = (bf16[144,512]{1,0:T(8,128)(2,1)S(1)}, bf16[144,512]{1,0:T(8,128)(2,1)S(1)}, u32[]{:S(2)}, u32[]{:S(2)}) collective-permute-start(bf16[144,512]{1,0:T(8,128)(2,1)S(1)} %after.1.refs_2_), channel_id=1, source_target_pairs={{0,136},{1,137},{2,138},{3,139},{4,140},{5,141},{6,142},{7,143},{8... | collective-permute-start | bytes 442376 | tf_op jit(solution)/shard_map/ppermute | solution.py:407
  16.9 7.3 %collective-permute-start.8 = (bf16[144,512]{1,0:T(8,128)(2,1)S(1)}, bf16[144,512]{1,0:T(8,128)(2,1)S(1)}, u32[]{:S(2)}, u32[]{:S(2)}) collective-permute-start(bf16[144,512]{1,0:T(8,128)(2,1)S(1)} %collective-permute-done.refs_1_), channel_id=1, source_target_pairs={{0,16},{16,0},{32,48},{48,32},{64,80},{80,64},{96,112},{112,96},{1... | collective-permute-start | bytes 442376 | tf_op jit(solution)/shard_map/ppermute | solution.py:410
  20.5 3.8 %collective-permute-start.9 = (bf16[144,512]{1,0:T(8,128)(2,1)S(1)}, bf16[144,512]{1,0:T(8,128)(2,1)S(1)}, u32[]{:S(2)}, u32[]{:S(2)}) collective-permute-start(bf16[144,512]{1,0:T(8,128)(2,1)S(1)} %after.1.refs_2_), channel_id=1, source_target_pairs={{0,16},{16,0},{32,48},{48,32},{64,80},{80,64},{96,112},{112,96},{1... | collective-permute-start | bytes 442376 | tf_op jit(solution)/shard_map/ppermute | solution.py:410
  20.5 3.7 %collective-permute-start.12 = (bf16[144,512]{1,0:T(8,128)(2,1)S(1)}, bf16[144,512]{1,0:T(8,128)(2,1)S(1)}, u32[]{:S(2)}, u32[]{:S(2)}) collective-permute-start(bf16[144,512]{1,0:T(8,128)(2,1)S(1)} %collective-permute-done.4.refs_5_), channel_id=1, source_target_pairs={{0,16},{16,0},{32,48},{48,32},{64,80},{80,64},{96,112},{112,96},{1... | collective-permute-start | bytes 442376 | tf_op jit(solution)/shard_map/ppermute | solution.py:410
  21.5 2.7 %collective-permute-start.14 = (bf16[144,512]{1,0:T(8,128)(2,1)S(1)}, bf16[144,512]{1,0:T(8,128)(2,1)S(1)}, u32[]{:S(2)}, u32[]{:S(2)}) collective-permute-start(bf16[144,512]{1,0:T(8,128)(2,1)S(1)} %collective-permute-done.6.refs_7_), channel_id=1, source_target_pairs={{0,16},{16,0},{32,48},{48,32},{64,80},{80,64},{96,112},{112,96},{1... | collective-permute-start | bytes 442376 | tf_op jit(solution)/shard_map/ppermute | solution.py:410
  24.2 1.4 %collective-permute-start.13 = (bf16[144,512]{1,0:T(8,128)(2,1)S(1)}, bf16[144,512]{1,0:T(8,128)(2,1)S(1)}, u32[]{:S(2)}, u32[]{:S(2)}) collective-permute-start(bf16[144,512]{1,0:T(8,128)(2,1)S(1)} %collective-permute-done.5.refs_6_), channel_id=1, source_target_pairs={{0,16},{16,0},{32,48},{48,32},{64,80},{80,64},{96,112},{112,96},{1... | collective-permute-start | bytes 442376 | tf_op jit(solution)/shard_map/ppermute | solution.py:410
  34.2 2.9 %collective-permute-start.15 = (bf16[8,144,512]{2,1,0:T(8,128)(2,1)S(1)}, bf16[8,144,512]{2,1,0:T(8,128)(2,1)S(1)}, u32[]{:S(2)}, u32[]{:S(2)}) collective-permute-start(bf16[8,144,512]{2,1,0:T(8,128)(2,1)S(1)} %get-tuple-element.24), channel_id=1, source_target_pairs={{0,16},{16,0},{32,48},{48,32},{64,80},{80,64},{96,112},{112,96},{1... | collective-permute-start | bytes 3538952 | tf_op jit(solution)/shard_map/ppermute | solution.py:452
  38.5 20.6 %all-to-all-start = ((bf16[8,144,512]{2,1,0:T(8,128)(2,1)}), bf16[8,144,512]{2,1,0:T(8,128)(2,1)S(1)}, u32[]{:S(2)}, u32[]{:S(2)}) async-start(bf16[8,144,512]{2,1,0:T(8,128)(2,1)} %pair.1), calls=%async_computation | async-start | bytes 2359296 | tf_op jit(solution)/shard_map/all_to_all | solution.py:461
  43.1 16.0 %copy-start = (f32[128,128]{1,0:T(8,128)S(1)}, f32[128,128]{1,0:T(8,128)}, u32[]{:S(2)}) copy-start(f32[128,128]{1,0:T(8,128)} %get-tuple-element.14.cos_ref) | copy-start | bytes 196612
  43.1 16.0 %copy-start.1 = (f32[128,128]{1,0:T(8,128)S(1)}, f32[128,128]{1,0:T(8,128)}, u32[]{:S(2)}) copy-start(f32[128,128]{1,0:T(8,128)} %get-tuple-element.15.sin_ref) | copy-start | bytes 196612
